TPU v7x, 32 devices: a whole 2x2x4 slice. The times are simulated.
32 devices in a mesh: ma: 4 (over y, x), mb: 8 (over z, core).
Axes of the slice: x: 2, y: 2, z: 4, core: 2. Of those that a mesh axis runs over, the one named last changes fastest.
Arguments:
- tier_four: float32 [256, 2, 128, 128], P(('ma', 'mb')), may hold values from -6 to 6
- tier_six: float32 [256, 2, 128, 128], P(('ma', 'mb')), may hold values from -6 to 6
- tier_seven: float32 [256, 2, 128, 128], P(('ma', 'mb')), may hold values from -6 to 6
- coupling: float32 [128, 128], replicated
- eigenbasis: float32 [128, 128], replicated
- energies: float32 [128], replicated, may hold values from -6 to 6
- decay_rates: float32 [12], replicated, may hold values from 0.5 to 4
- bath_coefficients: float32 [2, 12], replicated, may hold values from -1 to 1
- occupation_five: int32 [256, 12], P(('ma', 'mb')), may hold values from 0 to 5, as said below
- local_five: int32 [256, 2, 9], P(('ma', 'mb')), may hold values from 0 to 7
- peers_five: int32 [256, 4], P(('ma', 'mb')), may hold values from 0 to 7, all different within a row; in each aligned block of 8 rows (0 to 7, 8 to 15, ...) at most 6 rows name the same one
- places_five: int32 [256, 4], P(('ma', 'mb')), may hold values from 0 to 7
- occupation_six: int32 [256, 12], P(('ma', 'mb')), may hold values from 0 to 6, as said below
- local_six: int32 [256, 2, 9], P(('ma', 'mb')), may hold values from 0 to 7
- peers_six: int32 [256, 4], P(('ma', 'mb')), may hold values from 0 to 7, all different within a row; in each aligned block of 8 rows (0 to 7, 8 to 15, ...) at most 6 rows name the same one
- places_six: int32 [256, 4], P(('ma', 'mb')), may hold values from 0 to 7
Outputs:
- updated_five: float32 [256, 2, 128, 128], P(('ma', 'mb'))
- updated_six: float32 [256, 2, 128, 128], P(('ma', 'mb'))
Inputs may be any that keep to these rules, and one draw needn't show every extreme that they name: `occupation_five`: each row sums to 5; the first row of every block of 8 rows has all 5 in one mode. `occupation_six`: each row sums to 6; the first row of every block of 8 rows has all 6 in one mode. `local_five`: positions within the matrix's own block of 8 rows; a lowered entry is read only where its mode's occupation is positive. `local_six`: positions within the matrix's own block of 8 rows; a lowered entry is read only where its mode's occupation is positive. `peers_five`: the four entries of a row differ; among the rows of one block of 8 rows no value appears more than 6 times, and some value appears exactly 6 times. `peers_six`: the four entries of a row differ; among the rows of one block of 8 rows no value appears more than 6 times, and some value appears exactly 6 times.
All inputs are finite; a program needn't handle non-finite values.
Results may differ from a plain program's by a relative error of at most 0.0003.
Values sent between devices are 32-bit elements; how exact they have to be, the bound alone decides.
No kernel may reach another device: no remote copies, remote signals or barrier semaphores. Data moves between devices by JAX's collectives and lax.ppermute only.
A program may use at most 128 MiB of HBM per device.

v0:
```python
import jax
import jax.numpy as jnp
from jax import lax
from jax.sharding import PartitionSpec as P

HIGHEST = lax.Precision.HIGHEST


def passed_along(array, axis, by):
    peers = lax.axis_size(axis)
    return lax.ppermute(array, axis, [(i, (i + by) % peers) for i in range(peers)])


def left_product(matrix, batch):
    return jnp.einsum("ij,mjk->mik", matrix, batch, precision=HIGHEST)


def right_product(batch, matrix):
    return jnp.einsum("mij,jk->mik", batch, matrix, precision=HIGHEST)


def mix_terms(up_real, up_imag, sum_rr, sum_ri, sum_ir, sum_ii):
    return (
        up_real + sum_rr - sum_ii,
        up_imag + sum_ri + sum_ir,
        up_real + sum_rr + sum_ii,
        up_imag + sum_ri - sum_ir,
    )


def settle(
    pair_real,
    pair_imag,
    other_real,
    other_imag,
    occupation,
    coupling,
    eigenbasis,
    energies,
    decay_rates,
):
    comm_real = left_product(coupling, pair_real) - right_product(other_real, coupling)
    comm_imag = left_product(coupling, pair_imag) - right_product(other_imag, coupling)
    turned = jnp.transpose(eigenbasis)
    eigen_real = right_product(left_product(turned, -comm_imag), eigenbasis)
    eigen_imag = right_product(left_product(turned, comm_real), eigenbasis)
    damping = jnp.dot(occupation.astype(jnp.float32), decay_rates, precision=HIGHEST)[:, None, None]
    splitting = (energies[:, None] - energies[None, :])[None]
    denominator = damping * damping + splitting * splitting
    factor_real = -damping / denominator
    factor_imag = splitting / denominator
    solved_real = eigen_real * factor_real - eigen_imag * factor_imag
    solved_imag = eigen_real * factor_imag + eigen_imag * factor_real
    back_real = right_product(left_product(eigenbasis, solved_real), turned)
    back_imag = right_product(left_product(eigenbasis, solved_imag), turned)
    return jnp.stack([back_real, back_imag], axis=1)


def first_mode(lower_tier, upper_tier):
    raised_first = passed_along(upper_tier, "ma", -1)
    lowered_first = passed_along(lower_tier, "ma", 1)
    return (raised_first, lowered_first)


def request_table(peer_ids, wanted, capacity, peer_count):
    onehot = (peer_ids[:, None] == jnp.arange(peer_count, dtype=jnp.int32)[None, :]).astype(
        jnp.int32
    )
    ranking = jnp.cumsum(onehot, axis=0) - 1
    placed = peer_ids * capacity + jnp.sum(ranking * onehot, axis=1)
    table = jnp.zeros((peer_count * capacity,), jnp.int32).at[placed].set(wanted)
    return (table.reshape(peer_count, capacity), placed)


def fetch_plain(table, store):
    return lax.all_to_all(
        store[lax.all_to_all(table, "mb", split_axis=0, concat_axis=0, tiled=True)],
        "mb",
        split_axis=0,
        concat_axis=0,
        tiled=True,
    )


def pick_rows(received, placed):
    flat_rows = received.reshape((-1,) + received.shape[2:])
    return flat_rows[placed]


def combine(
    lower_tier,
    upper_tier,
    raised_first,
    lowered_first,
    remote,
    nearby,
    occupation,
    bath_coefficients,
):
    count_rows = lower_tier.shape[0]
    shape_tail = lower_tier.shape[2:]
    spots = jnp.arange(count_rows, dtype=jnp.int32)
    counted = occupation.astype(jnp.float32)
    weight_real = counted * bath_coefficients[0][None, :]
    weight_imag = counted * bath_coefficients[1][None, :]
    up_hits = jnp.sum((nearby[:, 0, :, None] == spots[None, None, :]).astype(jnp.float32), axis=1)
    down_hits = (nearby[:, 1, :, None] == spots[None, None, :]).astype(jnp.float32)
    local_real = jnp.einsum("mk,mkj->mj", weight_real[:, 3:], down_hits, precision=HIGHEST)
    local_imag = jnp.einsum("mk,mkj->mj", weight_imag[:, 3:], down_hits, precision=HIGHEST)
    flat_upper = upper_tier.reshape(count_rows, -1)
    up_sum = jnp.dot(up_hits, flat_upper, precision=HIGHEST).reshape(upper_tier.shape)
    up_sum = up_sum + raised_first + remote[:, 0] + remote[:, 1]
    edges = jnp.stack([lowered_first, remote[:, 2], remote[:, 3]], axis=1)

    def weighted(local_weights, edge_weights, part_index):
        flat_part = lower_tier[:, part_index].reshape(count_rows, -1)
        inner = jnp.dot(local_weights, flat_part, precision=HIGHEST).reshape(
            (count_rows,) + shape_tail
        )
        return inner + jnp.einsum(
            "mk,mkij->mij", edge_weights, edges[:, :, part_index], precision=HIGHEST
        )

    return mix_terms(
        up_sum[:, 0],
        up_sum[:, 1],
        weighted(local_real, weight_real[:, :3], 0),
        weighted(local_real, weight_real[:, :3], 1),
        weighted(local_imag, weight_imag[:, :3], 0),
        weighted(local_imag, weight_imag[:, :3], 1),
    )


def body(
    tier_four,
    tier_six,
    tier_seven,
    coupling,
    eigenbasis,
    energies,
    decay_rates,
    bath_coefficients,
    occupation_five,
    local_five,
    peers_five,
    places_five,
    occupation_six,
    local_six,
    peers_six,
    places_six,
):
    count_rows = tier_four.shape[0]
    peer_count = lax.axis_size("mb")
    capacity = max(2, (12 * count_rows + 2 * peer_count - 1) // (2 * peer_count))
    matrix_shape = tier_four.shape[1:]
    column_ids = jnp.arange(4, dtype=jnp.int32)[None, :]
    wanted_five = (places_five + (column_ids >= 2).astype(jnp.int32) * count_rows).reshape(-1)
    raised_five, lowered_five = first_mode(tier_four, tier_six)
    table_five, placed_five = request_table(
        peers_five.reshape(-1), wanted_five, capacity, peer_count
    )
    got_five = fetch_plain(table_five, jnp.concatenate((tier_six, tier_four)))
    remote_five = pick_rows(got_five, placed_five).reshape((count_rows, 4) + matrix_shape)
    pair_real, pair_imag, other_real, other_imag = combine(
        tier_four,
        tier_six,
        raised_five,
        lowered_five,
        remote_five,
        local_five,
        occupation_five,
        bath_coefficients,
    )
    updated_five = settle(
        pair_real,
        pair_imag,
        other_real,
        other_imag,
        occupation_five,
        coupling,
        eigenbasis,
        energies,
        decay_rates,
    )
    raised_six, lowered_six = first_mode(updated_five, tier_seven)
    wanted_six = (places_six + (column_ids >= 2).astype(jnp.int32) * count_rows).reshape(-1)
    table_six, placed_six = request_table(peers_six.reshape(-1), wanted_six, capacity, peer_count)
    got_six = fetch_plain(table_six, jnp.concatenate((tier_seven, updated_five)))
    remote_six = pick_rows(got_six, placed_six).reshape((count_rows, 4) + matrix_shape)
    pair_real, pair_imag, other_real, other_imag = combine(
        updated_five,
        tier_seven,
        raised_six,
        lowered_six,
        remote_six,
        local_six,
        occupation_six,
        bath_coefficients,
    )
    updated_six = settle(
        pair_real,
        pair_imag,
        other_real,
        other_imag,
        occupation_six,
        coupling,
        eigenbasis,
        energies,
        decay_rates,
    )
    return (updated_five, updated_six)


def solution(mesh):
    in_specs = (
        P(("ma", "mb"), None, None, None),
        P(("ma", "mb"), None, None, None),
        P(("ma", "mb"), None, None, None),
        P(),
        P(),
        P(),
        P(),
        P(),
        P(("ma", "mb"), None),
        P(("ma", "mb"), None, None),
        P(("ma", "mb"), None),
        P(("ma", "mb"), None),
        P(("ma", "mb"), None),
        P(("ma", "mb"), None, None),
        P(("ma", "mb"), None),
        P(("ma", "mb"), None),
    )
    out_specs = (P(("ma", "mb"), None, None, None), P(("ma", "mb"), None, None, None))
    return jax.shard_map(body, mesh=mesh, in_specs=in_specs, out_specs=out_specs, check_vma=False)
```

profile of v0, /device:TPU:0, one launch (start us, length us, event | category | flops | bytes accessed | tf_op | source)
XLA Modules:
  0.0 411.9 jit_solution(3846609978342731163)
XLA Ops:
  5.0 6.3 %all-to-all-start = ((s32[8,1,6]{2,1,0:T(1,128)}), s32[8,1,6]{2,1,0:T(1,128)S(1)}, u32[]{:S(2)}, u32[]{:S(2)}) async-start(s32[8,1,6]{2,1,0:T(1,128)} %bitcast.7), calls=%async_computation | async-start | bytes 8192 | tf_op jit(solution)/shard_map/all_to_all | solution.py:77
  13.3 1.7 pad_maximum_fusion
  16.8 4.8 %all-to-all-start.2 = ((s32[8,1,6]{2,1,0:T(1,128)}), s32[8,1,6]{2,1,0:T(1,128)S(1)}, u32[]{:S(2)}, u32[]{:S(2)}) async-start(s32[8,1,6]{2,1,0:T(1,128)} %bitcast.67), calls=%async_computation.2 | async-start | bytes 8192 | tf_op jit(solution)/shard_map/all_to_all | solution.py:77
  21.9 3.6 gather_fusion
  25.5 1.7 all-to-all-done.2
  27.1 4.9 %all-to-all-start.1 = ((f32[8,6,2,128,128]{4,3,2,1,0:T(8,128)}), f32[8,6,2,128,128]{4,3,2,1,0:T(8,128)}, u32[]{:S(2)}, u32[]{:S(2)}) async-start(f32[8,6,2,128,128]{4,3,2,1,0:T(8,128)} %bitcast.407), calls=%async_computation.1 | async-start | bytes 12582912 | tf_op jit(solution)/shard_map/all_to_all | solution.py:76
  32.1 1.6 collective-permute-start.1
  33.7 1.6 copy.114
  35.2 1.6 collective-permute-start
  38.8 132.2 %all-to-all-done.1 = f32[8,6,2,128,128]{4,3,2,1,0:T(8,128)} async-done(((f32[8,6,2,128,128]{4,3,2,1,0:T(8,128)}), f32[8,6,2,128,128]{4,3,2,1,0:T(8,128)}, u32[]{:S(2)}, u32[]{:S(2)}) %all-to-all-start.1) | async-done | bytes 6291488 | tf_op jit(solution)/shard_map/all_to_all | solution.py:76
  171.0 5.7 %gather_fusion.1 = f32[32,2,128,128]{3,2,1,0:T(8,128)} fusion(f32[48,2,128,128]{3,2,1,0:T(8,128)} %bitcast.10, s32[1024]{0:T(1024)S(1)} %pad_clamp_fusion.2), kind=kCustom, calls=%fused_computation.1 | custom fusion | bytes 8388736 | tf_op jit(solution)/shard_map/gather | solution.py:87
  176.6 1.8 slice.147
  178.5 1.6 fusion.19
  180.0 4.3 %fusion.10 = f32[8,1,128,128]{3,1,2,0:T(1,128)S(1)} fusion(f32[8,3,1,1]{1,2,3,0:T(1,128)S(1)} %bitcast.431, f32[8,3,128,128]{3,2,1,0:T(8,128)S(1)} %get-tuple-element.17), kind=kOutput, calls=%fused_computation.20 | convolution fusion | flops 4718592 | bytes 2097248 | tf_op jit(solution)/shard_map/mk,mkij->mij/dot_general | solution.py:120
  184.3 4.3 %fusion.12 = f32[8,1,128,128]{3,1,2,0:T(1,128)S(1)} fusion(f32[8,3,1,1]{1,2,3,0:T(1,128)S(1)} %bitcast.432, f32[8,3,128,128]{3,2,1,0:T(8,128)S(1)} %get-tuple-element.16), kind=kOutput, calls=%fused_computation.22 | convolution fusion | flops 4718592 | bytes 2097248 | tf_op jit(solution)/shard_map/mk,mkij->mij/dot_general | solution.py:120
  189.6 4.3 %fusion.14 = f32[8,1,128,128]{3,1,2,0:T(1,128)S(1)} fusion(f32[8,3,1,1]{1,2,3,0:T(1,128)S(1)} %bitcast.429, f32[8,3,128,128]{3,2,1,0:T(8,128)S(1)} %get-tuple-element.16), kind=kOutput, calls=%fused_computation.24 | convolution fusion | flops 4718592 | bytes 2097248 | tf_op jit(solution)/shard_map/mk,mkij->mij/dot_general | solution.py:120
  193.9 4.5 %fusion.8 = f32[8,1,128,128]{3,1,2,0:T(1,128)S(1)} fusion(f32[8,3,1,1]{1,2,3,0:T(1,128)S(1)} %bitcast.430, f32[8,3,128,128]{3,2,1,0:T(8,128)S(1)} %get-tuple-element.17), kind=kOutput, calls=%fused_computation.18 | convolution fusion | flops 4718592 | bytes 2097248 | tf_op jit(solution)/shard_map/mk,mkij->mij/dot_general | solution.py:120
  198.6 3.4 fusion.25
  216.6 3.6 gather_fusion.2
  220.2 4.9 %all-to-all-start.3 = ((f32[8,6,2,128,128]{4,3,2,1,0:T(8,128)}), f32[8,6,2,128,128]{4,3,2,1,0:T(8,128)}, u32[]{:S(2)}, u32[]{:S(2)}) async-start(f32[8,6,2,128,128]{4,3,2,1,0:T(8,128)} %bitcast.408), calls=%async_computation.3 | async-start | bytes 12582912 | tf_op jit(solution)/shard_map/all_to_all | solution.py:76
  225.1 1.6 copy.137
  226.7 2.5 collective-permute-start.2
  229.4 1.6 copy.325
  232.8 131.2 %all-to-all-done.3 = f32[8,6,2,128,128]{4,3,2,1,0:T(8,128)} async-done(((f32[8,6,2,128,128]{4,3,2,1,0:T(8,128)}), f32[8,6,2,128,128]{4,3,2,1,0:T(8,128)}, u32[]{:S(2)}, u32[]{:S(2)}) %all-to-all-start.3) | async-done | bytes 6291488 | tf_op jit(solution)/shard_map/all_to_all | solution.py:76
  364.0 5.7 %gather_fusion.3 = f32[32,2,128,128]{3,2,1,0:T(8,128)} fusion(f32[48,2,128,128]{3,2,1,0:T(8,128)} %bitcast.70, s32[1024]{0:T(1024)S(1)} %pad_clamp_fusion), kind=kCustom, calls=%fused_computation.3 | custom fusion | bytes 8388736 | tf_op jit(solution)/shard_map/gather | solution.py:87
  369.7 1.8 slice.154
  371.5 1.5 fusion.17
  373.1 4.4 %fusion.2 = f32[8,1,128,128]{3,1,2,0:T(1,128)S(1)} fusion(f32[8,3,1,1]{1,2,3,0:T(1,128)S(1)} %bitcast.427, f32[8,3,128,128]{3,2,1,0:T(8,128)S(1)} %get-tuple-element.15), kind=kOutput, calls=%fused_computation.12 | convolution fusion | flops 4718592 | bytes 2097248 | tf_op jit(solution)/shard_map/mk,mkij->mij/dot_general | solution.py:120
  377.5 4.3 %fusion.4 = f32[8,1,128,128]{3,1,2,0:T(1,128)S(1)} fusion(f32[8,3,1,1]{1,2,3,0:T(1,128)S(1)} %bitcast.428, f32[8,3,128,128]{3,2,1,0:T(8,128)S(1)} %get-tuple-element.14), kind=kOutput, calls=%fused_computation.14 | convolution fusion | flops 4718592 | bytes 2097248 | tf_op jit(solution)/shard_map/mk,mkij->mij/dot_general | solution.py:120
  382.9 4.3 %fusion.6 = f32[8,1,128,128]{3,1,2,0:T(1,128)S(1)} fusion(f32[8,3,1,1]{1,2,3,0:T(1,128)S(1)} %bitcast.425, f32[8,3,128,128]{3,2,1,0:T(8,128)S(1)} %get-tuple-element.14), kind=kOutput, calls=%fused_computation.16 | convolution fusion | flops 4718592 | bytes 2097248 | tf_op jit(solution)/shard_map/mk,mkij->mij/dot_general | solution.py:120
  387.2 4.5 %fusion = f32[8,1,128,128]{3,1,2,0:T(1,128)S(1)} fusion(f32[8,3,1,1]{1,2,3,0:T(1,128)S(1)} %bitcast.426, f32[8,3,128,128]{3,2,1,0:T(8,128)S(1)} %get-tuple-element.15), kind=kOutput, calls=%fused_computation.10 | convolution fusion | flops 4718592 | bytes 2097248 | tf_op jit(solution)/shard_map/mk,mkij->mij/dot_general | solution.py:120
  392.9 3.3 fusion.23
  (136 shorter events, 45.6 us)
Async XLA Ops:
  0.6 204.2 %copy-start = (f32[128,128]{1,0:T(8,128)S(1)}, f32[128,128]{1,0:T(8,128)}, u32[]{:S(2)}) copy-start(f32[128,128]{1,0:T(8,128)} %param.20) | copy-start | bytes 196612
  5.0 11.8 %all-to-all-start = ((s32[8,1,6]{2,1,0:T(1,128)}), s32[8,1,6]{2,1,0:T(1,128)S(1)}, u32[]{:S(2)}, u32[]{:S(2)}) async-start(s32[8,1,6]{2,1,0:T(1,128)} %bitcast.7), calls=%async_computation | async-start | bytes 8192 | tf_op jit(solution)/shard_map/all_to_all | solution.py:77
  16.8 10.3 %all-to-all-start.2 = ((s32[8,1,6]{2,1,0:T(1,128)}), s32[8,1,6]{2,1,0:T(1,128)S(1)}, u32[]{:S(2)}, u32[]{:S(2)}) async-start(s32[8,1,6]{2,1,0:T(1,128)} %bitcast.67), calls=%async_computation.2 | async-start | bytes 8192 | tf_op jit(solution)/shard_map/all_to_all | solution.py:77
  27.1 4.9 %copy-start.7 = (f32[8,2,128,128]{3,2,1,0:T(8,128)S(1)}, f32[8,2,128,128]{3,2,1,0:T(8,128)}, u32[]{:S(2)}) copy-start(f32[8,2,128,128]{3,2,1,0:T(8,128)} %param.16) | copy-start | bytes 3145732
  27.1 6.5 %copy-start.3 = (f32[8,2,128,128]{3,2,1,0:T(8,128)S(1)}, f32[8,2,128,128]{3,2,1,0:T(8,128)}, u32[]{:S(2)}) copy-start(f32[8,2,128,128]{3,2,1,0:T(8,128)} %param.17) | copy-start | bytes 3145732
  27.1 143.8 %all-to-all-start.1 = ((f32[8,6,2,128,128]{4,3,2,1,0:T(8,128)}), f32[8,6,2,128,128]{4,3,2,1,0:T(8,128)}, u32[]{:S(2)}, u32[]{:S(2)}) async-start(f32[8,6,2,128,128]{4,3,2,1,0:T(8,128)} %bitcast.407), calls=%async_computation.1 | async-start | bytes 12582912 | tf_op jit(solution)/shard_map/all_to_all | solution.py:76
  32.0 4.8 %copy-start.15 = (f32[2,12]{1,0:T(2,128)S(1)}, f32[2,12]{1,0:T(2,128)}, u32[]{:S(2)}) copy-start(f32[2,12]{1,0:T(2,128)} %param.23) | copy-start | bytes 292
  32.0 4.8 %copy-start.9 = (s32[8,12]{1,0:T(8,128)S(1)}, s32[8,12]{1,0:T(8,128)}, u32[]{:S(2)}) copy-start(s32[8,12]{1,0:T(8,128)} %param.24) | copy-start | bytes 1156
  32.0 4.8 %copy-start.10 = (s32[8,12]{1,0:T(8,128)S(1)}, s32[8,12]{1,0:T(8,128)}, u32[]{:S(2)}) copy-start(s32[8,12]{1,0:T(8,128)} %param.28) | copy-start | bytes 1156
  32.1 5.6 %copy-start.11 = (s32[8,2,9]{2,1,0:T(2,128)S(1)}, s32[8,2,9]{2,1,0:T(2,128)}, u32[]{:S(2)}) copy-start(s32[8,2,9]{2,1,0:T(2,128)} %param.25) | copy-start | bytes 1732
  32.1 6.1 %copy-start.14 = (f32[12]{0:T(128)S(1)}, f32[12]{0:T(128)}, u32[]{:S(2)}) copy-start(f32[12]{0:T(128)} %param.22) | copy-start | bytes 148
  32.1 6.2 %copy-start.13 = (f32[128]{0:T(128)S(1)}, f32[128]{0:T(128)}, u32[]{:S(2)}) copy-start(f32[128]{0:T(128)} %param.21) | copy-start | bytes 1540
  32.1 146.3 %collective-permute-start.1 = (f32[8,2,128,128]{3,2,1,0:T(8,128)S(1)}, f32[8,2,128,128]{3,2,1,0:T(8,128)}, u32[]{:S(2)}, u32[]{:S(2)}) collective-permute-start(f32[8,2,128,128]{3,2,1,0:T(8,128)S(1)} %copy-done.7), channel_id=1, source_target_pairs={{0,8},{8,16},{16,24},{24,0},{1,9},{9,17},{17,25},{25,1},{2,10},{10... | collective-permute-start | bytes 3145736 | tf_op jit(solution)/shard_map/ppermute | solution.py:11
  35.2 163.4 %collective-permute-start = (f32[8,2,128,128]{3,0,2,1:T(8,128)}, f32[8,2,128,128]{3,0,2,1:T(8,128)}, u32[]{:S(2)}, u32[]{:S(2)}) collective-permute-start(f32[8,2,128,128]{3,0,2,1:T(8,128)} %copy.114), channel_id=1, source_target_pairs={{0,24},{8,0},{16,8},{24,16},{1,25},{9,1},{17,9},{25,17},{2,26},{10... | collective-permute-start | bytes 3145736 | tf_op jit(solution)/shard_map/ppermute | solution.py:11
  189.6 8.8 %copy-start.2 = (f32[32,2,128,128]{3,2,1,0:T(8,128)S(1)}, f32[32,2,128,128]{3,2,1,0:T(8,128)}, u32[]{:S(2)}) copy-start(f32[32,2,128,128]{3,2,1,0:T(8,128)} %gather_fusion.1) | copy-start | bytes 12582916
  202.0 1.1 copy-start.6
  214.4 2.0 copy-start.4
  220.2 4.9 %copy-start.5 = (f32[8,2,128,128]{3,2,1,0:T(8,128)S(1)}, f32[8,2,128,128]{3,2,1,0:T(8,128)}, u32[]{:S(2)}) copy-start(f32[8,2,128,128]{3,2,1,0:T(8,128)} %param.18) | copy-start | bytes 3145732
  220.2 143.8 %all-to-all-start.3 = ((f32[8,6,2,128,128]{4,3,2,1,0:T(8,128)}), f32[8,6,2,128,128]{4,3,2,1,0:T(8,128)}, u32[]{:S(2)}, u32[]{:S(2)}) async-start(f32[8,6,2,128,128]{4,3,2,1,0:T(8,128)} %bitcast.408), calls=%async_computation.3 | async-start | bytes 12582912 | tf_op jit(solution)/shard_map/all_to_all | solution.py:76
  226.7 4.4 %copy-start.12 = (s32[8,2,9]{2,1,0:T(2,128)S(1)}, s32[8,2,9]{2,1,0:T(2,128)}, u32[]{:S(2)}) copy-start(s32[8,2,9]{2,1,0:T(2,128)} %param.29) | copy-start | bytes 1732
  226.7 165.2 %collective-permute-start.2 = (f32[8,2,128,128]{3,0,2,1:T(8,128)}, f32[8,2,128,128]{3,0,2,1:T(8,128)}, u32[]{:S(2)}, u32[]{:S(2)}) collective-permute-start(f32[8,2,128,128]{3,0,2,1:T(8,128)} %copy.137), channel_id=1, source_target_pairs={{0,24},{8,0},{16,8},{24,16},{1,25},{9,1},{17,9},{25,17},{2,26},{10... | collective-permute-start | bytes 3145736 | tf_op jit(solution)/shard_map/ppermute | solution.py:11
  229.2 142.3 %collective-permute-start.3 = (f32[8,2,128,128]{3,2,0,1:T(8,128)S(1)}, f32[8,2,128,128]{3,2,0,1:T(8,128)}, u32[]{:S(2)}, u32[]{:S(2)}) collective-permute-start(f32[8,2,128,128]{3,2,0,1:T(8,128)S(1)} %pad_maximum_fusion.3), channel_id=1, source_target_pairs={{0,8},{8,16},{16,24},{24,0},{1,9},{9,17},{17,25},{25,1},{2,10},{10... | collective-permute-start | bytes 3145736 | tf_op jit(solution)/shard_map/ppermute | solution.py:11
  382.9 8.8 %copy-start.1 = (f32[32,2,128,128]{3,2,1,0:T(8,128)S(1)}, f32[32,2,128,128]{3,2,1,0:T(8,128)}, u32[]{:S(2)}) copy-start(f32[32,2,128,128]{3,2,1,0:T(8,128)} %gather_fusion.3) | copy-start | bytes 12582916
  391.7 1.2 copy-start.8
where the time goes:
time: 415 us; the launch traced here: 412 us
  waiting for transfers between devices  265 us (64%)
  matrix products  73.2 us (18%)
  local copies, waits for them, and re-layouts  36.9 us (9%)
  starting transfers between devices  26.6 us (6%)
  other arithmetic  8.24 us (2%)
    all_to_all x2, waiting for transfers between devices, fetch_plain(): lax.all_to_all(store[lax.all_to_all(table, 'mb', split_axis=0, concat_axi...  263 us
    dot_general x8, matrix products, weighted(): jnp.einsum('mk,mkij->mij', edge_weights, edges[:, :, part_index], precisi...  34.8 us
    gather x2, local copies, waits for them, and re-layouts, pick_rows(): return flat_rows[placed]  11.3 us
    dot_general x12, matrix products, right_product(): return jnp.einsum('mij,jk->mik', batch, matrix, precision=HIGHEST)  11.3 us
    all_to_all x2, starting transfers between devices, fetch_plain(): lax.all_to_all(table, 'mb', split_axis=0, concat_axis=0, tiled=True)  11.2 us
    dot_general x12, matrix products, left_product(): return jnp.einsum('ij,mjk->mik', matrix, batch, precision=HIGHEST)  10.7 us
    unnamed x41, local copies, waits for them, and re-layouts  10.2 us
    all_to_all x2, starting transfers between devices, fetch_plain(): lax.all_to_all(store[lax.all_to_all(table, 'mb', split_axis=0, concat_axi...  9.76 us
  transfers between devices with their start and end apart: 8, of which 4 were waited for; matrix products, arithmetic and copies ran while one was open for 18% of the time, Pallas kernels for 0%

commit v1 on v0

v1 whole, which is shorter than its diff:
```python
import functools

import jax
import jax.numpy as jnp
from jax import lax
from jax.experimental import pallas as pl
from jax.experimental.pallas import tpu as pltpu
from jax.sharding import PartitionSpec as P

SMEM = pltpu.SMEM
VMEM = pltpu.VMEM
HALVES = 2


def split(x):
    high = x.astype(jnp.bfloat16)
    return high, (x - high.astype(jnp.float32)).astype(jnp.bfloat16)


def as_left(w):
    high, low = split(w)
    return jnp.concatenate([high, high, low], axis=1)


def as_right(w):
    high, low = split(w)
    return jnp.concatenate([high, high, low], axis=0)


def left_dot(w_left, x):
    high, low = split(x)
    return jnp.dot(
        w_left, jnp.concatenate([high, low, high], axis=0), preferred_element_type=jnp.float32
    )


def right_dot(x, w_right):
    high, low = split(x)
    return jnp.dot(
        jnp.concatenate([high, low, high], axis=1), w_right, preferred_element_type=jnp.float32
    )


def sandwich(w_left, real, imag, w_right):
    n = real.shape[0]
    right = right_dot(jnp.concatenate([real, imag], axis=0), w_right)
    both = left_dot(w_left, jnp.concatenate([right[:n], right[n:]], axis=1))
    return both[:, :n], both[:, n:]


def drive_of(mixed, turned, c_left, c_right):
    n = mixed.shape[-1]
    ahead = left_dot(
        c_left, jnp.concatenate([mixed[1] + turned[0], mixed[0] - turned[1]], axis=1)
    )
    behind = right_dot(
        jnp.concatenate([mixed[1] - turned[0], mixed[0] + turned[1]], axis=0), c_right
    )
    return behind[:n] - ahead[:, :n], ahead[:, n:] - behind[n:]


def add_requests(
    row, column, target, rows, place, table, bath, upper, lower, mixed, turned
):
    chip = place[0]
    core = place[1]
    for j in range(4):
        peer = table[target, column + row * 4 + j]
        spot = table[target, column + rows * 4 + row * 4 + j]
        here = peer >> 1 == chip
        for sibling in range(2):
            own = (peer & 1 == core) if sibling == 0 else (peer & 1 != core)

            @pl.when(jnp.logical_and(here, own))
            def _(j=j, sibling=sibling, spot=spot):
                if j < 2:
                    mixed[...] += upper[sibling][spot]
                else:
                    mode = j - 1
                    count = table[target, column + rows * 8 + row * 2 + j - 2].astype(jnp.float32)
                    source = lower[sibling][spot]
                    mixed[...] += (count * bath[0, mode]) * source
                    turned[...] += (count * bath[1, mode]) * source


def partial_kernel(
    slot, column, place, table, bath, upper_own, upper_sib, lower_own, lower_sib, c_ref, *rest
):
    outs, (mixed, turned) = rest[:-2], rest[-2:]
    rows = upper_own.shape[0]
    target = place[2 + slot]
    c_left = as_left(c_ref[...])
    c_right = as_right(c_ref[...])
    per = rows // len(outs)
    for half, out in enumerate(outs):

        @pl.loop(0, per)
        def _(m, half=half, out=out):
            mixed[...] = jnp.zeros_like(mixed)
            turned[...] = jnp.zeros_like(turned)
            add_requests(
                half * per + m,
                column,
                target,
                rows,
                place,
                table,
                bath,
                (upper_own, upper_sib),
                (lower_own, lower_sib),
                mixed,
                turned,
            )
            real, imag = drive_of(mixed[...], turned[...], c_left, c_right)
            out[m, 0] = real
            out[m, 1] = imag


def own_kernel(
    slot,
    column,
    place,
    table,
    bath,
    nearby,
    occupation,
    upper_own,
    upper_sib,
    lower_own,
    lower_sib,
    raised,
    lowered,
    c_ref,
    out,
    mixed,
    turned,
):
    rows = upper_own.shape[0]
    modes = bath.shape[1]
    target = place[2 + slot]
    c_left = as_left(c_ref[...])
    c_right = as_right(c_ref[...])

    @pl.loop(0, rows)
    def _(m):
        count = occupation[m, 0].astype(jnp.float32)
        below = lowered[m]
        mixed[...] = raised[m] + (count * bath[0, 0]) * below
        turned[...] = (count * bath[1, 0]) * below
        add_requests(
            m,
            column,
            target,
            rows,
            place,
            table,
            bath,
            (upper_own, upper_sib),
            (lower_own, lower_sib),
            mixed,
            turned,
        )
        for k in range(3, modes):
            mixed[...] += upper_own[nearby[m, k - 3]]
            held = occupation[m, k]

            @pl.when(held > 0)
            def _(k=k, held=held):
                source = lower_own[nearby[m, modes - 3 + k - 3]]
                mixed[...] += (held.astype(jnp.float32) * bath[0, k]) * source
                turned[...] += (held.astype(jnp.float32) * bath[1, k]) * source

        real, imag = drive_of(mixed[...], turned[...], c_left, c_right)
        out[m, 0] = real
        out[m, 1] = imag


def solved(real, imag, damping, splitting):
    inverse = 1.0 / (damping * damping + splitting * splitting)
    factor_real = -damping * inverse
    factor_imag = splitting * inverse
    return real * factor_real - imag * factor_imag, real * factor_imag + imag * factor_real


def solve_kernel(
    arrivals, turn_in, turn_out, occupation, decay, e_row, e_column, e_ref, et_ref, own, *rest
):
    parts, outs = rest[:arrivals], rest[arrivals:]
    rows = own.shape[0]
    splitting = e_column[...] - e_row[...]
    if turn_in:
        in_left = as_left(et_ref[...])
        in_right = as_right(e_ref[...])
    if turn_out:
        out_left = as_left(e_ref[...])
        out_right = as_right(et_ref[...])
    per = parts[0].shape[0]
    for m in range(rows):
        real = own[m, 0]
        imag = own[m, 1]
        for part in parts[m // per :: rows // per]:
            real = real + part[m % per, 0]
            imag = imag + part[m % per, 1]
        if turn_in:
            real, imag = sandwich(in_left, real, imag, in_right)
        damping = occupation[m, 0].astype(jnp.float32) * decay[0]
        for k in range(1, decay.shape[0]):
            damping = damping + occupation[m, k].astype(jnp.float32) * decay[k]
        real, imag = solved(real, imag, damping, splitting)
        if turn_out:
            real, imag = sandwich(out_left, real, imag, out_right)
        outs[0][m, 0] = real
        outs[0][m, 1] = imag


def turn_kernel(left_ref, right_ref, x, out):
    w_left = as_left(left_ref[...])
    w_right = as_right(right_ref[...])
    for m in range(x.shape[0]):
        real, imag = sandwich(w_left, x[m, 0], x[m, 1], w_right)
        out[m, 0] = real
        out[m, 1] = imag


def turn_one_kernel(left_ref, right_ref, x, out):
    out[...] = left_dot(as_left(left_ref[...]), right_dot(x[...], as_right(right_ref[...])))


def call(kernel, outs, scalars, arrays, scratch=(), products=0, name=None):
    n = arrays[0].shape[-1]
    moved = sum(a.size * 4 for a in arrays) + sum(o.size * 4 for o in outs)
    return pl.pallas_call(
        kernel,
        out_shape=outs,
        in_specs=[pl.BlockSpec(memory_space=SMEM)] * len(scalars)
        + [pl.BlockSpec(memory_space=VMEM)] * len(arrays),
        out_specs=[pl.BlockSpec(memory_space=VMEM)] * len(outs),
        scratch_shapes=scratch,
        compiler_params=pltpu.CompilerParams(vmem_limit_bytes=40 * 1024 * 1024),
        cost_estimate=pl.CostEstimate(
            flops=products * 6 * n**3, bytes_accessed=moved, transcendentals=0
        ),
        name=name,
    )(*scalars, *arrays)


def body(
    tier_four,
    tier_six,
    tier_seven,
    coupling,
    eigenbasis,
    energies,
    decay_rates,
    bath_coefficients,
    occupation_five,
    local_five,
    peers_five,
    places_five,
    occupation_six,
    local_six,
    peers_six,
    places_six,
):
    rows = tier_four.shape[0]
    n = tier_four.shape[-1]
    peer_count = lax.axis_size("mb")
    row_count = lax.axis_size("ma")
    chips = peer_count // 2
    whole = jax.ShapeDtypeStruct(tier_four.shape, jnp.float32)
    piece = jax.ShapeDtypeStruct((rows // HALVES,) + tier_four.shape[1:], jnp.float32)
    pair = [pltpu.VMEM(tier_four.shape[1:], jnp.float32)] * 2

    def table_of(peers, places, occupation):
        return [peers.reshape(-1), places.reshape(-1), occupation[:, 1:3].reshape(-1)]

    mine = jnp.concatenate(
        table_of(peers_five, places_five, occupation_five)
        + table_of(peers_six, places_six, occupation_six)
    )
    table = lax.all_to_all(
        jnp.broadcast_to(mine[None], (peer_count,) + mine.shape),
        "mb",
        split_axis=0,
        concat_axis=0,
        tiled=True,
    )
    columns = (0, mine.shape[0] // 2)

    index = lax.axis_index("mb")
    chip = index // 2
    core = index % 2
    mirrored = chip >= chips // 2
    depth = jnp.where(mirrored, chips - 1 - chip, chip)
    order = jnp.arange(chips, dtype=jnp.int32)
    ahead = chips - 1 - depth
    seen = jnp.where(order < ahead, chips - 1 - order, order - ahead)
    seen = jnp.where(order == chips - 1, depth, seen)
    goal = jnp.where(mirrored, chips - 1 - seen, seen) * 2 + core
    place = jnp.concatenate([chip[None], core[None], goal]).astype(jnp.int32)

    def sibling_of(array):
        return lax.ppermute(array, "mb", [(i, i ^ 1) for i in range(peer_count)])

    def along(array, by):
        return lax.ppermute(
            array, "ma", [(i, (i + by) % row_count) for i in range(row_count)]
        )

    def hop(array, step):
        pairs = []
        for c in range(2):
            pairs.append((step * 2 + c, (step + 1) * 2 + c))
            pairs.append(((chips - 1 - step) * 2 + c, (chips - 2 - step) * 2 + c))
        return lax.ppermute(array, "mb", pairs)

    def reduce_line(tier, upper, lower, c):
        sent = {}
        for slot in range(chips - 1):
            sent[slot] = call(
                functools.partial(partial_kernel, slot, columns[tier]),
                [piece] * HALVES,
                [place, table, bath_coefficients],
                [*upper, *lower, c],
                pair,
                rows * 4,
                f"partial_{tier}_{slot}",
            )
        arrived = {}
        last = []
        for goal_step in range(chips - 1, 0, -1):
            for half in range(HALVES):
                for step in range(goal_step):
                    slot = chips - 1 - goal_step + (step if step >= chips // 2 else 0)
                    message = sent[slot][half]
                    if step > 0:
                        message = message + arrived[step - 1, half]
                    arrived[step, half] = hop(message, step)
                last.append(arrived[goal_step - 1, half])
        return last

    def own_part(tier, upper, lower, raised, lowered, nearby, occupation, c):
        return call(
            functools.partial(own_kernel, chips - 1, columns[tier]),
            [whole],
            [place, table, bath_coefficients, nearby.reshape(rows, -1), occupation],
            [*upper, *lower, raised, lowered, c],
            pair,
            rows * 4,
            f"own_{tier}",
        )[0]

    turned = jnp.transpose(eigenbasis)
    e_row = energies[None, :]
    e_column = energies[:, None]

    def solve(own, last, occupation, turn_in, turn_out, name):
        return call(
            functools.partial(solve_kernel, len(last), turn_in, turn_out),
            [whole],
            [occupation, decay_rates],
            [e_row, e_column, eigenbasis, turned, own, *last],
            (),
            rows * 4,
            name,
        )[0]

    upper_five = (tier_six, sibling_of(tier_six))
    lower_five = (tier_four, sibling_of(tier_four))
    raised_five = along(tier_six, -1)
    lowered_five = along(tier_four, 1)
    last_five = reduce_line(0, upper_five, lower_five, coupling)
    own_five = own_part(
        0, upper_five, lower_five, raised_five, lowered_five, local_five, occupation_five, coupling
    )

    tilted = call(
        turn_one_kernel,
        [jax.ShapeDtypeStruct((n, n), jnp.float32)],
        [],
        [turned, eigenbasis, coupling],
        (),
        2,
        "tilt_coupling",
    )[0]
    eigen_seven = call(
        turn_kernel, [whole], [], [turned, eigenbasis, tier_seven], (), rows * 4, "tilt_seven"
    )[0]
    upper_six = (eigen_seven, sibling_of(eigen_seven))
    raised_six = along(eigen_seven, -1)

    eigen_five = solve(own_five, last_five, occupation_five, True, False, "solve_five")
    lower_six = (eigen_five, sibling_of(eigen_five))
    lowered_six = along(eigen_five, 1)
    last_six = reduce_line(1, upper_six, lower_six, tilted)
    updated_five = call(
        turn_kernel, [whole], [], [eigenbasis, turned, eigen_five], (), rows * 4, "back_five"
    )[0]
    own_six = own_part(
        1, upper_six, lower_six, raised_six, lowered_six, local_six, occupation_six, tilted
    )
    updated_six = solve(own_six, last_six, occupation_six, False, True, "solve_six")
    return (updated_five, updated_six)


def solution(mesh):
    by_block = P(("ma", "mb"))
    in_specs = (by_block,) * 3 + (P(),) * 5 + (by_block,) * 8
    return jax.shard_map(
        body, mesh=mesh, in_specs=in_specs, out_specs=(by_block, by_block), check_vma=False
    )
```

time: 415 us -> 219 us (0.53)
  waiting for transfers between devices: 265 us -> 84.9 us
  matrix products: 73.2 us -> 0 us
  Pallas kernels: 0 us -> 46.5 us
  starting transfers between devices: 26.6 us -> 55.9 us
  local copies, waits for them, and re-layouts: 36.9 us -> 19.8 us
    all_to_all x4 -> x1, waiting for transfers between devices: 265 us -> 5.52 us  [body(): lax.all_to_all(jnp.broadcast_to(mine[None], (peer_count,) + mine.shape),...]
    ppermute x4 -> x32, waiting for transfers between devices: 0.01 us -> 79.4 us  [the longest x24 77.1 us: hop(): return lax.ppermute(array, 'mb', pairs)]
    dot_general x48 -> x0, matrix products: 73.2 us -> none  [the longest x8 34.8 us: weighted(): jnp.einsum('mk,mkij->mij', edge_weights, edges[:, :, part_index], precisi...]
    pallas_call x0 -> x13, Pallas kernels: none -> 46.5 us  [call(): pl.pallas_call(kernel, out_shape=outs, in_specs=[pl.BlockSpec(memory_spac...]
    ppermute x4 -> x32, starting transfers between devices: 5.66 us -> 49.6 us  [the longest x24 42.2 us: hop(): return lax.ppermute(array, 'mb', pairs)]
    gather x4 -> x0, local copies, waits for them, and re-layouts: 18.4 us -> none  [the longest x2 11.3 us: pick_rows(): return flat_rows[placed]]
    all_to_all x4 -> x1, starting transfers between devices: 20.9 us -> 6.3 us  [body(): lax.all_to_all(jnp.broadcast_to(mine[None], (peer_count,) + mine.shape),...]
    add x1 -> x13, other arithmetic: 0.78 us -> 9.18 us  [the longest x12 9.17 us: reduce_line(): message = message + arrived[step - 1, half]]
  transfers between devices with their start and end apart: 8 -> 33, of which waited for: 4 -> 14; matrix products, arithmetic and copies ran while one was open for 18% -> 5% of each run, Pallas kernels for 0% -> 16%
where the time goes in v1:
time: 219 us; the launch traced here: 218 us
  waiting for transfers between devices  84.9 us (39%)
  starting transfers between devices  55.9 us (26%)
  Pallas kernels  46.5 us (21%)
  local copies, waits for them, and re-layouts  19.8 us (9%)
  other arithmetic  9.25 us (4%)
    ppermute x24, waiting for transfers between devices, hop(): return lax.ppermute(array, 'mb', pairs)  77.1 us
    pallas_call x13, Pallas kernels, call(): pl.pallas_call(kernel, out_shape=outs, in_specs=[pl.BlockSpec(memory_spac...  46.5 us
    ppermute x24, starting transfers between devices, hop(): return lax.ppermute(array, 'mb', pairs)  42.2 us
    unnamed x68, local copies, waits for them, and re-layouts  18.2 us
    add x12, other arithmetic, reduce_line(): message = message + arrived[step - 1, half]  9.17 us
    ppermute x4, starting transfers between devices, along(): lax.ppermute(array, 'ma', [(i, (i + by) % row_count) for i in range(row_c...  6.7 us
    all_to_all x1, starting transfers between devices, body(): lax.all_to_all(jnp.broadcast_to(mine[None], (peer_count,) + mine.shape),...  6.3 us
    all_to_all x1, waiting for transfers between devices, body(): lax.all_to_all(jnp.broadcast_to(mine[None], (peer_count,) + mine.shape),...  5.52 us
  transfers between devices with their start and end apart: 33, of which 14 were waited for; matrix products, arithmetic and copies ran while one was open for 5% of the time, Pallas kernels for 16%

profile of v1, /device:TPU:0, one launch (start us, length us, event | category | flops | bytes accessed | tf_op | source)
XLA Modules:
  0.0 217.5 jit_solution(10959656940623584594)
XLA Ops:
  5.8 6.3 %all-to-all-start = ((s32[8,1,160]{2,1,0:T(1,128)}), s32[8,1,160]{2,1,0:T(1,128)S(1)}, u32[]{:S(2)}, u32[]{:S(2)}) async-start(s32[8,1,160]{2,1,0:T(1,128)} %broadcast_in_dim.27), calls=%async_computation | async-start | bytes 16384 | tf_op jit(solution)/shard_map/all_to_all | solution.py:281
  12.2 5.5 %all-to-all-done = s32[8,1,160]{2,1,0:T(1,128)S(1)} async-done(((s32[8,1,160]{2,1,0:T(1,128)}), s32[8,1,160]{2,1,0:T(1,128)S(1)}, u32[]{:S(2)}, u32[]{:S(2)}) %all-to-all-start) | async-done | bytes 5152 | tf_op jit(solution)/shard_map/all_to_all | solution.py:281
  20.8 3.2 %partial_0_0.1 = (f32[4,2,128,128]{3,2,1,0:T(8,128)S(1)}, f32[4,2,128,128]{3,2,1,0:T(8,128)S(1)}) custom-call(s32[6]{0:T(128)S(1)} %pad_add_fusion.place, s32[8,160]{1,0:T(8,128)S(1)} %bitcast.13, f32[2,12]{1,0:T(2,128)S(1)} %copy-done.21, f32[8,2,128,128]{3,2,1,0:T(8,128)S(1)} %copy-done, f32[8,2,128,128]{3,2,1,0:T(8,128)S(1)} %collective-permute-done.upper_sib, ...), custom_call_target="tpu_custom_call" | custom-call | flops 402653184 | bytes 5308416 | tf_op jit(solution)/shard_map/partial_0_0/pallas_call | solution.py:232
  24.1 2.7 %collective-permute-start.4 = (f32[4,2,128,128]{3,2,1,0:T(8,128)S(1)}, f32[4,2,128,128]{3,2,1,0:T(8,128)S(1)}, u32[]{:S(2)}, u32[]{:S(2)}) collective-permute-start(f32[4,2,128,128]{3,2,1,0:T(8,128)S(1)} %get-tuple-element.15), channel_id=1, source_target_pairs={{0,2},{6,4},{1,3},{7,5},{8,10},{14,12},{9,11},{15,13},{16,18},{22,... | collective-permute-start | bytes 1572872 | tf_op jit(solution)/shard_map/ppermute | solution.py:315
  28.1 3.3 %partial_0_1.1 = (f32[4,2,128,128]{3,2,1,0:T(8,128)S(1)}, f32[4,2,128,128]{3,2,1,0:T(8,128)S(1)}) custom-call(s32[6]{0:T(128)S(1)} %pad_add_fusion.place, s32[8,160]{1,0:T(8,128)S(1)} %bitcast.14, f32[2,12]{1,0:T(2,128)S(1)} %copy-done.21, f32[8,2,128,128]{3,2,1,0:T(8,128)S(1)} %copy-done, f32[8,2,128,128]{3,2,1,0:T(8,128)S(1)} %collective-permute-done.upper_sib, ...), custom_call_target="tpu_custom_call" | custom-call | flops 402653184 | bytes 5308416 | tf_op jit(solution)/shard_map/partial_0_1/pallas_call | solution.py:232
  32.7 2.6 %collective-permute-start.2 = (f32[8,2,128,128]{3,2,1,0:T(8,128)S(1)}, f32[8,2,128,128]{3,2,1,0:T(8,128)S(1)}, u32[]{:S(2)}, u32[]{:S(2)}) collective-permute-start(f32[8,2,128,128]{3,2,1,0:T(8,128)S(1)} %copy-done), channel_id=1, source_target_pairs={{0,24},{8,0},{16,8},{24,16},{1,25},{9,1},{17,9},{25,17},{2,26},{10... | collective-permute-start | bytes 3145736 | tf_op jit(solution)/shard_map/ppermute | solution.py:306
  35.3 3.7 %collective-permute-done.4 = f32[4,2,128,128]{3,2,1,0:T(8,128)S(1)} collective-permute-done((f32[4,2,128,128]{3,2,1,0:T(8,128)S(1)}, f32[4,2,128,128]{3,2,1,0:T(8,128)S(1)}, u32[]{:S(2)}, u32[]{:S(2)}) %collective-permute-start.4) | collective-permute-done | bytes 524320 | tf_op jit(solution)/shard_map/ppermute | solution.py:315
  39.1 4.4 %collective-permute-start.12 = (f32[4,2,128,128]{3,2,1,0:T(8,128)S(1)}, f32[4,2,128,128]{3,2,1,0:T(8,128)S(1)}, u32[]{:S(2)}, u32[]{:S(2)}) collective-permute-start(f32[4,2,128,128]{3,2,1,0:T(8,128)S(1)} %get-tuple-element.19), channel_id=1, source_target_pairs={{0,2},{6,4},{1,3},{7,5},{8,10},{14,12},{9,11},{15,13},{16,18},{22,... | collective-permute-start | bytes 1572872 | tf_op jit(solution)/shard_map/ppermute | solution.py:315
  43.5 6.8 %collective-permute-done.7 = f32[4,2,128,128]{3,2,1,0:T(8,128)S(1)} collective-permute-done((f32[4,2,128,128]{3,2,1,0:T(8,128)S(1)}, f32[4,2,128,128]{3,2,1,0:T(8,128)S(1)}, u32[]{:S(2)}, u32[]{:S(2)}) %collective-permute-start.7) | collective-permute-done | bytes 524320 | tf_op jit(solution)/shard_map/ppermute | solution.py:315
  51.0 10.5 %collective-permute-done.10 = f32[4,2,128,128]{3,2,1,0:T(8,128)S(1)} collective-permute-done((f32[4,2,128,128]{3,2,1,0:T(8,128)S(1)}, f32[4,2,128,128]{3,2,1,0:T(8,128)S(1)}, u32[]{:S(2)}, u32[]{:S(2)}) %collective-permute-start.10) | collective-permute-done | bytes 524320 | tf_op jit(solution)/shard_map/ppermute | solution.py:315
  62.2 4.1 %partial_0_2.1 = (f32[4,2,128,128]{3,2,1,0:T(8,128)S(1)}, f32[4,2,128,128]{3,2,1,0:T(8,128)}) custom-call(s32[6]{0:T(128)S(1)} %pad_add_fusion.place, s32[8,160]{1,0:T(8,128)S(1)} %bitcast.15, f32[2,12]{1,0:T(2,128)S(1)} %copy-done.21, f32[8,2,128,128]{3,2,1,0:T(8,128)S(1)} %copy-done, f32[8,2,128,128]{3,2,1,0:T(8,128)S(1)} %collective-permute-done.upper_sib, ...), custom_call_target="tpu_custom_call" | custom-call | flops 402653184 | bytes 5308416 | tf_op jit(solution)/shard_map/partial_0_2/pallas_call | solution.py:232
  66.3 5.3 %collective-permute-done.12 = f32[4,2,128,128]{3,2,1,0:T(8,128)S(1)} collective-permute-done((f32[4,2,128,128]{3,2,1,0:T(8,128)S(1)}, f32[4,2,128,128]{3,2,1,0:T(8,128)S(1)}, u32[]{:S(2)}, u32[]{:S(2)}) %collective-permute-start.12) | collective-permute-done | bytes 524320 | tf_op jit(solution)/shard_map/ppermute | solution.py:315
  71.6 4.4 %collective-permute-start.14 = (f32[4,2,128,128]{3,2,1,0:T(8,128)S(1)}, f32[4,2,128,128]{3,2,1,0:T(8,128)S(1)}, u32[]{:S(2)}, u32[]{:S(2)}) collective-permute-start(f32[4,2,128,128]{3,2,1,0:T(8,128)S(1)} %get-tuple-element.14), channel_id=1, source_target_pairs={{0,2},{6,4},{1,3},{7,5},{8,10},{14,12},{9,11},{15,13},{16,18},{22,... | collective-permute-start | bytes 1572872 | tf_op jit(solution)/shard_map/ppermute | solution.py:315
  93.7 2.1 tilt_seven.1.upper_own
  98.3 5.2 %own_0.1.own = f32[8,2,128,128]{3,2,1,0:T(8,128)S(1)} custom-call(s32[6]{0:T(128)S(1)} %pad_add_fusion.place, s32[8,160]{1,0:T(8,128)S(1)} %bitcast.16, f32[2,12]{1,0:T(2,128)S(1)} %copy-done.21, s32[8,18]{1,0:T(8,128)S(1)} %reshape.40.nearby, s32[8,12]{1,0:T(8,128)S(1)} %copy-done.22, f32[8,2,128,128]{3,2,1,0:T(8,128)S(1)} %copy-done.1, ...), custom_call_target="tpu_custom_call" | custom-call | flops 402653184 | bytes 7405568 | tf_op jit(solution)/shard_map/own_0/pallas_call | solution.py:232
  104.6 8.8 %collective-permute-done.9.rest_1_ = f32[4,2,128,128]{3,2,1,0:T(8,128)} collective-permute-done((f32[4,2,128,128]{3,2,1,0:T(8,128)}, f32[4,2,128,128]{3,2,1,0:T(8,128)}, u32[]{:S(2)}, u32[]{:S(2)}) %collective-permute-start.9) | collective-permute-done | bytes 524320 | tf_op jit(solution)/shard_map/ppermute | solution.py:315
  113.5 3.8 %solve_five.1.x.lower_own = f32[8,2,128,128]{3,2,1,0:T(8,128)S(1)} custom-call(s32[8,12]{1,0:T(8,128)S(1)} %copy-done.22, f32[12]{0:T(128)S(1)} %copy-done.25, f32[1,128]{1,0:T(1,128)S(1)} %bitcast.22, f32[128,1]{1,0:T(8,128)S(1)} %copy.37.e_column, f32[128,128]{1,0:T(8,128)S(1)} %copy-done.6, f32[128,128]{1,0:T(8,128)S(1)} %bitcast.9, ...), custom_call_target="tpu_custom_call" | custom-call | flops 402653184 | bytes 5374976 | tf_op jit(solution)/shard_map/solve_five/pallas_call | solution.py:232
  117.7 2.3 %collective-permute-done.17.lower_sib = f32[8,2,128,128]{3,2,1,0:T(8,128)S(1)} collective-permute-done((f32[8,2,128,128]{3,2,1,0:T(8,128)S(1)}, f32[8,2,128,128]{3,2,1,0:T(8,128)S(1)}, u32[]{:S(2)}, u32[]{:S(2)}) %collective-permute-start.17) | collective-permute-done | bytes 1048608 | tf_op jit(solution)/shard_map/ppermute | solution.py:303
  120.0 3.4 %partial_1_0.1 = (f32[4,2,128,128]{3,2,1,0:T(8,128)S(1)}, f32[4,2,128,128]{3,2,1,0:T(8,128)S(1)}) custom-call(s32[6]{0:T(128)S(1)} %pad_add_fusion.place, s32[8,160]{1,0:T(8,128)S(1)} %bitcast.17, f32[2,12]{1,0:T(2,128)S(1)} %copy-done.21, f32[8,2,128,128]{3,2,1,0:T(8,128)S(1)} %tilt_seven.1.upper_own, ...), custom_call_target="tpu_custom_call" | custom-call | flops 402653184 | bytes 5308416 | tf_op jit(solution)/shard_map/partial_1_0/pallas_call | solution.py:232
  126.1 3.4 %partial_1_1.1 = (f32[4,2,128,128]{3,2,1,0:T(8,128)S(1)}, f32[4,2,128,128]{3,2,1,0:T(8,128)S(1)}) custom-call(s32[6]{0:T(128)S(1)} %pad_add_fusion.place, s32[8,160]{1,0:T(8,128)S(1)} %bitcast.18, f32[2,12]{1,0:T(2,128)S(1)} %copy-done.21, f32[8,2,128,128]{3,2,1,0:T(8,128)S(1)} %tilt_seven.1.upper_own, ...), custom_call_target="tpu_custom_call" | custom-call | flops 402653184 | bytes 5308416 | tf_op jit(solution)/shard_map/partial_1_1/pallas_call | solution.py:232
  130.8 2.6 %collective-permute-start.18 = (f32[8,2,128,128]{3,2,1,0:T(8,128)S(1)}, f32[8,2,128,128]{3,2,1,0:T(8,128)S(1)}, u32[]{:S(2)}, u32[]{:S(2)}) collective-permute-start(f32[8,2,128,128]{3,2,1,0:T(8,128)S(1)} %tilt_seven.1.upper_own), channel_id=1, source_target_pairs={{0,24},{8,0},{16,8},{24,16},{1,25},{9,1},{17,9},{25,17},{2,26},{10... | collective-permute-start | bytes 3145736 | tf_op jit(solution)/shard_map/ppermute | solution.py:306
  134.8 2.2 %collective-permute-done.20 = f32[4,2,128,128]{3,2,1,0:T(8,128)S(1)} collective-permute-done((f32[4,2,128,128]{3,2,1,0:T(8,128)S(1)}, f32[4,2,128,128]{3,2,1,0:T(8,128)S(1)}, u32[]{:S(2)}, u32[]{:S(2)}) %collective-permute-start.20) | collective-permute-done | bytes 524320 | tf_op jit(solution)/shard_map/ppermute | solution.py:315
  138.6 9.7 %collective-permute-done.23 = f32[4,2,128,128]{3,2,1,0:T(8,128)S(1)} collective-permute-done((f32[4,2,128,128]{3,2,1,0:T(8,128)S(1)}, f32[4,2,128,128]{3,2,1,0:T(8,128)S(1)}, u32[]{:S(2)}, u32[]{:S(2)}) %collective-permute-start.23) | collective-permute-done | bytes 524320 | tf_op jit(solution)/shard_map/ppermute | solution.py:315
  149.2 10.3 %collective-permute-done.26 = f32[4,2,128,128]{3,2,1,0:T(8,128)S(1)} collective-permute-done((f32[4,2,128,128]{3,2,1,0:T(8,128)S(1)}, f32[4,2,128,128]{3,2,1,0:T(8,128)S(1)}, u32[]{:S(2)}, u32[]{:S(2)}) %collective-permute-start.26) | collective-permute-done | bytes 524320 | tf_op jit(solution)/shard_map/ppermute | solution.py:315
  160.2 4.2 %partial_1_2.1 = (f32[4,2,128,128]{3,2,1,0:T(8,128)S(1)}, f32[4,2,128,128]{3,2,1,0:T(8,128)}) custom-call(s32[6]{0:T(128)S(1)} %pad_add_fusion.place, s32[8,160]{1,0:T(8,128)S(1)} %bitcast.19, f32[2,12]{1,0:T(2,128)S(1)} %copy-done.21, f32[8,2,128,128]{3,2,1,0:T(8,128)S(1)} %tilt_seven.1.upper_own, f32[8,2,128,128]{3,2,1,0:T(8,128)S(1)} %collective-permute-done.16.upper_sib, ...), custom_call_target="tpu_custom_call" | custom-call | flops 402653184 | bytes 5308416 | tf_op jit(solution)/shard_map/partial_1_2/pallas_call | solution.py:232
  164.4 5.7 %collective-permute-done.28 = f32[4,2,128,128]{3,2,1,0:T(8,128)S(1)} collective-permute-done((f32[4,2,128,128]{3,2,1,0:T(8,128)S(1)}, f32[4,2,128,128]{3,2,1,0:T(8,128)S(1)}, u32[]{:S(2)}, u32[]{:S(2)}) %collective-permute-start.28) | collective-permute-done | bytes 524320 | tf_op jit(solution)/shard_map/ppermute | solution.py:315
  170.1 4.4 %collective-permute-start.30 = (f32[4,2,128,128]{3,2,1,0:T(8,128)S(1)}, f32[4,2,128,128]{3,2,1,0:T(8,128)S(1)}, u32[]{:S(2)}, u32[]{:S(2)}) collective-permute-start(f32[4,2,128,128]{3,2,1,0:T(8,128)S(1)} %get-tuple-element.20), channel_id=1, source_target_pairs={{0,2},{6,4},{1,3},{7,5},{8,10},{14,12},{9,11},{15,13},{16,18},{22,... | collective-permute-start | bytes 1572872 | tf_op jit(solution)/shard_map/ppermute | solution.py:315
  189.7 3.1 %back_five.1 = f32[8,2,128,128]{3,2,1,0:T(8,128)} custom-call(f32[128,128]{1,0:T(8,128)S(1)} %copy-done.6, f32[128,128]{1,0:T(8,128)S(1)} %bitcast.11, f32[8,2,128,128]{3,2,1,0:T(8,128)S(1)} %solve_five.1.x.lower_own), custom_call_target="tpu_custom_call" | custom-call | flops 402653184 | bytes 2228224 | tf_op jit(solution)/shard_map/back_five/pallas_call | solution.py:232
  194.0 5.5 %own_1.1.own = f32[8,2,128,128]{3,2,1,0:T(8,128)S(1)} custom-call(s32[6]{0:T(128)S(1)} %pad_add_fusion.place, s32[8,160]{1,0:T(8,128)S(1)} %bitcast.20, f32[2,12]{1,0:T(2,128)S(1)} %copy-done.21, s32[8,18]{1,0:T(8,128)S(1)} %reshape.41.nearby, s32[8,12]{1,0:T(8,128)S(1)} %copy-done.23, f32[8,2,128,128]{3,2,1,0:T(8,128)S(1)} %tilt_seven.1.upper_own, ...), custom_call_target="tpu_custom_call" | custom-call | flops 402653184 | bytes 7405568 | tf_op jit(solution)/shard_map/own_1/pallas_call | solution.py:232
  199.5 3.7 %collective-permute-done.22.rest_0_ = f32[4,2,128,128]{3,2,1,0:T(8,128)} collective-permute-done((f32[4,2,128,128]{3,2,1,0:T(8,128)}, f32[4,2,128,128]{3,2,1,0:T(8,128)}, u32[]{:S(2)}, u32[]{:S(2)}) %collective-permute-start.22) | collective-permute-done | bytes 524320 | tf_op jit(solution)/shard_map/ppermute | solution.py:315
  203.2 9.4 %collective-permute-done.25.rest_1_ = f32[4,2,128,128]{3,2,1,0:T(8,128)} collective-permute-done((f32[4,2,128,128]{3,2,1,0:T(8,128)}, f32[4,2,128,128]{3,2,1,0:T(8,128)}, u32[]{:S(2)}, u32[]{:S(2)}) %collective-permute-start.25) | collective-permute-done | bytes 524320 | tf_op jit(solution)/shard_map/ppermute | solution.py:315
  212.6 4.9 %solve_six.1 = f32[8,2,128,128]{3,2,1,0:T(8,128)} custom-call(s32[8,12]{1,0:T(8,128)S(1)} %copy-done.23, f32[12]{0:T(128)S(1)} %copy-done.25, f32[1,128]{1,0:T(1,128)S(1)} %bitcast.23, f32[128,1]{1,0:T(8,128)S(1)} %copy.37.e_column, f32[128,128]{1,0:T(8,128)S(1)} %copy-done.6, f32[128,128]{1,0:T(8,128)S(1)} %bitcast.12, f32[8,2,128,128]{3,2,1,0:T(8,128)S(1)} %own_1.1.own, ...), custom_call_target="tpu_custom_call" | custom-call | flops 402653184 | bytes 5374976 | tf_op jit(solution)/shard_map/solve_six/pallas_call | solution.py:232
  (142 shorter events, 58.9 us)
Async XLA Ops:
  0.6 17.1 %collective-permute-start = (f32[8,2,128,128]{3,2,1,0:T(8,128)}, f32[8,2,128,128]{3,2,1,0:T(8,128)S(1)}, u32[]{:S(2)}, u32[]{:S(2)}) collective-permute-start(f32[8,2,128,128]{3,2,1,0:T(8,128)} %upper_own.7), channel_id=1, source_target_pairs={{0,1},{1,0},{2,3},{3,2},{4,5},{5,4},{6,7},{7,6},{8,9},{9,8},{10,11... | collective-permute-start | bytes 3145736 | tf_op jit(solution)/shard_map/ppermute | solution.py:303
  1.1 16.6 %collective-permute-start.1 = (f32[8,2,128,128]{3,2,1,0:T(8,128)}, f32[8,2,128,128]{3,2,1,0:T(8,128)S(1)}, u32[]{:S(2)}, u32[]{:S(2)}) collective-permute-start(f32[8,2,128,128]{3,2,1,0:T(8,128)} %lower_own.7), channel_id=1, source_target_pairs={{0,1},{1,0},{2,3},{3,2},{4,5},{5,4},{6,7},{7,6},{8,9},{9,8},{10,11... | collective-permute-start | bytes 3145736 | tf_op jit(solution)/shard_map/ppermute | solution.py:303
  5.8 11.9 %all-to-all-start = ((s32[8,1,160]{2,1,0:T(1,128)}), s32[8,1,160]{2,1,0:T(1,128)S(1)}, u32[]{:S(2)}, u32[]{:S(2)}) async-start(s32[8,1,160]{2,1,0:T(1,128)} %broadcast_in_dim.27), calls=%async_computation | async-start | bytes 16384 | tf_op jit(solution)/shard_map/all_to_all | solution.py:281
  24.1 14.9 %collective-permute-start.4 = (f32[4,2,128,128]{3,2,1,0:T(8,128)S(1)}, f32[4,2,128,128]{3,2,1,0:T(8,128)S(1)}, u32[]{:S(2)}, u32[]{:S(2)}) collective-permute-start(f32[4,2,128,128]{3,2,1,0:T(8,128)S(1)} %get-tuple-element.15), channel_id=1, source_target_pairs={{0,2},{6,4},{1,3},{7,5},{8,10},{14,12},{9,11},{15,13},{16,18},{22,... | collective-permute-start | bytes 1572872 | tf_op jit(solution)/shard_map/ppermute | solution.py:315
  26.8 23.5 %collective-permute-start.7 = (f32[4,2,128,128]{3,2,1,0:T(8,128)S(1)}, f32[4,2,128,128]{3,2,1,0:T(8,128)S(1)}, u32[]{:S(2)}, u32[]{:S(2)}) collective-permute-start(f32[4,2,128,128]{3,2,1,0:T(8,128)S(1)} %get-tuple-element.17), channel_id=1, source_target_pairs={{0,2},{6,4},{1,3},{7,5},{8,10},{14,12},{9,11},{15,13},{16,18},{22,... | collective-permute-start | bytes 1572872 | tf_op jit(solution)/shard_map/ppermute | solution.py:315
  31.4 30.1 %collective-permute-start.10 = (f32[4,2,128,128]{3,2,1,0:T(8,128)S(1)}, f32[4,2,128,128]{3,2,1,0:T(8,128)S(1)}, u32[]{:S(2)}, u32[]{:S(2)}) collective-permute-start(f32[4,2,128,128]{3,2,1,0:T(8,128)S(1)} %get-tuple-element.18), channel_id=1, source_target_pairs={{0,2},{6,4},{1,3},{7,5},{8,10},{14,12},{9,11},{15,13},{16,18},{22,... | collective-permute-start | bytes 1572872 | tf_op jit(solution)/shard_map/ppermute | solution.py:315
  32.7 51.4 %collective-permute-start.2 = (f32[8,2,128,128]{3,2,1,0:T(8,128)S(1)}, f32[8,2,128,128]{3,2,1,0:T(8,128)S(1)}, u32[]{:S(2)}, u32[]{:S(2)}) collective-permute-start(f32[8,2,128,128]{3,2,1,0:T(8,128)S(1)} %copy-done), channel_id=1, source_target_pairs={{0,24},{8,0},{16,8},{24,16},{1,25},{9,1},{17,9},{25,17},{2,26},{10... | collective-permute-start | bytes 3145736 | tf_op jit(solution)/shard_map/ppermute | solution.py:306
  35.3 51.3 %collective-permute-start.3 = (f32[8,2,128,128]{3,2,1,0:T(8,128)S(1)}, f32[8,2,128,128]{3,2,1,0:T(8,128)S(1)}, u32[]{:S(2)}, u32[]{:S(2)}) collective-permute-start(f32[8,2,128,128]{3,2,1,0:T(8,128)S(1)} %copy-done.2), channel_id=1, source_target_pairs={{0,8},{8,16},{16,24},{24,0},{1,9},{9,17},{17,25},{25,1},{2,10},{10... | collective-permute-start | bytes 3145736 | tf_op jit(solution)/shard_map/ppermute | solution.py:306
  39.1 32.5 %collective-permute-start.12 = (f32[4,2,128,128]{3,2,1,0:T(8,128)S(1)}, f32[4,2,128,128]{3,2,1,0:T(8,128)S(1)}, u32[]{:S(2)}, u32[]{:S(2)}) collective-permute-start(f32[4,2,128,128]{3,2,1,0:T(8,128)S(1)} %get-tuple-element.19), channel_id=1, source_target_pairs={{0,2},{6,4},{1,3},{7,5},{8,10},{14,12},{9,11},{15,13},{16,18},{22,... | collective-permute-start | bytes 1572872 | tf_op jit(solution)/shard_map/ppermute | solution.py:315
  50.3 27.4 %collective-permute-start.5 = (f32[4,2,128,128]{3,2,1,0:T(8,128)S(1)}, f32[4,2,128,128]{3,2,1,0:T(8,128)S(1)}, u32[]{:S(2)}, u32[]{:S(2)}) collective-permute-start(f32[4,2,128,128]{3,2,1,0:T(8,128)S(1)} %add.50), channel_id=1, source_target_pairs={{2,4},{4,2},{3,5},{5,3},{10,12},{12,10},{11,13},{13,11},{18,20},{2... | collective-permute-start | bytes 1572872 | tf_op jit(solution)/shard_map/ppermute | solution.py:315
  61.5 19.1 %collective-permute-start.8 = (f32[4,2,128,128]{3,2,1,0:T(8,128)S(1)}, f32[4,2,128,128]{3,2,1,0:T(8,128)S(1)}, u32[]{:S(2)}, u32[]{:S(2)}) collective-permute-start(f32[4,2,128,128]{3,2,1,0:T(8,128)S(1)} %add.52), channel_id=1, source_target_pairs={{2,4},{4,2},{3,5},{5,3},{10,12},{12,10},{11,13},{13,11},{18,20},{2... | collective-permute-start | bytes 1572872 | tf_op jit(solution)/shard_map/ppermute | solution.py:315
  71.6 17.3 %collective-permute-start.14 = (f32[4,2,128,128]{3,2,1,0:T(8,128)S(1)}, f32[4,2,128,128]{3,2,1,0:T(8,128)S(1)}, u32[]{:S(2)}, u32[]{:S(2)}) collective-permute-start(f32[4,2,128,128]{3,2,1,0:T(8,128)S(1)} %get-tuple-element.14), channel_id=1, source_target_pairs={{0,2},{6,4},{1,3},{7,5},{8,10},{14,12},{9,11},{15,13},{16,18},{22,... | collective-permute-start | bytes 1572872 | tf_op jit(solution)/shard_map/ppermute | solution.py:315
  77.7 25.9 %collective-permute-start.15 = (f32[4,2,128,128]{3,2,1,0:T(8,128)}, f32[4,2,128,128]{3,2,1,0:T(8,128)}, u32[]{:S(2)}, u32[]{:S(2)}) collective-permute-start(f32[4,2,128,128]{3,2,1,0:T(8,128)} %get-tuple-element.16), channel_id=1, source_target_pairs={{0,2},{6,4},{1,3},{7,5},{8,10},{14,12},{9,11},{15,13},{16,18},{22,... | collective-permute-start | bytes 1572872 | tf_op jit(solution)/shard_map/ppermute | solution.py:315
  80.7 23.0 %collective-permute-start.11 = (f32[4,2,128,128]{3,2,1,0:T(8,128)}, f32[4,2,128,128]{3,2,1,0:T(8,128)}, u32[]{:S(2)}, u32[]{:S(2)}) collective-permute-start(f32[4,2,128,128]{3,2,1,0:T(8,128)} %add.54), channel_id=1, source_target_pairs={{2,4},{4,2},{3,5},{5,3},{10,12},{12,10},{11,13},{13,11},{18,20},{2... | collective-permute-start | bytes 1572872 | tf_op jit(solution)/shard_map/ppermute | solution.py:315
  85.1 18.6 %collective-permute-start.13 = (f32[4,2,128,128]{3,2,1,0:T(8,128)}, f32[4,2,128,128]{3,2,1,0:T(8,128)}, u32[]{:S(2)}, u32[]{:S(2)}) collective-permute-start(f32[4,2,128,128]{3,2,1,0:T(8,128)} %add.55), channel_id=1, source_target_pairs={{2,4},{4,2},{3,5},{5,3},{10,12},{12,10},{11,13},{13,11},{18,20},{2... | collective-permute-start | bytes 1572872 | tf_op jit(solution)/shard_map/ppermute | solution.py:315
  87.6 17.1 %collective-permute-start.6 = (f32[4,2,128,128]{3,2,1,0:T(8,128)}, f32[4,2,128,128]{3,2,1,0:T(8,128)}, u32[]{:S(2)}, u32[]{:S(2)}) collective-permute-start(f32[4,2,128,128]{3,2,1,0:T(8,128)} %add.51), channel_id=1, source_target_pairs={{4,6},{2,0},{5,7},{3,1},{12,14},{10,8},{13,15},{11,9},{20,22},{18,... | collective-permute-start | bytes 1572872 | tf_op jit(solution)/shard_map/ppermute | solution.py:315
  89.7 23.8 %collective-permute-start.9 = (f32[4,2,128,128]{3,2,1,0:T(8,128)}, f32[4,2,128,128]{3,2,1,0:T(8,128)}, u32[]{:S(2)}, u32[]{:S(2)}) collective-permute-start(f32[4,2,128,128]{3,2,1,0:T(8,128)} %add.53), channel_id=1, source_target_pairs={{4,6},{2,0},{5,7},{3,1},{12,14},{10,8},{13,15},{11,9},{20,22},{18,... | collective-permute-start | bytes 1572872 | tf_op jit(solution)/shard_map/ppermute | solution.py:315
  103.6 14.1 %collective-permute-start.16 = (f32[8,2,128,128]{3,2,1,0:T(8,128)S(1)}, f32[8,2,128,128]{3,2,1,0:T(8,128)S(1)}, u32[]{:S(2)}, u32[]{:S(2)}) collective-permute-start(f32[8,2,128,128]{3,2,1,0:T(8,128)S(1)} %tilt_seven.1.upper_own), channel_id=1, source_target_pairs={{0,1},{1,0},{2,3},{3,2},{4,5},{5,4},{6,7},{7,6},{8,9},{9,8},{10,11... | collective-permute-start | bytes 3145736 | tf_op jit(solution)/shard_map/ppermute | solution.py:303
  123.4 13.6 %collective-permute-start.20 = (f32[4,2,128,128]{3,2,1,0:T(8,128)S(1)}, f32[4,2,128,128]{3,2,1,0:T(8,128)S(1)}, u32[]{:S(2)}, u32[]{:S(2)}) collective-permute-start(f32[4,2,128,128]{3,2,1,0:T(8,128)S(1)} %get-tuple-element.21), channel_id=1, source_target_pairs={{0,2},{6,4},{1,3},{7,5},{8,10},{14,12},{9,11},{15,13},{16,18},{22,... | collective-permute-start | bytes 1572872 | tf_op jit(solution)/shard_map/ppermute | solution.py:315
  124.8 23.5 %collective-permute-start.23 = (f32[4,2,128,128]{3,2,1,0:T(8,128)S(1)}, f32[4,2,128,128]{3,2,1,0:T(8,128)S(1)}, u32[]{:S(2)}, u32[]{:S(2)}) collective-permute-start(f32[4,2,128,128]{3,2,1,0:T(8,128)S(1)} %get-tuple-element.23), channel_id=1, source_target_pairs={{0,2},{6,4},{1,3},{7,5},{8,10},{14,12},{9,11},{15,13},{16,18},{22,... | collective-permute-start | bytes 1572872 | tf_op jit(solution)/shard_map/ppermute | solution.py:315
  129.5 30.0 %collective-permute-start.26 = (f32[4,2,128,128]{3,2,1,0:T(8,128)S(1)}, f32[4,2,128,128]{3,2,1,0:T(8,128)S(1)}, u32[]{:S(2)}, u32[]{:S(2)}) collective-permute-start(f32[4,2,128,128]{3,2,1,0:T(8,128)S(1)} %get-tuple-element.24), channel_id=1, source_target_pairs={{0,2},{6,4},{1,3},{7,5},{8,10},{14,12},{9,11},{15,13},{16,18},{22,... | collective-permute-start | bytes 1572872 | tf_op jit(solution)/shard_map/ppermute | solution.py:315
  130.8 51.8 %collective-permute-start.18 = (f32[8,2,128,128]{3,2,1,0:T(8,128)S(1)}, f32[8,2,128,128]{3,2,1,0:T(8,128)S(1)}, u32[]{:S(2)}, u32[]{:S(2)}) collective-permute-start(f32[8,2,128,128]{3,2,1,0:T(8,128)S(1)} %tilt_seven.1.upper_own), channel_id=1, source_target_pairs={{0,24},{8,0},{16,8},{24,16},{1,25},{9,1},{17,9},{25,17},{2,26},{10... | collective-permute-start | bytes 3145736 | tf_op jit(solution)/shard_map/ppermute | solution.py:306
  133.5 36.6 %collective-permute-start.28 = (f32[4,2,128,128]{3,2,1,0:T(8,128)S(1)}, f32[4,2,128,128]{3,2,1,0:T(8,128)S(1)}, u32[]{:S(2)}, u32[]{:S(2)}) collective-permute-start(f32[4,2,128,128]{3,2,1,0:T(8,128)S(1)} %get-tuple-element.25), channel_id=1, source_target_pairs={{0,2},{6,4},{1,3},{7,5},{8,10},{14,12},{9,11},{15,13},{16,18},{22,... | collective-permute-start | bytes 1572872 | tf_op jit(solution)/shard_map/ppermute | solution.py:315
  137.0 48.1 %collective-permute-start.19 = (f32[8,2,128,128]{3,2,1,0:T(8,128)S(1)}, f32[8,2,128,128]{3,2,1,0:T(8,128)S(1)}, u32[]{:S(2)}, u32[]{:S(2)}) collective-permute-start(f32[8,2,128,128]{3,2,1,0:T(8,128)S(1)} %solve_five.1.x.lower_own), channel_id=1, source_target_pairs={{0,8},{8,16},{16,24},{24,0},{1,9},{9,17},{17,25},{25,1},{2,10},{10... | collective-permute-start | bytes 3145736 | tf_op jit(solution)/shard_map/ppermute | solution.py:306
  148.2 28.0 %collective-permute-start.21 = (f32[4,2,128,128]{3,2,1,0:T(8,128)S(1)}, f32[4,2,128,128]{3,2,1,0:T(8,128)S(1)}, u32[]{:S(2)}, u32[]{:S(2)}) collective-permute-start(f32[4,2,128,128]{3,2,1,0:T(8,128)S(1)} %add.56), channel_id=1, source_target_pairs={{2,4},{4,2},{3,5},{5,3},{10,12},{12,10},{11,13},{13,11},{18,20},{2... | collective-permute-start | bytes 1572872 | tf_op jit(solution)/shard_map/ppermute | solution.py:315
  159.5 19.7 %collective-permute-start.24 = (f32[4,2,128,128]{3,2,1,0:T(8,128)S(1)}, f32[4,2,128,128]{3,2,1,0:T(8,128)S(1)}, u32[]{:S(2)}, u32[]{:S(2)}) collective-permute-start(f32[4,2,128,128]{3,2,1,0:T(8,128)S(1)} %add.58), channel_id=1, source_target_pairs={{2,4},{4,2},{3,5},{5,3},{10,12},{12,10},{11,13},{13,11},{18,20},{2... | collective-permute-start | bytes 1572872 | tf_op jit(solution)/shard_map/ppermute | solution.py:315
  170.1 17.4 %collective-permute-start.30 = (f32[4,2,128,128]{3,2,1,0:T(8,128)S(1)}, f32[4,2,128,128]{3,2,1,0:T(8,128)S(1)}, u32[]{:S(2)}, u32[]{:S(2)}) collective-permute-start(f32[4,2,128,128]{3,2,1,0:T(8,128)S(1)} %get-tuple-element.20), channel_id=1, source_target_pairs={{0,2},{6,4},{1,3},{7,5},{8,10},{14,12},{9,11},{15,13},{16,18},{22,... | collective-permute-start | bytes 1572872 | tf_op jit(solution)/shard_map/ppermute | solution.py:315
  176.2 23.2 %collective-permute-start.31 = (f32[4,2,128,128]{3,2,1,0:T(8,128)}, f32[4,2,128,128]{3,2,1,0:T(8,128)}, u32[]{:S(2)}, u32[]{:S(2)}) collective-permute-start(f32[4,2,128,128]{3,2,1,0:T(8,128)} %get-tuple-element.22), channel_id=1, source_target_pairs={{0,2},{6,4},{1,3},{7,5},{8,10},{14,12},{9,11},{15,13},{16,18},{22,... | collective-permute-start | bytes 1572872 | tf_op jit(solution)/shard_map/ppermute | solution.py:315
  179.2 20.3 %collective-permute-start.27 = (f32[4,2,128,128]{3,2,1,0:T(8,128)}, f32[4,2,128,128]{3,2,1,0:T(8,128)}, u32[]{:S(2)}, u32[]{:S(2)}) collective-permute-start(f32[4,2,128,128]{3,2,1,0:T(8,128)} %add.60), channel_id=1, source_target_pairs={{2,4},{4,2},{3,5},{5,3},{10,12},{12,10},{11,13},{13,11},{18,20},{2... | collective-permute-start | bytes 1572872 | tf_op jit(solution)/shard_map/ppermute | solution.py:315
  183.7 15.8 %collective-permute-start.29 = (f32[4,2,128,128]{3,2,1,0:T(8,128)}, f32[4,2,128,128]{3,2,1,0:T(8,128)}, u32[]{:S(2)}, u32[]{:S(2)}) collective-permute-start(f32[4,2,128,128]{3,2,1,0:T(8,128)} %add.61), channel_id=1, source_target_pairs={{2,4},{4,2},{3,5},{5,3},{10,12},{12,10},{11,13},{13,11},{18,20},{2... | collective-permute-start | bytes 1572872 | tf_op jit(solution)/shard_map/ppermute | solution.py:315
  186.2 17.1 %collective-permute-start.22 = (f32[4,2,128,128]{3,2,1,0:T(8,128)}, f32[4,2,128,128]{3,2,1,0:T(8,128)}, u32[]{:S(2)}, u32[]{:S(2)}) collective-permute-start(f32[4,2,128,128]{3,2,1,0:T(8,128)} %add.57), channel_id=1, source_target_pairs={{4,6},{2,0},{5,7},{3,1},{12,14},{10,8},{13,15},{11,9},{20,22},{18,... | collective-permute-start | bytes 1572872 | tf_op jit(solution)/shard_map/ppermute | solution.py:315
  188.3 24.3 %collective-permute-start.25 = (f32[4,2,128,128]{3,2,1,0:T(8,128)}, f32[4,2,128,128]{3,2,1,0:T(8,128)}, u32[]{:S(2)}, u32[]{:S(2)}) collective-permute-start(f32[4,2,128,128]{3,2,1,0:T(8,128)} %add.59), channel_id=1, source_target_pairs={{4,6},{2,0},{5,7},{3,1},{12,14},{10,8},{13,15},{11,9},{20,22},{18,... | collective-permute-start | bytes 1572872 | tf_op jit(solution)/shard_map/ppermute | solution.py:315
  (32 other events, 149.1 us)

commit v2 on v1

v2 whole, which is shorter than its diff:
```python
import functools

import jax
import jax.numpy as jnp
from jax import lax
from jax.experimental import pallas as pl
from jax.experimental.pallas import tpu as pltpu
from jax.sharding import PartitionSpec as P

SMEM = pltpu.SMEM
VMEM = pltpu.VMEM
HALVES = 2
TOGETHER = 2


def split(x):
    high = x.astype(jnp.bfloat16)
    return high, (x - high.astype(jnp.float32)).astype(jnp.bfloat16)


def as_left(w):
    high, low = split(w)
    return jnp.concatenate([high, high, low], axis=1)


def as_right(w):
    high, low = split(w)
    return jnp.concatenate([high, high, low], axis=0)


def left_dot(w_left, x):
    high, low = split(x)
    return jnp.dot(
        w_left, jnp.concatenate([high, low, high], axis=0), preferred_element_type=jnp.float32
    )


def right_dot(x, w_right):
    high, low = split(x)
    return jnp.dot(
        jnp.concatenate([high, low, high], axis=1), w_right, preferred_element_type=jnp.float32
    )


def sandwich(w_left, real, imag, w_right):
    n = real.shape[0]
    right = right_dot(jnp.concatenate([real, imag], axis=0), w_right)
    both = left_dot(w_left, jnp.concatenate([right[:n], right[n:]], axis=1))
    return both[:, :n], both[:, n:]


def drive_of(mixed, turned, c_left, c_right):
    n = mixed.shape[-1]
    ahead = left_dot(
        c_left, jnp.concatenate([mixed[1] + turned[0], mixed[0] - turned[1]], axis=1)
    )
    behind = right_dot(
        jnp.concatenate([mixed[1] - turned[0], mixed[0] + turned[1]], axis=0), c_right
    )
    return behind[:n] - ahead[:, :n], ahead[:, n:] - behind[n:]


def add_requests(row, column, place, table, bath, upper, lower, mixed, turned):
    chip = place[0]
    core = place[1]
    for j in range(4):
        peer = table[row, column + j]
        spot = table[row, column + 4 + j]
        here = peer >> 1 == chip
        for sibling in range(2):
            own = (peer & 1 == core) if sibling == 0 else (peer & 1 != core)

            @pl.when(jnp.logical_and(here, own))
            def _(j=j, sibling=sibling, spot=spot):
                if j < 2:
                    mixed[...] += upper[sibling][spot]
                else:
                    mode = j - 1
                    count = table[row, column + 6 + j].astype(jnp.float32)
                    source = lower[sibling][spot]
                    mixed[...] += (count * bath[0, mode]) * source
                    turned[...] += (count * bath[1, mode]) * source


def joined(pieces, scratch):
    if len(pieces) == 1:
        return pieces[0]
    row = 0
    for piece in pieces:
        scratch[row : row + piece.shape[0]] = piece[...]
        row += piece.shape[0]
    return scratch


def partial_kernel(slot, first, column, role, place, table, bath, *refs):
    upper, pieces, (c_ref, out, mixed, turned, sibling) = refs[:2], refs[3:-5], refs[-5:]
    rows = upper[0].shape[0]
    together = mixed.shape[0]

    def work():
        c_left = as_left(c_ref[...])
        c_right = as_right(c_ref[...])
        lower = (refs[2], joined(pieces, sibling))

        @pl.loop(0, out.shape[0], step=together)
        def _(m):
            mixed[...] = jnp.zeros_like(mixed)
            turned[...] = jnp.zeros_like(turned)
            for u in range(together):
                add_requests(
                    place[3 + slot] * rows + first + m + u,
                    column,
                    place,
                    table,
                    bath,
                    upper,
                    lower,
                    mixed.at[u],
                    turned.at[u],
                )
            for u in range(together):
                real, imag = drive_of(mixed[u], turned[u], c_left, c_right)
                out[m + u, 0] = real
                out[m + u, 1] = imag

    by_role(role, place, work)


def by_role(role, place, work):
    if role == "all":
        work()
    elif role == "ends":
        pl.when(place[2] == 0)(work)
    else:
        pl.when(place[2] != 0)(work)


def sums_kernel(slot, column, place, table, bath, nearby, occupation, *refs):
    upper, pieces, (mixed_out, turned_out, sibling) = refs[:2], refs[3:-3], refs[-3:]
    lower = (refs[2], joined(pieces, sibling))
    rows = upper[0].shape[0]
    modes = bath.shape[1]

    @pl.loop(0, rows)
    def _(m):
        mixed = mixed_out.at[m]
        turned = turned_out.at[m]
        mixed[...] = upper[0][nearby[m, 0]]
        turned[...] = jnp.zeros_like(turned)
        add_requests(
            place[3 + slot] * rows + m, column, place, table, bath, upper, lower, mixed, turned
        )
        for k in range(3, modes):
            if k > 3:
                mixed[...] += upper[0][nearby[m, k - 3]]
            held = occupation[m, k]

            @pl.when(held > 0)
            def _(k=k, held=held):
                source = lower[0][nearby[m, modes - 3 + k - 3]]
                mixed[...] += (held.astype(jnp.float32) * bath[0, k]) * source
                turned[...] += (held.astype(jnp.float32) * bath[1, k]) * source


def own_drive(m, occupation, bath, mixed, turned, raised, lowered, c_left, c_right):
    count = occupation[m, 0].astype(jnp.float32)
    below = lowered[m]
    return drive_of(
        mixed[m] + raised[m] + (count * bath[0, 0]) * below,
        turned[m] + (count * bath[1, 0]) * below,
        c_left,
        c_right,
    )


def finish_kernel(occupation, bath, c_ref, mixed, turned, raised, lowered, out):
    c_left = as_left(c_ref[...])
    c_right = as_right(c_ref[...])
    for m in range(out.shape[0]):
        real, imag = own_drive(
            m, occupation, bath, mixed, turned, raised, lowered, c_left, c_right
        )
        out[m, 0] = real
        out[m, 1] = imag


def solved(real, imag, damping, splitting):
    inverse = 1.0 / (damping * damping + splitting * splitting)
    factor_real = -damping * inverse
    factor_imag = splitting * inverse
    return real * factor_real - imag * factor_imag, real * factor_imag + imag * factor_real


def damping_of(occupation, decay, m):
    damping = occupation[m, 0].astype(jnp.float32) * decay[0]
    for k in range(1, decay.shape[0]):
        damping = damping + occupation[m, k].astype(jnp.float32) * decay[k]
    return damping


def solve_five_kernel(
    counts, role, place, occupation, decay, bath, e_row, e_column, e_ref, et_ref, c_ref, *rest
):
    mixed, turned, raised, lowered = rest[:4]
    rest = rest[4:]
    arrivals = []
    for count in counts[1:]:
        arrivals.append(rows_of(rest[:count]))
        rest = rest[count:]
    previous, (out, *pieces) = rest[: counts[0]], rest[counts[0] :]
    spots = rows_of(pieces)

    def work():
        splitting = e_column[...] - e_row[...]
        in_left = as_left(et_ref[...])
        in_right = as_right(e_ref[...])
        c_left = as_left(c_ref[...])
        c_right = as_right(c_ref[...])
        for m in range(out.shape[0]):
            real, imag = own_drive(
                m, occupation, bath, mixed, turned, raised, lowered, c_left, c_right
            )
            for arrival in arrivals:
                piece, row = arrival[m]
                real = real + piece[row, 0]
                imag = imag + piece[row, 1]
            real, imag = sandwich(in_left, real, imag, in_right)
            damping = damping_of(occupation, decay, m)
            real, imag = solved(real, imag, damping, splitting)
            out[m, 0] = real
            out[m, 1] = imag
            piece, row = spots[m]
            piece[row, 0] = real
            piece[row, 1] = imag

    by_role(role, place, work)
    if role == "rest":

        @pl.when(place[2] == 0)
        def _():
            out[...] = previous[0][...]
            first = 0
            for piece in pieces:
                piece[...] = previous[0][first : first + piece.shape[0]]
                first += piece.shape[0]


def solve_six_kernel(
    first, part_count, occupation, decay, e_row, e_column, e_ref, et_ref, own, *rest
):
    parts, out = rest[:part_count], rest[-1]
    splitting = e_column[...] - e_row[...]
    out_left = as_left(e_ref[...])
    out_right = as_right(et_ref[...])
    for m in range(out.shape[0]):
        real = own[m, 0]
        imag = own[m, 1]
        for part in parts:
            real = real + part[m, 0]
            imag = imag + part[m, 1]
        damping = damping_of(occupation, decay, first + m)
        real, imag = solved(real, imag, damping, splitting)
        real, imag = sandwich(out_left, real, imag, out_right)
        out[m, 0] = real
        out[m, 1] = imag


def turn_kernel(left_ref, right_ref, x, *outs):
    w_left = as_left(left_ref[...])
    w_right = as_right(right_ref[...])
    spots = [rows_of(outs[:1]), rows_of(outs[1:])] if len(outs) > 1 else [rows_of(outs)]
    for m in range(x.shape[0]):
        real, imag = sandwich(w_left, x[m, 0], x[m, 1], w_right)
        for spot in spots:
            out, row = spot[m]
            out[row, 0] = real
            out[row, 1] = imag


def turn_one_kernel(left_ref, right_ref, x, out):
    out[...] = left_dot(as_left(left_ref[...]), right_dot(x[...], as_right(right_ref[...])))


def rows_of(pieces):
    return [(piece, row) for piece in pieces for row in range(piece.shape[0])]


def add_kernel(counts, *refs):
    ours, theirs, outs = refs[: counts[0]], refs[counts[0] : sum(counts)], refs[sum(counts) :]
    for (a, i), (b, j), (out, k) in zip(rows_of(ours), rows_of(theirs), rows_of(outs)):
        out[k] = a[i] + b[j]


class Queue:
    def __init__(self):
        self.latest = []

    def call(
        self, kernel, outs, scalars, arrays, scratch=(), name=None, in_specs=None, after=(), **options
    ):
        waits = [w for w in [*self.latest, *after] if not any(w is a for a in arrays)]
        plain = pl.BlockSpec(memory_space=VMEM)
        count = len(scalars) + len(arrays)

        def without_waits(*refs):
            kernel(*refs[:count], *refs[count + len(waits) :])

        got = pl.pallas_call(
            without_waits,
            out_shape=outs,
            in_specs=[pl.BlockSpec(memory_space=SMEM)] * len(scalars)
            + (in_specs or [plain] * len(arrays))
            + [pl.BlockSpec(memory_space=pl.ANY)] * len(waits),
            out_specs=options.pop("out_specs", [plain] * len(outs)),
            scratch_shapes=scratch,
            compiler_params=pltpu.CompilerParams(vmem_limit_bytes=24 * 1024 * 1024),
            cost_estimate=pl.CostEstimate(flops=1, bytes_accessed=1, transcendentals=0),
            name=name,
            **options,
        )(*scalars, *arrays, *waits)
        self.latest = [got[0]]
        return got


def body(
    tier_four,
    tier_six,
    tier_seven,
    coupling,
    eigenbasis,
    energies,
    decay_rates,
    bath_coefficients,
    occupation_five,
    local_five,
    peers_five,
    places_five,
    occupation_six,
    local_six,
    peers_six,
    places_six,
):
    queue = Queue()
    call = queue.call
    rows = tier_four.shape[0]
    n = tier_four.shape[-1]
    peer_count = lax.axis_size("mb")
    row_count = lax.axis_size("ma")
    chips = peer_count // 2
    per = rows // HALVES
    whole = jax.ShapeDtypeStruct(tier_four.shape, jnp.float32)
    a_tier = pltpu.VMEM(tier_four.shape, jnp.float32)
    work_space = [pltpu.VMEM((TOGETHER,) + tier_four.shape[1:], jnp.float32)] * 2 + [a_tier]

    def sibling_of(array, of_chips):
        return lax.ppermute(
            array, "mb", [(2 * i + c, 2 * i + 1 - c) for i in of_chips for c in range(2)]
        )

    def along(array, by):
        return lax.ppermute(array, "ma", [(i, (i + by) % row_count) for i in range(row_count)])

    def turn_line(array, by):
        return lax.ppermute(
            array, "mb", [(i, (i + 2 * by) % peer_count) for i in range(peer_count)]
        )

    def hop(array, *moves):
        pairs = []
        for start, stop in moves:
            for c in range(2):
                pairs.append((start * 2 + c, stop * 2 + c))
                pairs.append(((chips - 1 - start) * 2 + c, (chips - 1 - stop) * 2 + c))
        return lax.ppermute(array, "mb", pairs)

    mine = jnp.concatenate(
        [
            peers_five,
            places_five,
            occupation_five[:, 1:3],
            peers_six,
            places_six,
            occupation_six[:, 1:3],
        ],
        axis=1,
    )
    table = jnp.concatenate([mine] + [turn_line(mine, by) for by in range(1, chips)], axis=0)
    columns = (0, mine.shape[1] // 2)

    goals = list(range(chips - 1, 0, -1))
    skips = chips > 3

    def slot_of(step, g):
        depth = min(step, chips - 1 - step)
        behind = step >= chips // 2
        return chips - 1 - g if behind else depth + chips - 1 - g

    index = lax.axis_index("mb")
    chip = index // 2
    mirrored = chip >= chips // 2
    depth = jnp.where(mirrored, chips - 1 - chip, chip)
    order = jnp.arange(chips, dtype=jnp.int32)
    seen = jnp.where(order < depth, order, chips - 1 - order + depth)
    goal = jnp.where(mirrored, chips - 1 - seen, seen)
    place = jnp.concatenate(
        [jnp.stack([chip, index % 2, depth]), (chip - goal + chips) % chips]
    ).astype(jnp.int32)

    def partial(tier, slot, upper, lower, c, role, after=(), half=None):
        first, count = (0, rows) if half is None else (half * per, per)
        return call(
            functools.partial(partial_kernel, slot, first, columns[tier], role),
            [jax.ShapeDtypeStruct((count,) + whole.shape[1:], jnp.float32)],
            [place, table, bath_coefficients],
            [*upper, *lower, c],
            work_space,
            f"partial_{tier}_{slot}_{first}_{role}",
            after=after,
        )[0]

    def steps_to(g):
        last = g - 1 if skips and g == chips - 1 else g
        return list(range(last))

    def next_stop(step, g):
        return g if step == steps_to(g)[-1] else step + 1

    def start(sent, g):
        return [hop(array, (0, next_stop(0, g))) for array in sent[slot_of(0, g)]]

    def go_on(tier, sent, arrived, g, after=(), count=1):
        for step in steps_to(g)[1:]:
            parts = count if step == steps_to(g)[-1] else 1
            ours = sent[slot_of(step, g)]
            piece = jax.ShapeDtypeStruct((rows // parts,) + whole.shape[1:], jnp.float32)
            messages = call(
                functools.partial(add_kernel, (len(ours), len(arrived))),
                [piece] * parts,
                [],
                [*ours, *arrived],
                (),
                f"add_{tier}_{step}_{g}",
                after=after,
            )
            arrived = [hop(message, (step, next_stop(step, g))) for message in messages]
        return arrived

    def sums(tier, upper, lower, nearby, occupation):
        return call(
            functools.partial(sums_kernel, chips - 1, columns[tier]),
            [whole, whole],
            [place, table, bath_coefficients, nearby.reshape(rows, -1), occupation],
            [*upper, *lower],
            [a_tier],
            f"sums_{tier}",
        )

    turned = jnp.transpose(eigenbasis)
    bases = [energies[None, :], energies[:, None], eigenbasis, turned]
    every = range(chips)
    ends = [0, chips - 1]

    def solve_five(arrays, last, role, previous, cuts, after=()):
        got = call(
            functools.partial(
                solve_five_kernel, [len(previous), *[len(pieces) for pieces in last]], role
            ),
            [whole]
            + [jax.ShapeDtypeStruct((cut,) + whole.shape[1:], jnp.float32) for cut in cuts],
            [place, occupation_five, decay_rates, bath_coefficients],
            [*bases, coupling, *arrays, *[piece for pieces in last for piece in pieces], *previous],
            (),
            f"solve_five_{role}",
            after=after,
        )
        return got[0], got[1:]

    def solve_six(own, last, half, previous):
        plain = pl.BlockSpec(memory_space=VMEM)
        block = pl.BlockSpec((per,) + whole.shape[1:], lambda i: (half, 0, 0, 0))
        parts = [pieces[half * len(pieces) // HALVES] for pieces in last]
        arrays = [*bases, own, *parts, *previous]
        return call(
            functools.partial(solve_six_kernel, half * per, len(parts)),
            [whole],
            [occupation_six, decay_rates],
            arrays,
            (),
            f"solve_six_{half}",
            [plain] * len(bases)
            + [block]
            + [block if len(pieces) == 1 else plain for pieces in last]
            + [pl.BlockSpec(memory_space=pl.ANY)] * len(previous),
            out_specs=[block],
            grid=(1,),
            input_output_aliases={2 + len(arrays) - 1: 0} if previous else {},
        )

    raised_five = along(tier_six, -1)
    lowered_five = along(tier_four, 1)
    upper_five = (tier_six, sibling_of(tier_six, every))
    lower_five = (tier_four, sibling_of(tier_four, every))
    slots = range(chips - 1)
    far = goals[0]
    aside = [(far - 1, far)] if skips else []
    sent_five = {}
    moving_five = {}
    sent_five[0] = [
        partial(0, 0, upper_five, lower_five, coupling, "all", (), half) for half in range(HALVES)
    ]
    moving_five[far] = [hop(array, (0, next_stop(0, far)), *aside) for array in sent_five[0]]
    beside_five = [moving_five[far]] if skips else []
    for slot in slots[1:]:
        sent_five[slot] = [partial(0, slot, upper_five, lower_five, coupling, "all")]
        moving_five[goals[slot]] = start(sent_five, goals[slot])
    sums_five = sums(0, upper_five, lower_five, local_five, occupation_five)
    tilted = call(
        turn_one_kernel,
        [jax.ShapeDtypeStruct((n, n), jnp.float32)],
        [],
        [turned, eigenbasis, coupling],
        (),
        "tilt_coupling",
    )[0]
    moving_five[far] = go_on(0, sent_five, moving_five[far], far)
    eigen_seven, *pieces = call(
        turn_kernel,
        [whole] + [jax.ShapeDtypeStruct((per,) + whole.shape[1:], jnp.float32)] * HALVES,
        [],
        [turned, eigenbasis, tier_seven],
        (),
        "tilt_seven",
        after=[raised_five],
    )
    pieces = [sibling_of(piece, every) for piece in pieces]
    upper_six = (eigen_seven, jnp.concatenate(pieces))
    raised_six = along(eigen_seven, -1)
    for g in goals[1:]:
        after = [lowered_five, *pieces] if g == goals[-2] else []
        moving_five[g] = go_on(0, sent_five, moving_five[g], g, after)
    own_five = [*sums_five, raised_five, lowered_five]
    last = [moving_five[far], *beside_five]
    ends_five, pieces = solve_five(own_five, last, "ends", [], [per] * HALVES)
    lower_ends = (ends_five, *[sibling_of(piece, ends) for piece in pieces])
    sent_ends = {}
    moving_six = {}

    def from_ends(slot, after=()):
        sent_ends[slot] = [partial(1, slot, upper_six, lower_ends, tilted, "ends", after)]
        moving_six[goals[slot]] = start(sent_ends, goals[slot])

    from_ends(0, moving_five[goals[-1]])
    for slot in slots[1:]:
        from_ends(slot)
    last = [moving_five[g] for g in goals[1:]]
    cuts = [rows - rows // 4, rows // 4]
    eigen_five, pieces = solve_five(own_five, last, "rest", [ends_five], cuts, [raised_six])
    lower_six = (eigen_five, *[sibling_of(piece, every) for piece in pieces])
    lowered_six = along(eigen_five, 1)
    sent_six = {}

    def from_rest(slot):
        if slot not in sent_six:
            sent_six[slot] = [partial(1, slot, upper_six, lower_six, tilted, "rest")]

    from_rest(0)
    beside_six = [hop(sent_six[0][0], *aside)] if skips else []
    for step in steps_to(far)[1:]:
        from_rest(slot_of(step, far))
    moving_six[far] = go_on(1, sent_six, moving_six[far], far)
    for slot in slots:
        from_rest(slot)
    sums_six = sums(1, upper_six, lower_six, local_six, occupation_six)
    for g in goals[1:]:
        moving_six[g] = go_on(1, sent_six, moving_six[g], g, [], HALVES)
    updated_five = call(
        turn_kernel, [whole], [], [eigenbasis, turned, eigen_five], (), "back_five"
    )[0]
    own_six = call(
        finish_kernel,
        [whole],
        [occupation_six, bath_coefficients],
        [tilted, *sums_six, raised_six, lowered_six],
        (),
        "finish_six",
    )[0]
    previous = []
    for half in range(HALVES):
        last = [moving_six[g] for g in goals[1:]]
        last += [moving_six[far], *[[array] for array in beside_six]]
        previous = solve_six(own_six, last, half, previous)
    return (updated_five, previous[0])


def solution(mesh):
    by_block = P(("ma", "mb"))
    in_specs = (by_block,) * 3 + (P(),) * 5 + (by_block,) * 8
    return jax.shard_map(
        body, mesh=mesh, in_specs=in_specs, out_specs=(by_block, by_block), check_vma=False
    )
```

time: 219 us -> 175 us (0.80)
  waiting for transfers between devices: 84.9 us -> 49.9 us
  Pallas kernels: 46.5 us -> 65.9 us
  starting transfers between devices: 55.9 us -> 40.2 us
  other arithmetic: 9.25 us -> 0.1 us
  local copies, waits for them, and re-layouts: 19.8 us -> 14.5 us
    ppermute x24 -> x13, waiting for transfers between devices: 77.1 us -> 42 us  [hop(): return lax.ppermute(array, 'mb', pairs)]
    pallas_call x13 -> x24, Pallas kernels: 46.5 us -> 65.9 us  [call(): pl.pallas_call(without_waits, out_shape=outs, in_specs=[pl.BlockSpec(memo...]
    ppermute x24 -> x13, starting transfers between devices: 42.2 us -> 22.8 us  [hop(): return lax.ppermute(array, 'mb', pairs)]
    ppermute x4 -> x11, starting transfers between devices: 0.74 us -> 13.2 us  [the longest x3 6.99 us: turn_line(): lax.ppermute(array, 'mb', [(i, (i + 2 * by) % peer_count) for i in range(...]
    add x13 -> x0, other arithmetic: 9.18 us -> none  [the longest x12 9.17 us: reduce_line(): message = message + arrived[step - 1, half]]
    all_to_all x1 -> x0, starting transfers between devices: 6.3 us -> none  [body(): lax.all_to_all(jnp.broadcast_to(mine[None], (peer_count,) + mine.shape),...]
    all_to_all x1 -> x0, waiting for transfers between devices: 5.52 us -> none  [body(): lax.all_to_all(jnp.broadcast_to(mine[None], (peer_count,) + mine.shape),...]
    unnamed x68 -> x74, local copies, waits for them, and re-layouts: 18.2 us -> 14 us
  transfers between devices with their start and end apart: 33 -> 28, of which waited for: 14 -> 12; matrix products, arithmetic and copies ran while one was open for 5% -> 1% of each run, Pallas kernels for 16% -> 36%
where the time goes in v2:
time: 175 us; the launch traced here: 172 us
  Pallas kernels  65.9 us (38%)
  waiting for transfers between devices  49.9 us (29%)
  starting transfers between devices  40.2 us (23%)
  local copies, waits for them, and re-layouts  14.5 us (8%)
    pallas_call x24, Pallas kernels, call(): pl.pallas_call(without_waits, out_shape=outs, in_specs=[pl.BlockSpec(memo...  65.9 us
    ppermute x13, waiting for transfers between devices, hop(): return lax.ppermute(array, 'mb', pairs)  42 us
    ppermute x13, starting transfers between devices, hop(): return lax.ppermute(array, 'mb', pairs)  22.8 us
    unnamed x74, local copies, waits for them, and re-layouts  14 us
    ppermute x3, starting transfers between devices, turn_line(): lax.ppermute(array, 'mb', [(i, (i + 2 * by) % peer_count) for i in range(...  6.99 us
    ppermute x8, starting transfers between devices, sibling_of(): lax.ppermute(array, 'mb', [(2 * i + c, 2 * i + 1 - c) for i in of_chips f...  6.18 us
    ppermute x4, starting transfers between devices, along(): lax.ppermute(array, 'ma', [(i, (i + by) % row_count) for i in range(row_c...  4.26 us
    ppermute x4, waiting for transfers between devices, along(): lax.ppermute(array, 'ma', [(i, (i + by) % row_count) for i in range(row_c...  3.84 us
  transfers between devices with their start and end apart: 28, of which 12 were waited for; matrix products, arithmetic and copies ran while one was open for 1% of the time, Pallas kernels for 36%

profile of v2, /device:TPU:0, one launch (start us, length us, event | category | flops | bytes accessed | tf_op | source)
XLA Modules:
  0.0 171.6 jit_solution(4184671122167738727)
XLA Ops:
  4.9 3.0 %collective-permute-start = (s32[8,20]{1,0:T(8,128)S(1)}, s32[8,20]{1,0:T(8,128)S(1)}, u32[]{:S(2)}, u32[]{:S(2)}) collective-permute-start(s32[8,20]{1,0:T(8,128)S(1)} %concatenate.13), channel_id=1, source_target_pairs={{0,2},{1,3},{2,4},{3,5},{4,6},{5,7},{6,0},{7,1},{8,10},{9,11},{10,... | collective-permute-start | bytes 1928 | tf_op jit(solution)/shard_map/ppermute | solution.py:364
  7.9 2.6 %collective-permute-start.1 = (s32[8,20]{1,0:T(8,128)S(1)}, s32[8,20]{1,0:T(8,128)S(1)}, u32[]{:S(2)}, u32[]{:S(2)}) collective-permute-start(s32[8,20]{1,0:T(8,128)S(1)} %concatenate.13), channel_id=1, source_target_pairs={{0,4},{1,5},{2,6},{3,7},{4,0},{5,1},{6,2},{7,3},{8,12},{9,13},{10,... | collective-permute-start | bytes 1928 | tf_op jit(solution)/shard_map/ppermute | solution.py:364
  10.5 2.4 %collective-permute-start.5 = (f32[8,2,128,128]{3,2,1,0:T(8,128)}, f32[8,2,128,128]{3,2,1,0:T(8,128)}, u32[]{:S(2)}, u32[]{:S(2)}) collective-permute-start(f32[8,2,128,128]{3,2,1,0:T(8,128)} %refs_5_.9), channel_id=1, source_target_pairs={{0,24},{8,0},{16,8},{24,16},{1,25},{9,1},{17,9},{25,17},{2,26},{10... | collective-permute-start | bytes 3145736 | tf_op jit(solution)/shard_map/ppermute | solution.py:361
  17.9 3.1 %partial_0_0_0_all.1.refs_8_ = f32[4,2,128,128]{3,2,1,0:T(8,128)} custom-call(s32[7]{0:T(128)S(1)} %pad_add_fusion.1.refs_0_, s32[32,20]{1,0:T(8,128)S(1)} %pad_add_fusion.refs_1_, f32[2,12]{1,0:T(2,128)S(1)} %copy-done.24, f32[8,2,128,128]{3,2,1,0:T(8,128)S(1)} %copy-done, f32[8,2,128,128]{3,2,1,0:T(8,128)S(1)} %collective-permute-done.3.refs_4_.refs_6_, ...), custom_call_target="tpu_custom_call" | custom-call | flops 1 | bytes 1 | tf_op jit(solution)/shard_map/partial_0_0_0_all/pallas_call | solution.py:308
  21.0 3.1 %partial_0_0_4_all.1.refs_8_ = f32[4,2,128,128]{3,2,1,0:T(8,128)} custom-call(s32[7]{0:T(128)S(1)} %pad_add_fusion.1.refs_0_, s32[32,20]{1,0:T(8,128)S(1)} %pad_add_fusion.refs_1_, f32[2,12]{1,0:T(2,128)S(1)} %copy-done.24, f32[8,2,128,128]{3,2,1,0:T(8,128)S(1)} %copy-done, f32[8,2,128,128]{3,2,1,0:T(8,128)S(1)} %collective-permute-done.3.refs_4_.refs_6_, ...), custom_call_target="tpu_custom_call" | custom-call | flops 1 | bytes 1 | tf_op jit(solution)/shard_map/partial_0_0_4_all/pallas_call | solution.py:308
  26.3 4.4 %partial_0_1_0_all.1.refs_8_.refs_0_ = f32[8,2,128,128]{3,2,1,0:T(8,128)} custom-call(s32[7]{0:T(128)S(1)} %pad_add_fusion.1.refs_0_, s32[32,20]{1,0:T(8,128)S(1)} %pad_add_fusion.refs_1_, f32[2,12]{1,0:T(2,128)S(1)} %copy-done.24, f32[8,2,128,128]{3,2,1,0:T(8,128)S(1)} %copy-done, f32[8,2,128,128]{3,2,1,0:T(8,128)S(1)} %collective-permute-done.3.refs_4_.refs_6_, ...), custom_call_target="tpu_custom_call" | custom-call | flops 1 | bytes 1 | tf_op jit(solution)/shard_map/partial_0_1_0_all/pallas_call | solution.py:308
  30.7 3.0 %collective-permute-start.7 = (f32[8,2,128,128]{3,2,1,0:T(8,128)}, f32[8,2,128,128]{3,2,1,0:T(8,128)}, u32[]{:S(2)}, u32[]{:S(2)}) collective-permute-start(f32[8,2,128,128]{3,2,1,0:T(8,128)} %partial_0_1_0_all.1.refs_8_.refs_0_), channel_id=1, source_target_pairs={{0,2},{6,4},{1,3},{7,5},{8,10},{14,12},{9,11},{15,13},{16,18},{22,... | collective-permute-start | bytes 3145736 | tf_op jit(solution)/shard_map/ppermute | solution.py:374
  33.7 3.4 %partial_0_2_0_all.1.refs_9_.refs_0_ = f32[8,2,128,128]{3,2,1,0:T(8,128)S(1)} custom-call(s32[7]{0:T(128)S(1)} %pad_add_fusion.1.refs_0_, s32[32,20]{1,0:T(8,128)S(1)} %pad_add_fusion.refs_1_, f32[2,12]{1,0:T(2,128)S(1)} %copy-done.24, f32[8,2,128,128]{3,2,1,0:T(8,128)S(1)} %copy-done.1, f32[8,2,128,128]{3,2,1,0:T(8,128)S(1)} %collective-permute-done.3.refs_4_.refs_6_, ...), custom_call_target="tpu_custom_call" | custom-call | flops 1 | bytes 1 | tf_op jit(solution)/shard_map/partial_0_2_0_all/pallas_call | solution.py:308
  39.4 3.6 %sums_0.1 = (f32[8,2,128,128]{3,2,1,0:T(8,128)S(1)}, f32[8,2,128,128]{3,2,1,0:T(8,128)S(1)}) custom-call(s32[7]{0:T(128)S(1)} %pad_add_fusion.1.refs_0_, s32[32,20]{1,0:T(8,128)S(1)} %pad_add_fusion.refs_1_, f32[2,12]{1,0:T(2,128)S(1)} %copy-done.24, s32[8,18]{1,0:T(8,128)S(1)} %reshape.10.refs_3_, s32[8,12]{1,0:T(8,128)S(1)} %copy-done.26, ...), custom_call_target="tpu_custom_call" | custom-call | flops 1 | bytes 1 | tf_op jit(solution)/shard_map/sums_0/pallas_call | solution.py:308
  45.1 3.2 %collective-permute-done.8.refs_1_.refs_14_ = f32[4,2,128,128]{3,2,1,0:T(8,128)} collective-permute-done((f32[4,2,128,128]{3,2,1,0:T(8,128)}, f32[4,2,128,128]{3,2,1,0:T(8,128)}, u32[]{:S(2)}, u32[]{:S(2)}) %collective-permute-start.8) | collective-permute-done | bytes 524320 | tf_op jit(solution)/shard_map/ppermute | solution.py:374
  48.2 2.6 %add_0_1_3.1.refs_3_ = f32[8,2,128,128]{3,2,1,0:T(8,128)} custom-call(f32[8,2,128,128]{3,2,1,0:T(8,128)} %partial_0_1_0_all.1.refs_8_.refs_0_, f32[4,2,128,128]{3,2,1,0:T(8,128)} %collective-permute-done.8.refs_1_.refs_14_, f32[4,2,128,128]{3,2,1,0:T(8,128)} %collective-permute-done.9.refs_2_.refs_15_, f32[128,128]{1,0:T(8,128)S(1)} %tilt_coupling.1.refs_3_.refs_8_.refs_2_), custom_call_target="tpu_custom_call" | custom-call | flops 1 | bytes 1 | tf_op jit(solution)/shard_map/add_0_1_3/pallas_call | solution.py:308
  55.0 3.8 %collective-permute-done.6.refs_3_.refs_12_ = f32[8,2,128,128]{3,2,1,0:T(8,128)} collective-permute-done((f32[8,2,128,128]{3,2,1,0:T(8,128)}, f32[8,2,128,128]{3,2,1,0:T(8,128)}, u32[]{:S(2)}, u32[]{:S(2)}) %collective-permute-start.6) | collective-permute-done | bytes 1048608 | tf_op jit(solution)/shard_map/ppermute | solution.py:361
  58.8 4.1 %collective-permute-start.13 = (f32[8,2,128,128]{3,2,1,0:T(8,128)S(1)}, f32[8,2,128,128]{3,2,1,0:T(8,128)}, u32[]{:S(2)}, u32[]{:S(2)}) collective-permute-start(f32[8,2,128,128]{3,2,1,0:T(8,128)S(1)} %copy-done.9), channel_id=1, source_target_pairs={{0,2},{6,4},{1,3},{7,5},{8,10},{14,12},{9,11},{15,13},{16,18},{22,... | collective-permute-start | bytes 3145736 | tf_op jit(solution)/shard_map/ppermute | solution.py:374
  64.5 6.2 %collective-permute-done.7.refs_1_ = f32[8,2,128,128]{3,2,1,0:T(8,128)} collective-permute-done((f32[8,2,128,128]{3,2,1,0:T(8,128)}, f32[8,2,128,128]{3,2,1,0:T(8,128)}, u32[]{:S(2)}, u32[]{:S(2)}) %collective-permute-start.7) | collective-permute-done | bytes 1048608 | tf_op jit(solution)/shard_map/ppermute | solution.py:374
  70.7 2.3 %add_0_1_2.1.refs_16_ = f32[8,2,128,128]{3,2,1,0:T(8,128)} custom-call(f32[8,2,128,128]{3,2,1,0:T(8,128)S(1)} %copy-done.9, f32[8,2,128,128]{3,2,1,0:T(8,128)} %collective-permute-done.7.refs_1_, f32[8,2,128,128]{3,2,1,0:T(8,128)S(1)} %get-tuple-element.19.refs_2_.refs_3_.refs_5_, f32[8,2,128,128]{3,2,1,0:T(8,128)} %collective-permute-done.6.refs_3_.refs_12_, ...), custom_call_target="tpu_custom_call" | custom-call | flops 1 | bytes 1 | tf_op jit(solution)/shard_map/add_0_1_2/pallas_call | solution.py:308
  75.0 2.7 %collective-permute-done.14.refs_13_ = f32[8,2,128,128]{3,2,1,0:T(8,128)} collective-permute-done((f32[8,2,128,128]{3,2,1,0:T(8,128)}, f32[8,2,128,128]{3,2,1,0:T(8,128)}, u32[]{:S(2)}, u32[]{:S(2)}) %collective-permute-start.14) | collective-permute-done | bytes 1048608 | tf_op jit(solution)/shard_map/ppermute | solution.py:374
  79.6 5.8 %solve_five_ends.1 = (f32[8,2,128,128]{3,2,1,0:T(8,128)S(1)}, f32[4,2,128,128]{3,2,1,0:T(8,128)S(1)}, f32[4,2,128,128]{3,2,1,0:T(8,128)S(1)}) custom-call(s32[7]{0:T(128)S(1)} %pad_add_fusion.1.refs_0_, s32[8,12]{1,0:T(8,128)S(1)} %copy-done.26, f32[12]{0:T(128)S(1)} %copy-done.28, f32[2,12]{1,0:T(2,128)S(1)} %copy-done.24, f32[1,128]{1,0:T(1,128)S(1)} %bitcast.14, ...), custom_call_target="tpu_custom_call" | custom-call | flops 1 | bytes 1 | tf_op jit(solution)/shard_map/solve_five_ends/pallas_call | solution.py:308
  87.3 2.5 %collective-permute-start.16 = (f32[4,2,128,128]{3,2,1,0:T(8,128)S(1)}, f32[4,2,128,128]{3,2,1,0:T(8,128)S(1)}, u32[]{:S(2)}, u32[]{:S(2)}) collective-permute-start(f32[4,2,128,128]{3,2,1,0:T(8,128)S(1)} %get-tuple-element.24), channel_id=1, source_target_pairs={{0,1},{1,0},{6,7},{7,6},{8,9},{9,8},{14,15},{15,14},{16,17},{17,16... | collective-permute-start | bytes 1572872 | tf_op jit(solution)/shard_map/ppermute | solution.py:356
  91.4 3.0 %partial_1_0_0_ends.1.refs_9_ = f32[8,2,128,128]{3,2,1,0:T(8,128)S(1)} custom-call(s32[7]{0:T(128)S(1)} %pad_add_fusion.1.refs_0_, s32[32,20]{1,0:T(8,128)S(1)} %pad_add_fusion.refs_1_, f32[2,12]{1,0:T(2,128)S(1)} %copy-done.24, f32[8,2,128,128]{3,2,1,0:T(8,128)S(1)} %get-tuple-element.19.refs_2_.refs_3_.refs_5_, ...), custom_call_target="tpu_custom_call" | custom-call | flops 1 | bytes 1 | tf_op jit(solution)/shard_map/partial_1_0_0_ends/pallas_call | solution.py:308
  96.1 4.1 %partial_1_1_0_ends.1.refs_9_ = f32[8,2,128,128]{3,2,1,0:T(8,128)} custom-call(s32[7]{0:T(128)S(1)} %pad_add_fusion.1.refs_0_, s32[32,20]{1,0:T(8,128)S(1)} %pad_add_fusion.refs_1_, f32[2,12]{1,0:T(2,128)S(1)} %copy-done.24, f32[8,2,128,128]{3,2,1,0:T(8,128)S(1)} %get-tuple-element.19.refs_2_.refs_3_.refs_5_, ...), custom_call_target="tpu_custom_call" | custom-call | flops 1 | bytes 1 | tf_op jit(solution)/shard_map/partial_1_1_0_ends/pallas_call | solution.py:308
  100.1 3.9 %partial_1_2_0_ends.1.refs_16_ = f32[8,2,128,128]{3,2,1,0:T(8,128)} custom-call(s32[7]{0:T(128)S(1)} %pad_add_fusion.1.refs_0_, s32[32,20]{1,0:T(8,128)S(1)} %pad_add_fusion.refs_1_, f32[2,12]{1,0:T(2,128)S(1)} %copy-done.24, f32[8,2,128,128]{3,2,1,0:T(8,128)S(1)} %get-tuple-element.19.refs_2_.refs_3_.refs_5_, ...), custom_call_target="tpu_custom_call" | custom-call | flops 1 | bytes 1 | tf_op jit(solution)/shard_map/partial_1_2_0_ends/pallas_call | solution.py:308
  104.1 2.3 %solve_five_rest.1 = (f32[8,2,128,128]{3,2,1,0:T(8,128)S(1)}, f32[6,2,128,128]{3,2,1,0:T(8,128)S(1)}, f32[2,2,128,128]{3,2,1,0:T(8,128)S(1)}) custom-call(s32[7]{0:T(128)S(1)} %pad_add_fusion.1.refs_0_, s32[8,12]{1,0:T(8,128)S(1)} %copy-done.26, f32[12]{0:T(128)S(1)} %copy-done.28, f32[2,12]{1,0:T(2,128)S(1)} %copy-done.24, f32[1,128]{1,0:T(1,128)S(1)} %bitcast.15, ...), custom_call_target="tpu_custom_call" | custom-call | flops 1 | bytes 1 | tf_op jit(solution)/shard_map/solve_five_rest/pallas_call | solution.py:308
  106.5 2.3 %collective-permute-start.21 = (f32[8,2,128,128]{3,2,1,0:T(8,128)}, f32[8,2,128,128]{3,2,1,0:T(8,128)}, u32[]{:S(2)}, u32[]{:S(2)}) collective-permute-start(f32[8,2,128,128]{3,2,1,0:T(8,128)} %partial_1_1_0_ends.1.refs_9_), channel_id=1, source_target_pairs={{0,2},{6,4},{1,3},{7,5},{8,10},{14,12},{9,11},{15,13},{16,18},{22,... | collective-permute-start | bytes 3145736 | tf_op jit(solution)/shard_map/ppermute | solution.py:374
  110.5 2.3 %collective-permute-start.24 = (f32[8,2,128,128]{3,2,1,0:T(8,128)}, f32[8,2,128,128]{3,2,1,0:T(8,128)}, u32[]{:S(2)}, u32[]{:S(2)}) collective-permute-start(f32[8,2,128,128]{3,2,1,0:T(8,128)} %partial_1_2_0_ends.1.refs_16_), channel_id=1, source_target_pairs={{0,2},{6,4},{1,3},{7,5},{8,10},{14,12},{9,11},{15,13},{16,18},{22,... | collective-permute-start | bytes 3145736 | tf_op jit(solution)/shard_map/ppermute | solution.py:374
  116.8 2.7 %collective-permute-done.20.refs_1_ = f32[8,2,128,128]{3,2,1,0:T(8,128)S(1)} collective-permute-done((f32[8,2,128,128]{3,2,1,0:T(8,128)S(1)}, f32[8,2,128,128]{3,2,1,0:T(8,128)S(1)}, u32[]{:S(2)}, u32[]{:S(2)}) %collective-permute-start.20) | collective-permute-done | bytes 1048608 | tf_op jit(solution)/shard_map/ppermute | solution.py:374
  125.1 3.4 %sums_1.1 = (f32[8,2,128,128]{3,2,1,0:T(8,128)S(1)}, f32[8,2,128,128]{3,2,1,0:T(8,128)S(1)}) custom-call(s32[7]{0:T(128)S(1)} %pad_add_fusion.1.refs_0_, s32[32,20]{1,0:T(8,128)S(1)} %pad_add_fusion.refs_1_, f32[2,12]{1,0:T(2,128)S(1)} %copy-done.24, s32[8,18]{1,0:T(8,128)S(1)} %reshape.11.refs_3_, s32[8,12]{1,0:T(8,128)S(1)} %copy-done.25, ...), custom_call_target="tpu_custom_call" | custom-call | flops 1 | bytes 1 | tf_op jit(solution)/shard_map/sums_1/pallas_call | solution.py:308
  128.5 13.6 %collective-permute-done.21.refs_1_ = f32[8,2,128,128]{3,2,1,0:T(8,128)} collective-permute-done((f32[8,2,128,128]{3,2,1,0:T(8,128)}, f32[8,2,128,128]{3,2,1,0:T(8,128)}, u32[]{:S(2)}, u32[]{:S(2)}) %collective-permute-start.21) | collective-permute-done | bytes 1048608 | tf_op jit(solution)/shard_map/ppermute | solution.py:374
  145.0 3.1 %back_five.1.refs_7_ = f32[8,2,128,128]{3,2,1,0:T(8,128)} custom-call(f32[128,128]{1,0:T(8,128)S(1)} %copy-done.10, f32[128,128]{1,0:T(8,128)S(1)} %bitcast.10, f32[8,2,128,128]{3,2,1,0:T(8,128)S(1)} %get-tuple-element.25.refs_5_.refs_7_.refs_2_, f32[4,2,128,128]{3,2,1,0:T(8,128)S(1)} %get-tuple-element.29.refs_3_), custom_call_target="tpu_custom_call" | custom-call | flops 1 | bytes 1 | tf_op jit(solution)/shard_map/back_five/pallas_call | solution.py:308
  149.4 2.4 %finish_six.1.refs_6_ = f32[8,2,128,128]{3,2,1,0:T(8,128)S(1)} custom-call(s32[8,12]{1,0:T(8,128)S(1)} %copy-done.25, f32[2,12]{1,0:T(2,128)S(1)} %copy-done.24, f32[128,128]{1,0:T(8,128)S(1)} %tilt_coupling.1.refs_3_.refs_8_.refs_2_, f32[8,2,128,128]{3,2,1,0:T(8,128)S(1)} %get-tuple-element.28.refs_2_.refs_3_, ...), custom_call_target="tpu_custom_call" | custom-call | flops 1 | bytes 1 | tf_op jit(solution)/shard_map/finish_six/pallas_call | solution.py:308
  151.8 12.1 %collective-permute-done.24.refs_8_ = f32[8,2,128,128]{3,2,1,0:T(8,128)} collective-permute-done((f32[8,2,128,128]{3,2,1,0:T(8,128)}, f32[8,2,128,128]{3,2,1,0:T(8,128)}, u32[]{:S(2)}, u32[]{:S(2)}) %collective-permute-start.24) | collective-permute-done | bytes 1048608 | tf_op jit(solution)/shard_map/ppermute | solution.py:374
  164.7 3.5 %solve_six_0.1.refs_11_ = f32[8,2,128,128]{3,2,1,0:T(8,128)} custom-call(s32[8,12]{1,0:T(8,128)S(1)} %copy-done.25, f32[12]{0:T(128)S(1)} %copy-done.28, f32[1,128]{1,0:T(1,128)S(1)} %bitcast.16, f32[128,1]{1,0:T(8,128)S(1)} %copy.25.refs_5_.refs_3_, f32[128,128]{1,0:T(8,128)S(1)} %copy-done.10, f32[128,128]{1,0:T(8,128)S(1)} %bitcast.11, ...), custom_call_target="tpu_custom_call" | custom-call | flops 1 | bytes 1 | tf_op jit(solution)/shard_map/solve_six_0/pallas_call | solution.py:308
  168.2 3.5 %solve_six_1.1 = f32[8,2,128,128]{3,2,1,0:T(8,128)} custom-call(s32[8,12]{1,0:T(8,128)S(1)} %copy-done.25, f32[12]{0:T(128)S(1)} %copy-done.28, f32[1,128]{1,0:T(1,128)S(1)} %bitcast.17, f32[128,1]{1,0:T(8,128)S(1)} %copy.25.refs_5_.refs_3_, f32[128,128]{1,0:T(8,128)S(1)} %copy-done.10, f32[128,128]{1,0:T(8,128)S(1)} %bitcast.12, ...), custom_call_target="tpu_custom_call", output_to_operand_aliasing={{}: (11, {})} | custom-call | flops 1 | bytes 1 | tf_op jit(solution)/shard_map/solve_six_1/pallas_call | solution.py:308
  (132 shorter events, 46.7 us)
Async XLA Ops:
  0.6 16.0 %collective-permute-start.3 = (f32[8,2,128,128]{3,2,1,0:T(8,128)}, f32[8,2,128,128]{3,2,1,0:T(8,128)S(1)}, u32[]{:S(2)}, u32[]{:S(2)}) collective-permute-start(f32[8,2,128,128]{3,2,1,0:T(8,128)} %refs_5_.9), channel_id=1, source_target_pairs={{0,1},{1,0},{2,3},{3,2},{4,5},{5,4},{6,7},{7,6},{8,9},{9,8},{10,11... | collective-permute-start | bytes 3145736 | tf_op jit(solution)/shard_map/ppermute | solution.py:356
  1.2 15.5 %collective-permute-start.4 = (f32[8,2,128,128]{3,2,1,0:T(8,128)}, f32[8,2,128,128]{3,2,1,0:T(8,128)S(1)}, u32[]{:S(2)}, u32[]{:S(2)}) collective-permute-start(f32[8,2,128,128]{3,2,1,0:T(8,128)} %refs_7_.9), channel_id=1, source_target_pairs={{0,1},{1,0},{2,3},{3,2},{4,5},{5,4},{6,7},{7,6},{8,9},{9,8},{10,11... | collective-permute-start | bytes 3145736 | tf_op jit(solution)/shard_map/ppermute | solution.py:356
  4.7 11.9 %copy-start.18 = (f32[128,128]{1,0:T(8,128)S(1)}, f32[128,128]{1,0:T(8,128)}, u32[]{:S(2)}) copy-start(f32[128,128]{1,0:T(8,128)} %refs_8_.3) | copy-start | bytes 196612
  4.9 8.1 %collective-permute-start = (s32[8,20]{1,0:T(8,128)S(1)}, s32[8,20]{1,0:T(8,128)S(1)}, u32[]{:S(2)}, u32[]{:S(2)}) collective-permute-start(s32[8,20]{1,0:T(8,128)S(1)} %concatenate.13), channel_id=1, source_target_pairs={{0,2},{1,3},{2,4},{3,5},{4,6},{5,7},{6,0},{7,1},{8,10},{9,11},{10,... | collective-permute-start | bytes 1928 | tf_op jit(solution)/shard_map/ppermute | solution.py:364
  7.9 6.6 %collective-permute-start.1 = (s32[8,20]{1,0:T(8,128)S(1)}, s32[8,20]{1,0:T(8,128)S(1)}, u32[]{:S(2)}, u32[]{:S(2)}) collective-permute-start(s32[8,20]{1,0:T(8,128)S(1)} %concatenate.13), channel_id=1, source_target_pairs={{0,4},{1,5},{2,6},{3,7},{4,0},{5,1},{6,2},{7,3},{8,12},{9,13},{10,... | collective-permute-start | bytes 1928 | tf_op jit(solution)/shard_map/ppermute | solution.py:364
  10.5 41.8 %collective-permute-start.5 = (f32[8,2,128,128]{3,2,1,0:T(8,128)}, f32[8,2,128,128]{3,2,1,0:T(8,128)}, u32[]{:S(2)}, u32[]{:S(2)}) collective-permute-start(f32[8,2,128,128]{3,2,1,0:T(8,128)} %refs_5_.9), channel_id=1, source_target_pairs={{0,24},{8,0},{16,8},{24,16},{1,25},{9,1},{17,9},{25,17},{2,26},{10... | collective-permute-start | bytes 3145736 | tf_op jit(solution)/shard_map/ppermute | solution.py:361
  13.0 3.7 %collective-permute-start.2 = (s32[8,20]{1,0:T(8,128)S(1)}, s32[8,20]{1,0:T(8,128)S(1)}, u32[]{:S(2)}, u32[]{:S(2)}) collective-permute-start(s32[8,20]{1,0:T(8,128)S(1)} %concatenate.13), channel_id=1, source_target_pairs={{0,6},{1,7},{2,0},{3,1},{4,2},{5,3},{6,4},{7,5},{8,14},{9,15},{10,... | collective-permute-start | bytes 1928 | tf_op jit(solution)/shard_map/ppermute | solution.py:364
  24.1 21.0 %collective-permute-start.9 = (f32[4,2,128,128]{3,2,1,0:T(8,128)}, f32[4,2,128,128]{3,2,1,0:T(8,128)}, u32[]{:S(2)}, u32[]{:S(2)}) collective-permute-start(f32[4,2,128,128]{3,2,1,0:T(8,128)} %partial_0_0_4_all.1.refs_8_), channel_id=1, source_target_pairs={{0,2},{6,4},{1,3},{7,5},{4,6},{2,0},{5,7},{3,1},{8,10},{14,12},{9,... | collective-permute-start | bytes 1572872 | tf_op jit(solution)/shard_map/ppermute | solution.py:374
  24.3 23.9 %collective-permute-start.8 = (f32[4,2,128,128]{3,2,1,0:T(8,128)}, f32[4,2,128,128]{3,2,1,0:T(8,128)}, u32[]{:S(2)}, u32[]{:S(2)}) collective-permute-start(f32[4,2,128,128]{3,2,1,0:T(8,128)} %partial_0_0_0_all.1.refs_8_), channel_id=1, source_target_pairs={{0,2},{6,4},{1,3},{7,5},{4,6},{2,0},{5,7},{3,1},{8,10},{14,12},{9,... | collective-permute-start | bytes 1572872 | tf_op jit(solution)/shard_map/ppermute | solution.py:374
  26.1 32.7 %collective-permute-start.6 = (f32[8,2,128,128]{3,2,1,0:T(8,128)}, f32[8,2,128,128]{3,2,1,0:T(8,128)}, u32[]{:S(2)}, u32[]{:S(2)}) collective-permute-start(f32[8,2,128,128]{3,2,1,0:T(8,128)} %refs_7_.9), channel_id=1, source_target_pairs={{0,8},{8,16},{16,24},{24,0},{1,9},{9,17},{17,25},{25,1},{2,10},{10... | collective-permute-start | bytes 3145736 | tf_op jit(solution)/shard_map/ppermute | solution.py:361
  30.7 40.0 %collective-permute-start.7 = (f32[8,2,128,128]{3,2,1,0:T(8,128)}, f32[8,2,128,128]{3,2,1,0:T(8,128)}, u32[]{:S(2)}, u32[]{:S(2)}) collective-permute-start(f32[8,2,128,128]{3,2,1,0:T(8,128)} %partial_0_1_0_all.1.refs_8_.refs_0_), channel_id=1, source_target_pairs={{0,2},{6,4},{1,3},{7,5},{8,10},{14,12},{9,11},{15,13},{16,18},{22,... | collective-permute-start | bytes 3145736 | tf_op jit(solution)/shard_map/ppermute | solution.py:374
  50.8 26.9 %collective-permute-start.14 = (f32[8,2,128,128]{3,2,1,0:T(8,128)}, f32[8,2,128,128]{3,2,1,0:T(8,128)}, u32[]{:S(2)}, u32[]{:S(2)}) collective-permute-start(f32[8,2,128,128]{3,2,1,0:T(8,128)} %add_0_1_3.1.refs_3_), channel_id=1, source_target_pairs={{2,6},{4,0},{3,7},{5,1},{10,14},{12,8},{11,15},{13,9},{18,22},{20,... | collective-permute-start | bytes 3145736 | tf_op jit(solution)/shard_map/ppermute | solution.py:374
  54.4 8.5 %collective-permute-start.10 = (f32[4,2,128,128]{3,2,1,0:T(8,128)S(1)}, f32[4,2,128,128]{3,2,1,0:T(8,128)S(1)}, u32[]{:S(2)}, u32[]{:S(2)}) collective-permute-start(f32[4,2,128,128]{3,2,1,0:T(8,128)S(1)} %get-tuple-element.20), channel_id=1, source_target_pairs={{0,1},{1,0},{2,3},{3,2},{4,5},{5,4},{6,7},{7,6},{8,9},{9,8},{10,11... | collective-permute-start | bytes 1572872 | tf_op jit(solution)/shard_map/ppermute | solution.py:356
  54.5 10.0 %collective-permute-start.11 = (f32[4,2,128,128]{3,2,1,0:T(8,128)S(1)}, f32[4,2,128,128]{3,2,1,0:T(8,128)S(1)}, u32[]{:S(2)}, u32[]{:S(2)}) collective-permute-start(f32[4,2,128,128]{3,2,1,0:T(8,128)S(1)} %get-tuple-element.21), channel_id=1, source_target_pairs={{0,1},{1,0},{2,3},{3,2},{4,5},{5,4},{6,7},{7,6},{8,9},{9,8},{10,11... | collective-permute-start | bytes 1572872 | tf_op jit(solution)/shard_map/ppermute | solution.py:356
  58.8 31.8 %collective-permute-start.13 = (f32[8,2,128,128]{3,2,1,0:T(8,128)S(1)}, f32[8,2,128,128]{3,2,1,0:T(8,128)}, u32[]{:S(2)}, u32[]{:S(2)}) collective-permute-start(f32[8,2,128,128]{3,2,1,0:T(8,128)S(1)} %copy-done.9), channel_id=1, source_target_pairs={{0,2},{6,4},{1,3},{7,5},{8,10},{14,12},{9,11},{15,13},{16,18},{22,... | collective-permute-start | bytes 3145736 | tf_op jit(solution)/shard_map/ppermute | solution.py:374
  62.9 10.1 %copy-start.19 = (f32[4,2,128,128]{3,2,1,0:T(8,128)}, f32[4,2,128,128]{3,2,1,0:T(8,128)S(1)}, u32[]{:S(2)}) copy-start(f32[4,2,128,128]{3,2,1,0:T(8,128)S(1)} %collective-permute-done.10.refs_4_) | copy-start | bytes 1572868
  62.9 14.8 %copy-start.5 = (f32[8,2,128,128]{3,2,1,0:T(8,128)S(1)}, f32[8,2,128,128]{3,2,1,0:T(8,128)}, u32[]{:S(2)}) copy-start(f32[8,2,128,128]{3,2,1,0:T(8,128)} %copy-done.4) | copy-start | bytes 3145732
  62.9 41.2 %collective-permute-start.17 = (f32[8,2,128,128]{3,2,1,0:T(8,128)S(1)}, f32[8,2,128,128]{3,2,1,0:T(8,128)}, u32[]{:S(2)}, u32[]{:S(2)}) collective-permute-start(f32[8,2,128,128]{3,2,1,0:T(8,128)S(1)} %get-tuple-element.19.refs_2_.refs_3_.refs_5_), channel_id=1, source_target_pairs={{0,24},{8,0},{16,8},{24,16},{1,25},{9,1},{17,9},{25,17},{2,26},{10... | collective-permute-start | bytes 3145736 | tf_op jit(solution)/shard_map/ppermute | solution.py:361
  73.0 31.1 %collective-permute-start.12 = (f32[8,2,128,128]{3,2,1,0:T(8,128)}, f32[8,2,128,128]{3,2,1,0:T(8,128)}, u32[]{:S(2)}, u32[]{:S(2)}) collective-permute-start(f32[8,2,128,128]{3,2,1,0:T(8,128)} %add_0_1_2.1.refs_16_), channel_id=1, source_target_pairs={{2,4},{4,2},{3,5},{5,3},{10,12},{12,10},{11,13},{13,11},{18,20},{2... | collective-permute-start | bytes 3145736 | tf_op jit(solution)/shard_map/ppermute | solution.py:374
  79.6 10.3 %copy-start.20 = (f32[4,2,128,128]{3,2,1,0:T(8,128)S(1)}, f32[4,2,128,128]{3,2,1,0:T(8,128)}, u32[]{:S(2)}) copy-start(f32[4,2,128,128]{3,2,1,0:T(8,128)} %copy-done.19) | copy-start | bytes 1572868
  85.4 5.3 %collective-permute-start.15 = (f32[4,2,128,128]{3,2,1,0:T(8,128)S(1)}, f32[4,2,128,128]{3,2,1,0:T(8,128)S(1)}, u32[]{:S(2)}, u32[]{:S(2)}) collective-permute-start(f32[4,2,128,128]{3,2,1,0:T(8,128)S(1)} %get-tuple-element.23), channel_id=1, source_target_pairs={{0,1},{1,0},{6,7},{7,6},{8,9},{9,8},{14,15},{15,14},{16,17},{17,16... | collective-permute-start | bytes 1572872 | tf_op jit(solution)/shard_map/ppermute | solution.py:356
  87.3 4.1 %collective-permute-start.16 = (f32[4,2,128,128]{3,2,1,0:T(8,128)S(1)}, f32[4,2,128,128]{3,2,1,0:T(8,128)S(1)}, u32[]{:S(2)}, u32[]{:S(2)}) collective-permute-start(f32[4,2,128,128]{3,2,1,0:T(8,128)S(1)} %get-tuple-element.24), channel_id=1, source_target_pairs={{0,1},{1,0},{6,7},{7,6},{8,9},{9,8},{14,15},{15,14},{16,17},{17,16... | collective-permute-start | bytes 1572872 | tf_op jit(solution)/shard_map/ppermute | solution.py:356
  94.3 25.2 %collective-permute-start.20 = (f32[8,2,128,128]{3,2,1,0:T(8,128)S(1)}, f32[8,2,128,128]{3,2,1,0:T(8,128)S(1)}, u32[]{:S(2)}, u32[]{:S(2)}) collective-permute-start(f32[8,2,128,128]{3,2,1,0:T(8,128)S(1)} %partial_1_0_0_ends.1.refs_9_), channel_id=1, source_target_pairs={{0,2},{6,4},{1,3},{7,5},{8,10},{14,12},{9,11},{15,13},{16,18},{22,... | collective-permute-start | bytes 3145736 | tf_op jit(solution)/shard_map/ppermute | solution.py:374
  106.5 6.3 %collective-permute-start.18 = (f32[6,2,128,128]{3,2,1,0:T(8,128)S(1)}, f32[6,2,128,128]{3,2,1,0:T(8,128)S(1)}, u32[]{:S(2)}, u32[]{:S(2)}) collective-permute-start(f32[6,2,128,128]{3,2,1,0:T(8,128)S(1)} %get-tuple-element.26), channel_id=1, source_target_pairs={{0,1},{1,0},{2,3},{3,2},{4,5},{5,4},{6,7},{7,6},{8,9},{9,8},{10,11... | collective-permute-start | bytes 2359304 | tf_op jit(solution)/shard_map/ppermute | solution.py:356
  106.5 35.5 %collective-permute-start.21 = (f32[8,2,128,128]{3,2,1,0:T(8,128)}, f32[8,2,128,128]{3,2,1,0:T(8,128)}, u32[]{:S(2)}, u32[]{:S(2)}) collective-permute-start(f32[8,2,128,128]{3,2,1,0:T(8,128)} %partial_1_1_0_ends.1.refs_9_), channel_id=1, source_target_pairs={{0,2},{6,4},{1,3},{7,5},{8,10},{14,12},{9,11},{15,13},{16,18},{22,... | collective-permute-start | bytes 3145736 | tf_op jit(solution)/shard_map/ppermute | solution.py:374
  108.8 35.3 %collective-permute-start.22 = (f32[8,2,128,128]{3,2,1,0:T(8,128)S(1)}, f32[8,2,128,128]{3,2,1,0:T(8,128)}, u32[]{:S(2)}, u32[]{:S(2)}) collective-permute-start(f32[8,2,128,128]{3,2,1,0:T(8,128)S(1)} %get-tuple-element.25.refs_5_.refs_7_.refs_2_), channel_id=1, source_target_pairs={{0,8},{8,16},{16,24},{24,0},{1,9},{9,17},{17,25},{25,1},{2,10},{10... | collective-permute-start | bytes 3145736 | tf_op jit(solution)/shard_map/ppermute | solution.py:361
  108.8 1.6 collective-permute-start.19
  110.5 53.4 %collective-permute-start.24 = (f32[8,2,128,128]{3,2,1,0:T(8,128)}, f32[8,2,128,128]{3,2,1,0:T(8,128)}, u32[]{:S(2)}, u32[]{:S(2)}) collective-permute-start(f32[8,2,128,128]{3,2,1,0:T(8,128)} %partial_1_2_0_ends.1.refs_16_), channel_id=1, source_target_pairs={{0,2},{6,4},{1,3},{7,5},{8,10},{14,12},{9,11},{15,13},{16,18},{22,... | collective-permute-start | bytes 3145736 | tf_op jit(solution)/shard_map/ppermute | solution.py:374
  114.6 50.1 %collective-permute-start.26 = (f32[8,2,128,128]{3,2,1,0:T(8,128)}, f32[8,2,128,128]{3,2,1,0:T(8,128)}, u32[]{:S(2)}, u32[]{:S(2)}) collective-permute-start(f32[8,2,128,128]{3,2,1,0:T(8,128)} %partial_1_0_0_rest.1.refs_9_), channel_id=1, source_target_pairs={{4,6},{2,0},{5,7},{3,1},{12,14},{10,8},{13,15},{11,9},{20,22},{18,... | collective-permute-start | bytes 3145736 | tf_op jit(solution)/shard_map/ppermute | solution.py:374
  120.7 44.0 %collective-permute-start.25 = (f32[8,2,128,128]{3,2,1,0:T(8,128)}, f32[8,2,128,128]{3,2,1,0:T(8,128)}, u32[]{:S(2)}, u32[]{:S(2)}) collective-permute-start(f32[8,2,128,128]{3,2,1,0:T(8,128)} %add_1_1_3.1.refs_9_), channel_id=1, source_target_pairs={{2,6},{4,0},{3,7},{5,1},{10,14},{12,8},{11,15},{13,9},{18,22},{20,... | collective-permute-start | bytes 3145736 | tf_op jit(solution)/shard_map/ppermute | solution.py:374
  143.4 20.5 %collective-permute-start.27 = (f32[4,2,128,128]{3,2,1,0:T(8,128)S(1)}, f32[4,2,128,128]{3,2,1,0:T(8,128)S(1)}, u32[]{:S(2)}, u32[]{:S(2)}) collective-permute-start(f32[4,2,128,128]{3,2,1,0:T(8,128)S(1)} %get-tuple-element.29.refs_3_), channel_id=1, source_target_pairs={{2,4},{4,2},{3,5},{5,3},{10,12},{12,10},{11,13},{13,11},{18,20},{2... | collective-permute-start | bytes 1572872 | tf_op jit(solution)/shard_map/ppermute | solution.py:374
  144.1 24.1 %collective-permute-start.23 = (f32[4,2,128,128]{3,2,1,0:T(8,128)S(1)}, f32[4,2,128,128]{3,2,1,0:T(8,128)S(1)}, u32[]{:S(2)}, u32[]{:S(2)}) collective-permute-start(f32[4,2,128,128]{3,2,1,0:T(8,128)S(1)} %get-tuple-element.31), channel_id=1, source_target_pairs={{2,4},{4,2},{3,5},{5,3},{10,12},{12,10},{11,13},{13,11},{18,20},{2... | collective-permute-start | bytes 1572872 | tf_op jit(solution)/shard_map/ppermute | solution.py:374
  (30 other events, 91.2 us)

commit v3 on v2

--- a/solution.py
+++ b/solution.py
@@ -1,4 +1,5 @@
 import functools
+import math
 
 import jax
 import jax.numpy as jnp
@@ -10,7 +11,7 @@
 SMEM = pltpu.SMEM
 VMEM = pltpu.VMEM
 HALVES = 2
-TOGETHER = 2
+TOGETHER = 4
 
 
 def split(x):
@@ -67,40 +68,40 @@
         peer = table[row, column + j]
         spot = table[row, column + 4 + j]
         here = peer >> 1 == chip
-        for sibling in range(2):
-            own = (peer & 1 == core) if sibling == 0 else (peer & 1 != core)
-
-            @pl.when(jnp.logical_and(here, own))
-            def _(j=j, sibling=sibling, spot=spot):
+        own, *pieces = upper if j < 2 else lower
+        first = 0
+        for number, source in enumerate([own, *pieces]):
+            if number == 0:
+                held = jnp.logical_and(here, peer & 1 == core)
+                at = spot
+            else:
+                held = jnp.logical_and(here, peer & 1 != core)
+                if len(pieces) > 1:
+                    inside = jnp.logical_and(spot >= first, spot < first + source.shape[0])
+                    held = jnp.logical_and(held, inside)
+                at = spot - first
+                first += source.shape[0]
+
+            @pl.when(held)
+            def _(j=j, source=source, at=at):
                 if j < 2:
-                    mixed[...] += upper[sibling][spot]
+                    mixed[...] += source[at]
                 else:
                     mode = j - 1
                     count = table[row, column + 6 + j].astype(jnp.float32)
-                    source = lower[sibling][spot]
-                    mixed[...] += (count * bath[0, mode]) * source
-                    turned[...] += (count * bath[1, mode]) * source
-
-
-def joined(pieces, scratch):
-    if len(pieces) == 1:
-        return pieces[0]
-    row = 0
-    for piece in pieces:
-        scratch[row : row + piece.shape[0]] = piece[...]
-        row += piece.shape[0]
-    return scratch
-
-
-def partial_kernel(slot, first, column, role, place, table, bath, *refs):
-    upper, pieces, (c_ref, out, mixed, turned, sibling) = refs[:2], refs[3:-5], refs[-5:]
+                    mixed[...] += (count * bath[0, mode]) * source[at]
+                    turned[...] += (count * bath[1, mode]) * source[at]
+
+
+def partial_kernel(slot, column, role, counts, place, table, bath, *refs):
+    upper, lower = refs[: counts[0]], refs[counts[0] : sum(counts)]
+    c_ref, out, mixed, turned = refs[sum(counts) :]
     rows = upper[0].shape[0]
     together = mixed.shape[0]
 
     def work():
         c_left = as_left(c_ref[...])
         c_right = as_right(c_ref[...])
-        lower = (refs[2], joined(pieces, sibling))
 
         @pl.loop(0, out.shape[0], step=together)
         def _(m):
@@ -108,7 +109,7 @@
             turned[...] = jnp.zeros_like(turned)
             for u in range(together):
                 add_requests(
-                    place[3 + slot] * rows + first + m + u,
+                    place[3 + slot] * rows + m + u,
                     column,
                     place,
                     table,
@@ -135,9 +136,9 @@
         pl.when(place[2] != 0)(work)
 
 
-def sums_kernel(slot, column, place, table, bath, nearby, occupation, *refs):
-    upper, pieces, (mixed_out, turned_out, sibling) = refs[:2], refs[3:-3], refs[-3:]
-    lower = (refs[2], joined(pieces, sibling))
+def sums_kernel(slot, column, counts, place, table, bath, nearby, occupation, *refs):
+    upper, lower = refs[: counts[0]], refs[counts[0] : sum(counts)]
+    mixed_out, turned_out = refs[sum(counts) :]
     rows = upper[0].shape[0]
     modes = bath.shape[1]
 
@@ -199,10 +200,8 @@
 
 
 def solve_five_kernel(
-    counts, role, place, occupation, decay, bath, e_row, e_column, e_ref, et_ref, c_ref, *rest
+    counts, role, place, occupation, decay, e_row, e_column, e_ref, et_ref, own, *rest
 ):
-    mixed, turned, raised, lowered = rest[:4]
-    rest = rest[4:]
     arrivals = []
     for count in counts[1:]:
         arrivals.append(rows_of(rest[:count]))
@@ -214,12 +213,9 @@
         splitting = e_column[...] - e_row[...]
         in_left = as_left(et_ref[...])
         in_right = as_right(e_ref[...])
-        c_left = as_left(c_ref[...])
-        c_right = as_right(c_ref[...])
         for m in range(out.shape[0]):
-            real, imag = own_drive(
-                m, occupation, bath, mixed, turned, raised, lowered, c_left, c_right
-            )
+            real = own[m, 0]
+            imag = own[m, 1]
             for arrival in arrivals:
                 piece, row = arrival[m]
                 real = real + piece[row, 0]
@@ -313,7 +309,7 @@
             + [pl.BlockSpec(memory_space=pl.ANY)] * len(waits),
             out_specs=options.pop("out_specs", [plain] * len(outs)),
             scratch_shapes=scratch,
-            compiler_params=pltpu.CompilerParams(vmem_limit_bytes=24 * 1024 * 1024),
+            compiler_params=pltpu.CompilerParams(vmem_limit_bytes=12 * 1024 * 1024),
             cost_estimate=pl.CostEstimate(flops=1, bytes_accessed=1, transcendentals=0),
             name=name,
             **options,
@@ -349,8 +345,8 @@
     chips = peer_count // 2
     per = rows // HALVES
     whole = jax.ShapeDtypeStruct(tier_four.shape, jnp.float32)
-    a_tier = pltpu.VMEM(tier_four.shape, jnp.float32)
-    work_space = [pltpu.VMEM((TOGETHER,) + tier_four.shape[1:], jnp.float32)] * 2 + [a_tier]
+    together = math.gcd(rows, TOGETHER)
+    work_space = [pltpu.VMEM((together,) + tier_four.shape[1:], jnp.float32)] * 2
 
     def sibling_of(array, of_chips):
         return lax.ppermute(
@@ -384,7 +380,8 @@
         ],
         axis=1,
     )
-    table = jnp.concatenate([mine] + [turn_line(mine, by) for by in range(1, chips)], axis=0)
+    tables = [mine] + [turn_line(mine, by) for by in range(1, chips)]
+    table = jnp.concatenate(tables, axis=0)
     columns = (0, mine.shape[1] // 2)
 
     goals = list(range(chips - 1, 0, -1))
@@ -406,17 +403,18 @@
         [jnp.stack([chip, index % 2, depth]), (chip - goal + chips) % chips]
     ).astype(jnp.int32)
 
-    def partial(tier, slot, upper, lower, c, role, after=(), half=None):
-        first, count = (0, rows) if half is None else (half * per, per)
+    def partial(tier, slot, upper, lower, c, role, after=()):
         return call(
-            functools.partial(partial_kernel, slot, first, columns[tier], role),
-            [jax.ShapeDtypeStruct((count,) + whole.shape[1:], jnp.float32)],
+            functools.partial(
+                partial_kernel, slot, columns[tier], role, (len(upper), len(lower))
+            ),
+            [whole],
             [place, table, bath_coefficients],
             [*upper, *lower, c],
             work_space,
-            f"partial_{tier}_{slot}_{first}_{role}",
+            f"partial_{tier}_{slot}_{role}",
             after=after,
-        )[0]
+        )
 
     def steps_to(g):
         last = g - 1 if skips and g == chips - 1 else g
@@ -428,14 +426,13 @@
     def start(sent, g):
         return [hop(array, (0, next_stop(0, g))) for array in sent[slot_of(0, g)]]
 
-    def go_on(tier, sent, arrived, g, after=(), count=1):
+    def go_on(tier, sent, arrived, g, after=(), cuts=None):
         for step in steps_to(g)[1:]:
-            parts = count if step == steps_to(g)[-1] else 1
+            parts = cuts if cuts and step == steps_to(g)[-1] else [rows]
             ours = sent[slot_of(step, g)]
-            piece = jax.ShapeDtypeStruct((rows // parts,) + whole.shape[1:], jnp.float32)
             messages = call(
                 functools.partial(add_kernel, (len(ours), len(arrived))),
-                [piece] * parts,
+                [jax.ShapeDtypeStruct((cut,) + whole.shape[1:], jnp.float32) for cut in parts],
                 [],
                 [*ours, *arrived],
                 (),
@@ -447,11 +444,11 @@
 
     def sums(tier, upper, lower, nearby, occupation):
         return call(
-            functools.partial(sums_kernel, chips - 1, columns[tier]),
+            functools.partial(sums_kernel, chips - 1, columns[tier], (len(upper), len(lower))),
             [whole, whole],
             [place, table, bath_coefficients, nearby.reshape(rows, -1), occupation],
             [*upper, *lower],
-            [a_tier],
+            (),
             f"sums_{tier}",
         )
 
@@ -460,33 +457,37 @@
     every = range(chips)
     ends = [0, chips - 1]
 
-    def solve_five(arrays, last, role, previous, cuts, after=()):
+    def solve_five(own, last, role, previous, cuts, after=()):
         got = call(
             functools.partial(
                 solve_five_kernel, [len(previous), *[len(pieces) for pieces in last]], role
             ),
             [whole]
             + [jax.ShapeDtypeStruct((cut,) + whole.shape[1:], jnp.float32) for cut in cuts],
-            [place, occupation_five, decay_rates, bath_coefficients],
-            [*bases, coupling, *arrays, *[piece for pieces in last for piece in pieces], *previous],
+            [place, occupation_five, decay_rates],
+            [*bases, own, *[piece for pieces in last for piece in pieces], *previous],
             (),
             f"solve_five_{role}",
             after=after,
         )
         return got[0], got[1:]
 
-    def solve_six(own, last, half, previous):
+    last_cuts = [rows - rows // 4, rows // 4]
+
+    def solve_six(own, last, number, previous):
+        cut = last_cuts[number]
         plain = pl.BlockSpec(memory_space=VMEM)
-        block = pl.BlockSpec((per,) + whole.shape[1:], lambda i: (half, 0, 0, 0))
-        parts = [pieces[half * len(pieces) // HALVES] for pieces in last]
+        first = sum(last_cuts[:number])
+        block = pl.BlockSpec((cut,) + whole.shape[1:], lambda i: (first // cut, 0, 0, 0))
+        parts = [pieces[number % len(pieces)] for pieces in last]
         arrays = [*bases, own, *parts, *previous]
         return call(
-            functools.partial(solve_six_kernel, half * per, len(parts)),
+            functools.partial(solve_six_kernel, first, len(parts)),
             [whole],
             [occupation_six, decay_rates],
             arrays,
             (),
-            f"solve_six_{half}",
+            f"solve_six_{number}",
             [plain] * len(bases)
             + [block]
             + [block if len(pieces) == 1 else plain for pieces in last]
@@ -505,13 +506,11 @@
     aside = [(far - 1, far)] if skips else []
     sent_five = {}
     moving_five = {}
-    sent_five[0] = [
-        partial(0, 0, upper_five, lower_five, coupling, "all", (), half) for half in range(HALVES)
-    ]
+    sent_five[0] = partial(0, 0, upper_five, lower_five, coupling, "all")
     moving_five[far] = [hop(array, (0, next_stop(0, far)), *aside) for array in sent_five[0]]
     beside_five = [moving_five[far]] if skips else []
     for slot in slots[1:]:
-        sent_five[slot] = [partial(0, slot, upper_five, lower_five, coupling, "all")]
+        sent_five[slot] = partial(0, slot, upper_five, lower_five, coupling, "all")
         moving_five[goals[slot]] = start(sent_five, goals[slot])
     sums_five = sums(0, upper_five, lower_five, local_five, occupation_five)
     tilted = call(
@@ -533,12 +532,20 @@
         after=[raised_five],
     )
     pieces = [sibling_of(piece, every) for piece in pieces]
-    upper_six = (eigen_seven, jnp.concatenate(pieces))
+    upper_six = (eigen_seven, *pieces)
     raised_six = along(eigen_seven, -1)
     for g in goals[1:]:
-        after = [lowered_five, *pieces] if g == goals[-2] else []
+        after = [lowered_five] if g == goals[-2] else []
         moving_five[g] = go_on(0, sent_five, moving_five[g], g, after)
-    own_five = [*sums_five, raised_five, lowered_five]
+    own_five = call(
+        finish_kernel,
+        [whole],
+        [occupation_five, bath_coefficients],
+        [coupling, *sums_five, raised_five, lowered_five],
+        (),
+        "finish_five",
+        after=pieces,
+    )[0]
     last = [moving_five[far], *beside_five]
     ends_five, pieces = solve_five(own_five, last, "ends", [], [per] * HALVES)
     lower_ends = (ends_five, *[sibling_of(piece, ends) for piece in pieces])
@@ -546,14 +553,13 @@
     moving_six = {}
 
     def from_ends(slot, after=()):
-        sent_ends[slot] = [partial(1, slot, upper_six, lower_ends, tilted, "ends", after)]
+        sent_ends[slot] = partial(1, slot, upper_six, lower_ends, tilted, "ends", after)
         moving_six[goals[slot]] = start(sent_ends, goals[slot])
 
-    from_ends(0, moving_five[goals[-1]])
-    for slot in slots[1:]:
-        from_ends(slot)
+    for slot in slots:
+        from_ends(slot, moving_five[goals[-1]] if slot == 1 else [])
     last = [moving_five[g] for g in goals[1:]]
-    cuts = [rows - rows // 4, rows // 4]
+    cuts = [4, 4]
     eigen_five, pieces = solve_five(own_five, last, "rest", [ends_five], cuts, [raised_six])
     lower_six = (eigen_five, *[sibling_of(piece, every) for piece in pieces])
     lowered_six = along(eigen_five, 1)
@@ -561,10 +567,10 @@
 
     def from_rest(slot):
         if slot not in sent_six:
-            sent_six[slot] = [partial(1, slot, upper_six, lower_six, tilted, "rest")]
+            sent_six[slot] = partial(1, slot, upper_six, lower_six, tilted, "rest")
 
     from_rest(0)
-    beside_six = [hop(sent_six[0][0], *aside)] if skips else []
+    beside_six = [[hop(sent_six[0][0], *aside)]] if skips else []
     for step in steps_to(far)[1:]:
         from_rest(slot_of(step, far))
     moving_six[far] = go_on(1, sent_six, moving_six[far], far)
@@ -572,7 +578,7 @@
         from_rest(slot)
     sums_six = sums(1, upper_six, lower_six, local_six, occupation_six)
     for g in goals[1:]:
-        moving_six[g] = go_on(1, sent_six, moving_six[g], g, [], HALVES)
+        moving_six[g] = go_on(1, sent_six, moving_six[g], g, [], last_cuts)
     updated_five = call(
         turn_kernel, [whole], [], [eigenbasis, turned, eigen_five], (), "back_five"
     )[0]
@@ -585,10 +591,9 @@
         "finish_six",
     )[0]
     previous = []
-    for half in range(HALVES):
-        last = [moving_six[g] for g in goals[1:]]
-        last += [moving_six[far], *[[array] for array in beside_six]]
-        previous = solve_six(own_six, last, half, previous)
+    for number in range(len(last_cuts)):
+        last = [*[moving_six[g] for g in goals[1:]], moving_six[far], *beside_six]
+        previous = solve_six(own_six, last, number, previous)
     return (updated_five, previous[0])
 
 

time: 175 us -> 169 us (0.966)
  local copies, waits for them, and re-layouts: 14.5 us -> 10.1 us
  Pallas kernels: 65.9 us -> 63.8 us
  waiting for transfers between devices: 49.9 us -> 51.9 us
    ppermute x4, waiting for transfers between devices: 3.84 us -> 15.9 us  [along(): lax.ppermute(array, 'ma', [(i, (i + by) % row_count) for i in range(row_c...]
    ppermute x13 -> x12, waiting for transfers between devices: 42 us -> 31.6 us  [hop(): return lax.ppermute(array, 'mb', pairs)]
    unnamed x74 -> x57, local copies, waits for them, and re-layouts: 14 us -> 9.6 us
    pallas_call x24, Pallas kernels: 65.9 us -> 63.8 us  [call(): pl.pallas_call(without_waits, out_shape=outs, in_specs=[pl.BlockSpec(memo...]
    ppermute x13 -> x12, starting transfers between devices: 22.8 us -> 21.5 us  [hop(): return lax.ppermute(array, 'mb', pairs)]
  transfers between devices with their start and end apart: 28 -> 27, of which waited for: 12 -> 9; matrix products, arithmetic and copies ran while one was open for 1% -> 1% of each run, Pallas kernels for 36% -> 34%
where the time goes in v3:
time: 169 us; the launch traced here: 166 us
  Pallas kernels  63.8 us (38%)
  waiting for transfers between devices  51.9 us (31%)
  starting transfers between devices  39.2 us (23%)
  local copies, waits for them, and re-layouts  10.1 us (6%)
    pallas_call x24, Pallas kernels, call(): pl.pallas_call(without_waits, out_shape=outs, in_specs=[pl.BlockSpec(memo...  63.8 us
    ppermute x12, waiting for transfers between devices, hop(): return lax.ppermute(array, 'mb', pairs)  31.6 us
    ppermute x12, starting transfers between devices, hop(): return lax.ppermute(array, 'mb', pairs)  21.5 us
    ppermute x4, waiting for transfers between devices, along(): lax.ppermute(array, 'ma', [(i, (i + by) % row_count) for i in range(row_c...  15.9 us
    unnamed x57, local copies, waits for them, and re-layouts  9.6 us
    ppermute x3, starting transfers between devices, turn_line(): lax.ppermute(array, 'mb', [(i, (i + 2 * by) % peer_count) for i in range(...  6.94 us
    ppermute x8, starting transfers between devices, sibling_of(): lax.ppermute(array, 'mb', [(2 * i + c, 2 * i + 1 - c) for i in of_chips f...  6.01 us
    ppermute x4, starting transfers between devices, along(): lax.ppermute(array, 'ma', [(i, (i + by) % row_count) for i in range(row_c...  4.73 us
  transfers between devices with their start and end apart: 27, of which 9 were waited for; matrix products, arithmetic and copies ran while one was open for 1% of the time, Pallas kernels for 34%

profile of v3, /device:TPU:0, one launch (start us, length us, event | category | flops | bytes accessed | tf_op | source)
XLA Modules:
  0.0 166.2 jit_solution(2019860060203798983)
XLA Ops:
  4.9 3.0 %collective-permute-start = (s32[8,20]{1,0:T(8,128)S(1)}, s32[8,20]{1,0:T(8,128)S(1)}, u32[]{:S(2)}, u32[]{:S(2)}) collective-permute-start(s32[8,20]{1,0:T(8,128)S(1)} %concatenate.10), channel_id=1, source_target_pairs={{0,2},{1,3},{2,4},{3,5},{4,6},{5,7},{6,0},{7,1},{8,10},{9,11},{10,... | collective-permute-start | bytes 1928 | tf_op jit(solution)/shard_map/ppermute | solution.py:360
  7.9 2.6 %collective-permute-start.1 = (s32[8,20]{1,0:T(8,128)S(1)}, s32[8,20]{1,0:T(8,128)S(1)}, u32[]{:S(2)}, u32[]{:S(2)}) collective-permute-start(s32[8,20]{1,0:T(8,128)S(1)} %concatenate.10), channel_id=1, source_target_pairs={{0,4},{1,5},{2,6},{3,7},{4,0},{5,1},{6,2},{7,3},{8,12},{9,13},{10,... | collective-permute-start | bytes 1928 | tf_op jit(solution)/shard_map/ppermute | solution.py:360
  14.1 4.3 %partial_0_0_all.1.refs_8_ = f32[8,2,128,128]{3,2,1,0:T(8,128)} custom-call(s32[7]{0:T(128)S(1)} %pad_add_fusion.1.refs_0_, s32[32,20]{1,0:T(8,128)S(1)} %pad_add_fusion.refs_1_, f32[2,12]{1,0:T(2,128)S(1)} %copy-done.16, f32[8,2,128,128]{3,2,1,0:T(8,128)} %refs_5_.9, f32[8,2,128,128]{3,2,1,0:T(8,128)S(1)} %collective-permute-done.3.refs_4_.refs_6_, ...), custom_call_target="tpu_custom_call" | custom-call | flops 1 | bytes 1 | tf_op jit(solution)/shard_map/partial_0_0_all/pallas_call | solution.py:304
  18.5 2.6 %collective-permute-start.5 = (f32[8,2,128,128]{3,2,1,0:T(8,128)}, f32[8,2,128,128]{3,2,1,0:T(8,128)}, u32[]{:S(2)}, u32[]{:S(2)}) collective-permute-start(f32[8,2,128,128]{3,2,1,0:T(8,128)} %refs_5_.9), channel_id=1, source_target_pairs={{0,24},{8,0},{16,8},{24,16},{1,25},{9,1},{17,9},{25,17},{2,26},{10... | collective-permute-start | bytes 3145736 | tf_op jit(solution)/shard_map/ppermute | solution.py:357
  21.2 4.3 %partial_0_1_all.1.refs_8_.refs_0_ = f32[8,2,128,128]{3,2,1,0:T(8,128)} custom-call(s32[7]{0:T(128)S(1)} %pad_add_fusion.1.refs_0_, s32[32,20]{1,0:T(8,128)S(1)} %pad_add_fusion.refs_1_, f32[2,12]{1,0:T(2,128)S(1)} %copy-done.16, f32[8,2,128,128]{3,2,1,0:T(8,128)} %refs_5_.9, f32[8,2,128,128]{3,2,1,0:T(8,128)S(1)} %collective-permute-done.3.refs_4_.refs_6_, ...), custom_call_target="tpu_custom_call" | custom-call | flops 1 | bytes 1 | tf_op jit(solution)/shard_map/partial_0_1_all/pallas_call | solution.py:304
  25.5 4.9 %collective-permute-start.7 = (f32[8,2,128,128]{3,2,1,0:T(8,128)}, f32[8,2,128,128]{3,2,1,0:T(8,128)}, u32[]{:S(2)}, u32[]{:S(2)}) collective-permute-start(f32[8,2,128,128]{3,2,1,0:T(8,128)} %partial_0_1_all.1.refs_8_.refs_0_), channel_id=1, source_target_pairs={{0,2},{6,4},{1,3},{7,5},{8,10},{14,12},{9,11},{15,13},{16,18},{22,... | collective-permute-start | bytes 3145736 | tf_op jit(solution)/shard_map/ppermute | solution.py:370
  30.4 3.3 %partial_0_2_all.1.refs_9_.refs_0_ = f32[8,2,128,128]{3,2,1,0:T(8,128)S(1)} custom-call(s32[7]{0:T(128)S(1)} %pad_add_fusion.1.refs_0_, s32[32,20]{1,0:T(8,128)S(1)} %pad_add_fusion.refs_1_, f32[2,12]{1,0:T(2,128)S(1)} %copy-done.16, f32[8,2,128,128]{3,2,1,0:T(8,128)} %refs_5_.9, f32[8,2,128,128]{3,2,1,0:T(8,128)S(1)} %collective-permute-done.3.refs_4_.refs_6_, ...), custom_call_target="tpu_custom_call" | custom-call | flops 1 | bytes 1 | tf_op jit(solution)/shard_map/partial_0_2_all/pallas_call | solution.py:304
  33.8 3.9 %sums_0.1 = (f32[8,2,128,128]{3,2,1,0:T(8,128)S(1)}, f32[8,2,128,128]{3,2,1,0:T(8,128)S(1)}) custom-call(s32[7]{0:T(128)S(1)} %pad_add_fusion.1.refs_0_, s32[32,20]{1,0:T(8,128)S(1)} %pad_add_fusion.refs_1_, f32[2,12]{1,0:T(2,128)S(1)} %copy-done.16, s32[8,18]{1,0:T(8,128)S(1)} %reshape.10.refs_3_, s32[8,12]{1,0:T(8,128)S(1)} %copy-done.17, ...), custom_call_target="tpu_custom_call" | custom-call | flops 1 | bytes 1 | tf_op jit(solution)/shard_map/sums_0/pallas_call | solution.py:304
  40.1 2.4 %collective-permute-done.8.refs_1_.refs_9_ = f32[8,2,128,128]{3,2,1,0:T(8,128)} collective-permute-done((f32[8,2,128,128]{3,2,1,0:T(8,128)}, f32[8,2,128,128]{3,2,1,0:T(8,128)}, u32[]{:S(2)}, u32[]{:S(2)}) %collective-permute-start.8) | collective-permute-done | bytes 1048608 | tf_op jit(solution)/shard_map/ppermute | solution.py:370
  42.5 2.6 %add_0_1_3.1.refs_3_ = f32[8,2,128,128]{3,2,1,0:T(8,128)} custom-call(f32[8,2,128,128]{3,2,1,0:T(8,128)} %partial_0_1_all.1.refs_8_.refs_0_, f32[8,2,128,128]{3,2,1,0:T(8,128)} %collective-permute-done.8.refs_1_.refs_9_, f32[128,128]{1,0:T(8,128)S(1)} %tilt_coupling.1.refs_2_.refs_9_), custom_call_target="tpu_custom_call" | custom-call | flops 1 | bytes 1 | tf_op jit(solution)/shard_map/add_0_1_3/pallas_call | solution.py:304
  46.4 2.9 %tilt_seven.1 = (f32[8,2,128,128]{3,2,1,0:T(8,128)S(1)}, f32[4,2,128,128]{3,2,1,0:T(8,128)}, f32[4,2,128,128]{3,2,1,0:T(8,128)}) custom-call(f32[128,128]{1,0:T(8,128)S(1)} %bitcast.7, f32[128,128]{1,0:T(8,128)S(1)} %copy-done.6, f32[8,2,128,128]{3,2,1,0:T(8,128)S(1)} %copy-done.13, f32[8,2,128,128]{3,2,1,0:T(8,128)} %add_0_1_3.1.refs_3_, ...), custom_call_target="tpu_custom_call" | custom-call | flops 1 | bytes 1 | tf_op jit(solution)/shard_map/tilt_seven/pallas_call | solution.py:304
  49.8 15.9 %collective-permute-done.6.refs_3_.refs_6_ = f32[8,2,128,128]{3,2,1,0:T(8,128)} collective-permute-done((f32[8,2,128,128]{3,2,1,0:T(8,128)}, f32[8,2,128,128]{3,2,1,0:T(8,128)}, u32[]{:S(2)}, u32[]{:S(2)}) %collective-permute-start.6) | collective-permute-done | bytes 1048608 | tf_op jit(solution)/shard_map/ppermute | solution.py:357
  65.7 4.6 %collective-permute-start.12 = (f32[8,2,128,128]{3,2,1,0:T(8,128)S(1)}, f32[8,2,128,128]{3,2,1,0:T(8,128)}, u32[]{:S(2)}, u32[]{:S(2)}) collective-permute-start(f32[8,2,128,128]{3,2,1,0:T(8,128)S(1)} %partial_0_2_all.1.refs_9_.refs_0_), channel_id=1, source_target_pairs={{0,2},{6,4},{1,3},{7,5},{8,10},{14,12},{9,11},{15,13},{16,18},{22,... | collective-permute-start | bytes 3145736 | tf_op jit(solution)/shard_map/ppermute | solution.py:370
  74.0 2.5 %finish_five.1.refs_7_ = f32[8,2,128,128]{3,2,1,0:T(8,128)S(1)} custom-call(s32[8,12]{1,0:T(8,128)S(1)} %copy-done.17, f32[2,12]{1,0:T(2,128)S(1)} %copy-done.16, f32[128,128]{1,0:T(8,128)S(1)} %copy-done.12, f32[8,2,128,128]{3,2,1,0:T(8,128)S(1)} %copy-done.8, f32[8,2,128,128]{3,2,1,0:T(8,128)S(1)} %copy-done.15, ...), custom_call_target="tpu_custom_call" | custom-call | flops 1 | bytes 1 | tf_op jit(solution)/shard_map/finish_five/pallas_call | solution.py:304
  77.2 3.7 %solve_five_ends.1 = (f32[8,2,128,128]{3,2,1,0:T(8,128)S(1)}, f32[4,2,128,128]{3,2,1,0:T(8,128)S(1)}, f32[4,2,128,128]{3,2,1,0:T(8,128)S(1)}) custom-call(s32[7]{0:T(128)S(1)} %pad_add_fusion.1.refs_0_, s32[8,12]{1,0:T(8,128)S(1)} %copy-done.17, f32[12]{0:T(128)S(1)} %copy-done.20, f32[1,128]{1,0:T(1,128)S(1)} %bitcast.14, ...), custom_call_target="tpu_custom_call" | custom-call | flops 1 | bytes 1 | tf_op jit(solution)/shard_map/solve_five_ends/pallas_call | solution.py:304
  80.9 1.9 %collective-permute-start.14 = (f32[4,2,128,128]{3,2,1,0:T(8,128)S(1)}, f32[4,2,128,128]{3,2,1,0:T(8,128)S(1)}, u32[]{:S(2)}, u32[]{:S(2)}) collective-permute-start(f32[4,2,128,128]{3,2,1,0:T(8,128)S(1)} %get-tuple-element.23), channel_id=1, source_target_pairs={{0,1},{1,0},{6,7},{7,6},{8,9},{9,8},{14,15},{15,14},{16,17},{17,16... | collective-permute-start | bytes 1572872 | tf_op jit(solution)/shard_map/ppermute | solution.py:352
  82.8 2.4 %collective-permute-start.15 = (f32[4,2,128,128]{3,2,1,0:T(8,128)S(1)}, f32[4,2,128,128]{3,2,1,0:T(8,128)S(1)}, u32[]{:S(2)}, u32[]{:S(2)}) collective-permute-start(f32[4,2,128,128]{3,2,1,0:T(8,128)S(1)} %get-tuple-element.24), channel_id=1, source_target_pairs={{0,1},{1,0},{6,7},{7,6},{8,9},{9,8},{14,15},{15,14},{16,17},{17,16... | collective-permute-start | bytes 1572872 | tf_op jit(solution)/shard_map/ppermute | solution.py:352
  86.7 3.1 %partial_1_0_ends.1.refs_10_ = f32[8,2,128,128]{3,2,1,0:T(8,128)S(1)} custom-call(s32[7]{0:T(128)S(1)} %pad_add_fusion.1.refs_0_, s32[32,20]{1,0:T(8,128)S(1)} %pad_add_fusion.refs_1_, f32[2,12]{1,0:T(2,128)S(1)} %copy-done.16, f32[8,2,128,128]{3,2,1,0:T(8,128)S(1)} %get-tuple-element.19.refs_2_.refs_3_.refs_5_, ...), custom_call_target="tpu_custom_call" | custom-call | flops 1 | bytes 1 | tf_op jit(solution)/shard_map/partial_1_0_ends/pallas_call | solution.py:304
  91.2 3.9 %partial_1_1_ends.1.refs_10_ = f32[8,2,128,128]{3,2,1,0:T(8,128)} custom-call(s32[7]{0:T(128)S(1)} %pad_add_fusion.1.refs_0_, s32[32,20]{1,0:T(8,128)S(1)} %pad_add_fusion.refs_1_, f32[2,12]{1,0:T(2,128)S(1)} %copy-done.16, f32[8,2,128,128]{3,2,1,0:T(8,128)S(1)} %get-tuple-element.19.refs_2_.refs_3_.refs_5_, ...), custom_call_target="tpu_custom_call" | custom-call | flops 1 | bytes 1 | tf_op jit(solution)/shard_map/partial_1_1_ends/pallas_call | solution.py:304
  95.0 2.3 %collective-permute-start.20 = (f32[8,2,128,128]{3,2,1,0:T(8,128)}, f32[8,2,128,128]{3,2,1,0:T(8,128)}, u32[]{:S(2)}, u32[]{:S(2)}) collective-permute-start(f32[8,2,128,128]{3,2,1,0:T(8,128)} %partial_1_1_ends.1.refs_10_), channel_id=1, source_target_pairs={{0,2},{6,4},{1,3},{7,5},{8,10},{14,12},{9,11},{15,13},{16,18},{22,... | collective-permute-start | bytes 3145736 | tf_op jit(solution)/shard_map/ppermute | solution.py:370
  97.3 3.9 %partial_1_2_ends.1.refs_11_ = f32[8,2,128,128]{3,2,1,0:T(8,128)} custom-call(s32[7]{0:T(128)S(1)} %pad_add_fusion.1.refs_0_, s32[32,20]{1,0:T(8,128)S(1)} %pad_add_fusion.refs_1_, f32[2,12]{1,0:T(2,128)S(1)} %copy-done.16, f32[8,2,128,128]{3,2,1,0:T(8,128)S(1)} %get-tuple-element.19.refs_2_.refs_3_.refs_5_, ...), custom_call_target="tpu_custom_call" | custom-call | flops 1 | bytes 1 | tf_op jit(solution)/shard_map/partial_1_2_ends/pallas_call | solution.py:304
  101.2 1.8 %solve_five_rest.1 = (f32[8,2,128,128]{3,2,1,0:T(8,128)S(1)}, f32[4,2,128,128]{3,2,1,0:T(8,128)S(1)}, f32[4,2,128,128]{3,2,1,0:T(8,128)S(1)}) custom-call(s32[7]{0:T(128)S(1)} %pad_add_fusion.1.refs_0_, s32[8,12]{1,0:T(8,128)S(1)} %copy-done.17, f32[12]{0:T(128)S(1)} %copy-done.20, f32[1,128]{1,0:T(1,128)S(1)} %bitcast.15, ...), custom_call_target="tpu_custom_call" | custom-call | flops 1 | bytes 1 | tf_op jit(solution)/shard_map/solve_five_rest/pallas_call | solution.py:304
  105.0 2.3 %collective-permute-start.23 = (f32[8,2,128,128]{3,2,1,0:T(8,128)}, f32[8,2,128,128]{3,2,1,0:T(8,128)}, u32[]{:S(2)}, u32[]{:S(2)}) collective-permute-start(f32[8,2,128,128]{3,2,1,0:T(8,128)} %partial_1_2_ends.1.refs_11_), channel_id=1, source_target_pairs={{0,2},{6,4},{1,3},{7,5},{8,10},{14,12},{9,11},{15,13},{16,18},{22,... | collective-permute-start | bytes 3145736 | tf_op jit(solution)/shard_map/ppermute | solution.py:370
  107.3 1.9 %partial_1_0_rest.1.refs_10_ = f32[8,2,128,128]{3,2,1,0:T(8,128)} custom-call(s32[7]{0:T(128)S(1)} %pad_add_fusion.1.refs_0_, s32[32,20]{1,0:T(8,128)S(1)} %pad_add_fusion.refs_1_, f32[2,12]{1,0:T(2,128)S(1)} %copy-done.16, f32[8,2,128,128]{3,2,1,0:T(8,128)S(1)} %get-tuple-element.19.refs_2_.refs_3_.refs_5_, ...), custom_call_target="tpu_custom_call" | custom-call | flops 1 | bytes 1 | tf_op jit(solution)/shard_map/partial_1_0_rest/pallas_call | solution.py:304
  111.3 3.3 %collective-permute-done.19.refs_1_ = f32[8,2,128,128]{3,2,1,0:T(8,128)S(1)} collective-permute-done((f32[8,2,128,128]{3,2,1,0:T(8,128)S(1)}, f32[8,2,128,128]{3,2,1,0:T(8,128)S(1)}, u32[]{:S(2)}, u32[]{:S(2)}) %collective-permute-start.19) | collective-permute-done | bytes 1048608 | tf_op jit(solution)/shard_map/ppermute | solution.py:370
  120.4 3.7 %sums_1.1 = (f32[8,2,128,128]{3,2,1,0:T(8,128)S(1)}, f32[8,2,128,128]{3,2,1,0:T(8,128)S(1)}) custom-call(s32[7]{0:T(128)S(1)} %pad_add_fusion.1.refs_0_, s32[32,20]{1,0:T(8,128)S(1)} %pad_add_fusion.refs_1_, f32[2,12]{1,0:T(2,128)S(1)} %copy-done.16, s32[8,18]{1,0:T(8,128)S(1)} %reshape.11.refs_3_, s32[8,12]{1,0:T(8,128)S(1)} %copy-done.18, ...), custom_call_target="tpu_custom_call" | custom-call | flops 1 | bytes 1 | tf_op jit(solution)/shard_map/sums_1/pallas_call | solution.py:304
  124.1 13.1 %collective-permute-done.20.refs_1_ = f32[8,2,128,128]{3,2,1,0:T(8,128)} collective-permute-done((f32[8,2,128,128]{3,2,1,0:T(8,128)}, f32[8,2,128,128]{3,2,1,0:T(8,128)}, u32[]{:S(2)}, u32[]{:S(2)}) %collective-permute-start.20) | collective-permute-done | bytes 1048608 | tf_op jit(solution)/shard_map/ppermute | solution.py:370
  140.1 3.1 %back_five.1.refs_7_ = f32[8,2,128,128]{3,2,1,0:T(8,128)} custom-call(f32[128,128]{1,0:T(8,128)S(1)} %copy-done.6, f32[128,128]{1,0:T(8,128)S(1)} %bitcast.10, f32[8,2,128,128]{3,2,1,0:T(8,128)S(1)} %get-tuple-element.25.refs_6_.refs_8_.refs_2_, f32[6,2,128,128]{3,2,1,0:T(8,128)S(1)} %get-tuple-element.29.refs_3_), custom_call_target="tpu_custom_call" | custom-call | flops 1 | bytes 1 | tf_op jit(solution)/shard_map/back_five/pallas_call | solution.py:304
  144.4 2.2 %finish_six.1.refs_6_ = f32[8,2,128,128]{3,2,1,0:T(8,128)S(1)} custom-call(s32[8,12]{1,0:T(8,128)S(1)} %copy-done.18, f32[2,12]{1,0:T(2,128)S(1)} %copy-done.16, f32[128,128]{1,0:T(8,128)S(1)} %tilt_coupling.1.refs_2_.refs_9_, f32[8,2,128,128]{3,2,1,0:T(8,128)S(1)} %get-tuple-element.28.refs_2_.refs_3_, f32[8,2,128,128]{3,2,1,0:T(8,128)S(1)} %get-tuple-element.30.refs_4_, ...), custom_call_target="tpu_custom_call" | custom-call | flops 1 | bytes 1 | tf_op jit(solution)/shard_map/finish_six/pallas_call | solution.py:304
  146.6 12.8 %collective-permute-done.23.refs_8_ = f32[8,2,128,128]{3,2,1,0:T(8,128)} collective-permute-done((f32[8,2,128,128]{3,2,1,0:T(8,128)}, f32[8,2,128,128]{3,2,1,0:T(8,128)}, u32[]{:S(2)}, u32[]{:S(2)}) %collective-permute-start.23) | collective-permute-done | bytes 1048608 | tf_op jit(solution)/shard_map/ppermute | solution.py:370
  159.4 4.3 %solve_six_0.1.refs_11_ = f32[8,2,128,128]{3,2,1,0:T(8,128)} custom-call(s32[8,12]{1,0:T(8,128)S(1)} %copy-done.18, f32[12]{0:T(128)S(1)} %copy-done.20, f32[1,128]{1,0:T(1,128)S(1)} %bitcast.16, f32[128,1]{1,0:T(8,128)S(1)} %copy.25.refs_4_.refs_3_, f32[128,128]{1,0:T(8,128)S(1)} %copy-done.6, f32[128,128]{1,0:T(8,128)S(1)} %bitcast.11, ...), custom_call_target="tpu_custom_call" | custom-call | flops 1 | bytes 1 | tf_op jit(solution)/shard_map/solve_six_0/pallas_call | solution.py:304
  163.6 2.6 %solve_six_1.1 = f32[8,2,128,128]{3,2,1,0:T(8,128)} custom-call(s32[8,12]{1,0:T(8,128)S(1)} %copy-done.18, f32[12]{0:T(128)S(1)} %copy-done.20, f32[1,128]{1,0:T(1,128)S(1)} %bitcast.17, f32[128,1]{1,0:T(8,128)S(1)} %copy.25.refs_4_.refs_3_, f32[128,128]{1,0:T(8,128)S(1)} %copy-done.6, f32[128,128]{1,0:T(8,128)S(1)} %bitcast.12, ...), custom_call_target="tpu_custom_call", output_to_operand_aliasing={{}: (11, {})} | custom-call | flops 1 | bytes 1 | tf_op jit(solution)/shard_map/solve_six_1/pallas_call | solution.py:304
  (112 shorter events, 33.3 us)
Async XLA Ops:
  0.6 13.5 %collective-permute-start.3 = (f32[8,2,128,128]{3,2,1,0:T(8,128)}, f32[8,2,128,128]{3,2,1,0:T(8,128)S(1)}, u32[]{:S(2)}, u32[]{:S(2)}) collective-permute-start(f32[8,2,128,128]{3,2,1,0:T(8,128)} %refs_5_.9), channel_id=1, source_target_pairs={{0,1},{1,0},{2,3},{3,2},{4,5},{5,4},{6,7},{7,6},{8,9},{9,8},{10,11... | collective-permute-start | bytes 3145736 | tf_op jit(solution)/shard_map/ppermute | solution.py:352
  1.2 12.9 %collective-permute-start.4 = (f32[8,2,128,128]{3,2,1,0:T(8,128)}, f32[8,2,128,128]{3,2,1,0:T(8,128)S(1)}, u32[]{:S(2)}, u32[]{:S(2)}) collective-permute-start(f32[8,2,128,128]{3,2,1,0:T(8,128)} %refs_7_.7), channel_id=1, source_target_pairs={{0,1},{1,0},{2,3},{3,2},{4,5},{5,4},{6,7},{7,6},{8,9},{9,8},{10,11... | collective-permute-start | bytes 3145736 | tf_op jit(solution)/shard_map/ppermute | solution.py:352
  4.7 9.4 %copy-start.12 = (f32[128,128]{1,0:T(8,128)S(1)}, f32[128,128]{1,0:T(8,128)}, u32[]{:S(2)}) copy-start(f32[128,128]{1,0:T(8,128)} %refs_2_.22) | copy-start | bytes 196612
  4.9 7.0 %collective-permute-start = (s32[8,20]{1,0:T(8,128)S(1)}, s32[8,20]{1,0:T(8,128)S(1)}, u32[]{:S(2)}, u32[]{:S(2)}) collective-permute-start(s32[8,20]{1,0:T(8,128)S(1)} %concatenate.10), channel_id=1, source_target_pairs={{0,2},{1,3},{2,4},{3,5},{4,6},{5,7},{6,0},{7,1},{8,10},{9,11},{10,... | collective-permute-start | bytes 1928 | tf_op jit(solution)/shard_map/ppermute | solution.py:360
  7.9 4.5 %collective-permute-start.1 = (s32[8,20]{1,0:T(8,128)S(1)}, s32[8,20]{1,0:T(8,128)S(1)}, u32[]{:S(2)}, u32[]{:S(2)}) collective-permute-start(s32[8,20]{1,0:T(8,128)S(1)} %concatenate.10), channel_id=1, source_target_pairs={{0,4},{1,5},{2,6},{3,7},{4,0},{5,1},{6,2},{7,3},{8,12},{9,13},{10,... | collective-permute-start | bytes 1928 | tf_op jit(solution)/shard_map/ppermute | solution.py:360
  10.5 3.6 %collective-permute-start.2 = (s32[8,20]{1,0:T(8,128)S(1)}, s32[8,20]{1,0:T(8,128)S(1)}, u32[]{:S(2)}, u32[]{:S(2)}) collective-permute-start(s32[8,20]{1,0:T(8,128)S(1)} %concatenate.10), channel_id=1, source_target_pairs={{0,6},{1,7},{2,0},{3,1},{4,2},{5,3},{6,4},{7,5},{8,14},{9,15},{10,... | collective-permute-start | bytes 1928 | tf_op jit(solution)/shard_map/ppermute | solution.py:360
  14.1 7.0 %copy-start.21 = (s32[8,2,9]{2,1,0:T(2,128)S(1)}, s32[8,2,9]{2,1,0:T(2,128)}, u32[]{:S(2)}) copy-start(s32[8,2,9]{2,1,0:T(2,128)} %param.25) | copy-start | bytes 1732
  18.4 24.0 %collective-permute-start.8 = (f32[8,2,128,128]{3,2,1,0:T(8,128)}, f32[8,2,128,128]{3,2,1,0:T(8,128)}, u32[]{:S(2)}, u32[]{:S(2)}) collective-permute-start(f32[8,2,128,128]{3,2,1,0:T(8,128)} %partial_0_0_all.1.refs_8_), channel_id=1, source_target_pairs={{0,2},{6,4},{1,3},{7,5},{4,6},{2,0},{5,7},{3,1},{8,10},{14,12},{9,... | collective-permute-start | bytes 3145736 | tf_op jit(solution)/shard_map/ppermute | solution.py:370
  18.5 27.8 %collective-permute-start.5 = (f32[8,2,128,128]{3,2,1,0:T(8,128)}, f32[8,2,128,128]{3,2,1,0:T(8,128)}, u32[]{:S(2)}, u32[]{:S(2)}) collective-permute-start(f32[8,2,128,128]{3,2,1,0:T(8,128)} %refs_5_.9), channel_id=1, source_target_pairs={{0,24},{8,0},{16,8},{24,16},{1,25},{9,1},{17,9},{25,17},{2,26},{10... | collective-permute-start | bytes 3145736 | tf_op jit(solution)/shard_map/ppermute | solution.py:357
  21.1 44.6 %collective-permute-start.6 = (f32[8,2,128,128]{3,2,1,0:T(8,128)}, f32[8,2,128,128]{3,2,1,0:T(8,128)}, u32[]{:S(2)}, u32[]{:S(2)}) collective-permute-start(f32[8,2,128,128]{3,2,1,0:T(8,128)} %refs_7_.7), channel_id=1, source_target_pairs={{0,8},{8,16},{16,24},{24,0},{1,9},{9,17},{17,25},{25,1},{2,10},{10... | collective-permute-start | bytes 3145736 | tf_op jit(solution)/shard_map/ppermute | solution.py:357
  25.5 8.3 %copy-start.6 = (f32[128,128]{1,0:T(8,128)S(1)}, f32[128,128]{1,0:T(8,128)}, u32[]{:S(2)}) copy-start(f32[128,128]{1,0:T(8,128)} %refs_4_.7) | copy-start | bytes 196612
  25.5 45.0 %collective-permute-start.7 = (f32[8,2,128,128]{3,2,1,0:T(8,128)}, f32[8,2,128,128]{3,2,1,0:T(8,128)}, u32[]{:S(2)}, u32[]{:S(2)}) collective-permute-start(f32[8,2,128,128]{3,2,1,0:T(8,128)} %partial_0_1_all.1.refs_8_.refs_0_), channel_id=1, source_target_pairs={{0,2},{6,4},{1,3},{7,5},{8,10},{14,12},{9,11},{15,13},{16,18},{22,... | collective-permute-start | bytes 3145736 | tf_op jit(solution)/shard_map/ppermute | solution.py:370
  40.1 6.3 %copy-start.13 = (f32[8,2,128,128]{3,2,1,0:T(8,128)S(1)}, f32[8,2,128,128]{3,2,1,0:T(8,128)}, u32[]{:S(2)}) copy-start(f32[8,2,128,128]{3,2,1,0:T(8,128)} %refs_2_.21) | copy-start | bytes 3145732
  45.1 31.5 %collective-permute-start.13 = (f32[8,2,128,128]{3,2,1,0:T(8,128)}, f32[8,2,128,128]{3,2,1,0:T(8,128)}, u32[]{:S(2)}, u32[]{:S(2)}) collective-permute-start(f32[8,2,128,128]{3,2,1,0:T(8,128)} %add_0_1_3.1.refs_3_), channel_id=1, source_target_pairs={{2,6},{4,0},{3,7},{5,1},{10,14},{12,8},{11,15},{13,9},{18,22},{20,... | collective-permute-start | bytes 3145736 | tf_op jit(solution)/shard_map/ppermute | solution.py:370
  49.3 23.9 %collective-permute-start.10 = (f32[4,2,128,128]{3,2,1,0:T(8,128)}, f32[4,2,128,128]{3,2,1,0:T(8,128)S(1)}, u32[]{:S(2)}, u32[]{:S(2)}) collective-permute-start(f32[4,2,128,128]{3,2,1,0:T(8,128)} %get-tuple-element.21), channel_id=1, source_target_pairs={{0,1},{1,0},{2,3},{3,2},{4,5},{5,4},{6,7},{7,6},{8,9},{9,8},{10,11... | collective-permute-start | bytes 1572872 | tf_op jit(solution)/shard_map/ppermute | solution.py:352
  49.3 21.0 %copy-start.19 = (f32[128]{0:T(128)S(1)}, f32[128]{0:T(128)}, u32[]{:S(2)}) copy-start(f32[128]{0:T(128)} %param.21) | copy-start | bytes 1540
  49.3 24.7 %collective-permute-start.9 = (f32[4,2,128,128]{3,2,1,0:T(8,128)}, f32[4,2,128,128]{3,2,1,0:T(8,128)S(1)}, u32[]{:S(2)}, u32[]{:S(2)}) collective-permute-start(f32[4,2,128,128]{3,2,1,0:T(8,128)} %get-tuple-element.20), channel_id=1, source_target_pairs={{0,1},{1,0},{2,3},{3,2},{4,5},{5,4},{6,7},{7,6},{8,9},{9,8},{10,11... | collective-permute-start | bytes 1572872 | tf_op jit(solution)/shard_map/ppermute | solution.py:352
  65.7 25.4 %collective-permute-start.12 = (f32[8,2,128,128]{3,2,1,0:T(8,128)S(1)}, f32[8,2,128,128]{3,2,1,0:T(8,128)}, u32[]{:S(2)}, u32[]{:S(2)}) collective-permute-start(f32[8,2,128,128]{3,2,1,0:T(8,128)S(1)} %partial_0_2_all.1.refs_9_.refs_0_), channel_id=1, source_target_pairs={{0,2},{6,4},{1,3},{7,5},{8,10},{14,12},{9,11},{15,13},{16,18},{22,... | collective-permute-start | bytes 3145736 | tf_op jit(solution)/shard_map/ppermute | solution.py:370
  70.4 30.8 %collective-permute-start.16 = (f32[8,2,128,128]{3,2,1,0:T(8,128)S(1)}, f32[8,2,128,128]{3,2,1,0:T(8,128)S(1)}, u32[]{:S(2)}, u32[]{:S(2)}) collective-permute-start(f32[8,2,128,128]{3,2,1,0:T(8,128)S(1)} %get-tuple-element.19.refs_2_.refs_3_.refs_5_), channel_id=1, source_target_pairs={{0,24},{8,0},{16,8},{24,16},{1,25},{9,1},{17,9},{25,17},{2,26},{10... | collective-permute-start | bytes 3145736 | tf_op jit(solution)/shard_map/ppermute | solution.py:357
  73.2 28.0 %collective-permute-start.11 = (f32[8,2,128,128]{3,2,1,0:T(8,128)S(1)}, f32[8,2,128,128]{3,2,1,0:T(8,128)S(1)}, u32[]{:S(2)}, u32[]{:S(2)}) collective-permute-start(f32[8,2,128,128]{3,2,1,0:T(8,128)S(1)} %add_0_1_2.1.refs_7_), channel_id=1, source_target_pairs={{2,4},{4,2},{3,5},{5,3},{10,12},{12,10},{11,13},{13,11},{18,20},{2... | collective-permute-start | bytes 3145736 | tf_op jit(solution)/shard_map/ppermute | solution.py:370
  80.9 4.3 %collective-permute-start.14 = (f32[4,2,128,128]{3,2,1,0:T(8,128)S(1)}, f32[4,2,128,128]{3,2,1,0:T(8,128)S(1)}, u32[]{:S(2)}, u32[]{:S(2)}) collective-permute-start(f32[4,2,128,128]{3,2,1,0:T(8,128)S(1)} %get-tuple-element.23), channel_id=1, source_target_pairs={{0,1},{1,0},{6,7},{7,6},{8,9},{9,8},{14,15},{15,14},{16,17},{17,16... | collective-permute-start | bytes 1572872 | tf_op jit(solution)/shard_map/ppermute | solution.py:352
  82.8 3.9 %collective-permute-start.15 = (f32[4,2,128,128]{3,2,1,0:T(8,128)S(1)}, f32[4,2,128,128]{3,2,1,0:T(8,128)S(1)}, u32[]{:S(2)}, u32[]{:S(2)}) collective-permute-start(f32[4,2,128,128]{3,2,1,0:T(8,128)S(1)} %get-tuple-element.24), channel_id=1, source_target_pairs={{0,1},{1,0},{6,7},{7,6},{8,9},{9,8},{14,15},{15,14},{16,17},{17,16... | collective-permute-start | bytes 1572872 | tf_op jit(solution)/shard_map/ppermute | solution.py:352
  89.8 24.8 %collective-permute-start.19 = (f32[8,2,128,128]{3,2,1,0:T(8,128)S(1)}, f32[8,2,128,128]{3,2,1,0:T(8,128)S(1)}, u32[]{:S(2)}, u32[]{:S(2)}) collective-permute-start(f32[8,2,128,128]{3,2,1,0:T(8,128)S(1)} %partial_1_0_ends.1.refs_10_), channel_id=1, source_target_pairs={{0,2},{6,4},{1,3},{7,5},{8,10},{14,12},{9,11},{15,13},{16,18},{22,... | collective-permute-start | bytes 3145736 | tf_op jit(solution)/shard_map/ppermute | solution.py:370
  95.0 42.2 %collective-permute-start.20 = (f32[8,2,128,128]{3,2,1,0:T(8,128)}, f32[8,2,128,128]{3,2,1,0:T(8,128)}, u32[]{:S(2)}, u32[]{:S(2)}) collective-permute-start(f32[8,2,128,128]{3,2,1,0:T(8,128)} %partial_1_1_ends.1.refs_10_), channel_id=1, source_target_pairs={{0,2},{6,4},{1,3},{7,5},{8,10},{14,12},{9,11},{15,13},{16,18},{22,... | collective-permute-start | bytes 3145736 | tf_op jit(solution)/shard_map/ppermute | solution.py:370
  103.0 2.0 %collective-permute-start.17 = (f32[4,2,128,128]{3,2,1,0:T(8,128)S(1)}, f32[4,2,128,128]{3,2,1,0:T(8,128)S(1)}, u32[]{:S(2)}, u32[]{:S(2)}) collective-permute-start(f32[4,2,128,128]{3,2,1,0:T(8,128)S(1)} %get-tuple-element.26), channel_id=1, source_target_pairs={{0,1},{1,0},{2,3},{3,2},{4,5},{5,4},{6,7},{7,6},{8,9},{9,8},{10,11... | collective-permute-start | bytes 1572872 | tf_op jit(solution)/shard_map/ppermute | solution.py:352
  103.5 3.8 %collective-permute-start.18 = (f32[4,2,128,128]{3,2,1,0:T(8,128)S(1)}, f32[4,2,128,128]{3,2,1,0:T(8,128)S(1)}, u32[]{:S(2)}, u32[]{:S(2)}) collective-permute-start(f32[4,2,128,128]{3,2,1,0:T(8,128)S(1)} %get-tuple-element.27), channel_id=1, source_target_pairs={{0,1},{1,0},{2,3},{3,2},{4,5},{5,4},{6,7},{7,6},{8,9},{9,8},{10,11... | collective-permute-start | bytes 1572872 | tf_op jit(solution)/shard_map/ppermute | solution.py:352
  103.6 35.6 %collective-permute-start.21 = (f32[8,2,128,128]{3,2,1,0:T(8,128)S(1)}, f32[8,2,128,128]{3,2,1,0:T(8,128)}, u32[]{:S(2)}, u32[]{:S(2)}) collective-permute-start(f32[8,2,128,128]{3,2,1,0:T(8,128)S(1)} %get-tuple-element.25.refs_6_.refs_8_.refs_2_), channel_id=1, source_target_pairs={{0,8},{8,16},{16,24},{24,0},{1,9},{9,17},{17,25},{25,1},{2,10},{10... | collective-permute-start | bytes 3145736 | tf_op jit(solution)/shard_map/ppermute | solution.py:357
  105.0 54.3 %collective-permute-start.23 = (f32[8,2,128,128]{3,2,1,0:T(8,128)}, f32[8,2,128,128]{3,2,1,0:T(8,128)}, u32[]{:S(2)}, u32[]{:S(2)}) collective-permute-start(f32[8,2,128,128]{3,2,1,0:T(8,128)} %partial_1_2_ends.1.refs_11_), channel_id=1, source_target_pairs={{0,2},{6,4},{1,3},{7,5},{8,10},{14,12},{9,11},{15,13},{16,18},{22,... | collective-permute-start | bytes 3145736 | tf_op jit(solution)/shard_map/ppermute | solution.py:370
  109.2 50.2 %collective-permute-start.25 = (f32[8,2,128,128]{3,2,1,0:T(8,128)}, f32[8,2,128,128]{3,2,1,0:T(8,128)}, u32[]{:S(2)}, u32[]{:S(2)}) collective-permute-start(f32[8,2,128,128]{3,2,1,0:T(8,128)} %partial_1_0_rest.1.refs_10_), channel_id=1, source_target_pairs={{4,6},{2,0},{5,7},{3,1},{12,14},{10,8},{13,15},{11,9},{20,22},{18,... | collective-permute-start | bytes 3145736 | tf_op jit(solution)/shard_map/ppermute | solution.py:370
  115.7 43.7 %collective-permute-start.24 = (f32[8,2,128,128]{3,2,1,0:T(8,128)}, f32[8,2,128,128]{3,2,1,0:T(8,128)}, u32[]{:S(2)}, u32[]{:S(2)}) collective-permute-start(f32[8,2,128,128]{3,2,1,0:T(8,128)} %add_1_1_3.1.refs_10_), channel_id=1, source_target_pairs={{2,6},{4,0},{3,7},{5,1},{10,14},{12,8},{11,15},{13,9},{18,22},{20,... | collective-permute-start | bytes 3145736 | tf_op jit(solution)/shard_map/ppermute | solution.py:370
  138.5 20.8 %collective-permute-start.26 = (f32[6,2,128,128]{3,2,1,0:T(8,128)S(1)}, f32[6,2,128,128]{3,2,1,0:T(8,128)S(1)}, u32[]{:S(2)}, u32[]{:S(2)}) collective-permute-start(f32[6,2,128,128]{3,2,1,0:T(8,128)S(1)} %get-tuple-element.29.refs_3_), channel_id=1, source_target_pairs={{2,4},{4,2},{3,5},{5,3},{10,12},{12,10},{11,13},{13,11},{18,20},{2... | collective-permute-start | bytes 2359304 | tf_op jit(solution)/shard_map/ppermute | solution.py:370
  139.3 24.4 %collective-permute-start.22 = (f32[2,2,128,128]{3,2,1,0:T(8,128)S(1)}, f32[2,2,128,128]{3,2,1,0:T(8,128)S(1)}, u32[]{:S(2)}, u32[]{:S(2)}) collective-permute-start(f32[2,2,128,128]{3,2,1,0:T(8,128)S(1)} %get-tuple-element.31), channel_id=1, source_target_pairs={{2,4},{4,2},{3,5},{5,3},{10,12},{12,10},{11,13},{13,11},{18,20},{2... | collective-permute-start | bytes 786440 | tf_op jit(solution)/shard_map/ppermute | solution.py:370
  (21 other events, 41.6 us)

commit v4 on v3

--- a/solution.py
+++ b/solution.py
@@ -472,7 +472,7 @@
         )
         return got[0], got[1:]
 
-    last_cuts = [rows - rows // 4, rows // 4]
+    last_cuts = [per] * HALVES
 
     def solve_six(own, last, number, previous):
         cut = last_cuts[number]
@@ -559,8 +559,8 @@
     for slot in slots:
         from_ends(slot, moving_five[goals[-1]] if slot == 1 else [])
     last = [moving_five[g] for g in goals[1:]]
-    cuts = [4, 4]
-    eigen_five, pieces = solve_five(own_five, last, "rest", [ends_five], cuts, [raised_six])
+    halves = [per] * HALVES
+    eigen_five, pieces = solve_five(own_five, last, "rest", [ends_five], halves, [raised_six])
     lower_six = (eigen_five, *[sibling_of(piece, every) for piece in pieces])
     lowered_six = along(eigen_five, 1)
     sent_six = {}

time: 169 us -> 169 us (level)
  no operation moved by 1% of the time
where the time goes in v4:
time: 169 us; the launch traced here: 165 us
  Pallas kernels  63.2 us (37%)
  waiting for transfers between devices  51.6 us (31%)
  starting transfers between devices  38.8 us (23%)
  local copies, waits for them, and re-layouts  10.5 us (6%)
    pallas_call x24, Pallas kernels, call(): pl.pallas_call(without_waits, out_shape=outs, in_specs=[pl.BlockSpec(memo...  63.2 us
    ppermute x12, waiting for transfers between devices, hop(): return lax.ppermute(array, 'mb', pairs)  32.3 us
    ppermute x12, starting transfers between devices, hop(): return lax.ppermute(array, 'mb', pairs)  20.6 us
    ppermute x4, waiting for transfers between devices, along(): lax.ppermute(array, 'ma', [(i, (i + by) % row_count) for i in range(row_c...  15.6 us
    unnamed x57, local copies, waits for them, and re-layouts  9.96 us
    ppermute x3, starting transfers between devices, turn_line(): lax.ppermute(array, 'mb', [(i, (i + 2 * by) % peer_count) for i in range(...  6.94 us
    ppermute x8, starting transfers between devices, sibling_of(): lax.ppermute(array, 'mb', [(2 * i + c, 2 * i + 1 - c) for i in of_chips f...  5.95 us
    ppermute x4, starting transfers between devices, along(): lax.ppermute(array, 'ma', [(i, (i + by) % row_count) for i in range(row_c...  5.41 us
  transfers between devices with their start and end apart: 27, of which 9 were waited for; matrix products, arithmetic and copies ran while one was open for 1% of the time, Pallas kernels for 34%

profile of v4, /device:TPU:0, one launch (start us, length us, event | category | flops | bytes accessed | tf_op | source)
XLA Modules:
  0.0 165.4 jit_solution(10207157044211322110)
XLA Ops:
  4.9 3.0 %collective-permute-start = (s32[8,20]{1,0:T(8,128)S(1)}, s32[8,20]{1,0:T(8,128)S(1)}, u32[]{:S(2)}, u32[]{:S(2)}) collective-permute-start(s32[8,20]{1,0:T(8,128)S(1)} %concatenate.10), channel_id=1, source_target_pairs={{0,2},{1,3},{2,4},{3,5},{4,6},{5,7},{6,0},{7,1},{8,10},{9,11},{10,... | collective-permute-start | bytes 1928 | tf_op jit(solution)/shard_map/ppermute | solution.py:360
  7.9 2.6 %collective-permute-start.1 = (s32[8,20]{1,0:T(8,128)S(1)}, s32[8,20]{1,0:T(8,128)S(1)}, u32[]{:S(2)}, u32[]{:S(2)}) collective-permute-start(s32[8,20]{1,0:T(8,128)S(1)} %concatenate.10), channel_id=1, source_target_pairs={{0,4},{1,5},{2,6},{3,7},{4,0},{5,1},{6,2},{7,3},{8,12},{9,13},{10,... | collective-permute-start | bytes 1928 | tf_op jit(solution)/shard_map/ppermute | solution.py:360
  12.4 1.7 %collective-permute-done.2 = s32[8,20]{1,0:T(8,128)S(1)} collective-permute-done((s32[8,20]{1,0:T(8,128)S(1)}, s32[8,20]{1,0:T(8,128)S(1)}, u32[]{:S(2)}, u32[]{:S(2)}) %collective-permute-start.2) | collective-permute-done | bytes 672 | tf_op jit(solution)/shard_map/ppermute | solution.py:360
  14.1 4.4 %partial_0_0_all.1.refs_8_ = f32[8,2,128,128]{3,2,1,0:T(8,128)} custom-call(s32[7]{0:T(128)S(1)} %pad_add_fusion.1.refs_0_, s32[32,20]{1,0:T(8,128)S(1)} %pad_add_fusion.refs_1_, f32[2,12]{1,0:T(2,128)S(1)} %copy-done.16, f32[8,2,128,128]{3,2,1,0:T(8,128)} %refs_5_.9, f32[8,2,128,128]{3,2,1,0:T(8,128)S(1)} %collective-permute-done.3.refs_4_.refs_6_, ...), custom_call_target="tpu_custom_call" | custom-call | flops 1 | bytes 1 | tf_op jit(solution)/shard_map/partial_0_0_all/pallas_call | solution.py:304
  18.5 2.6 %collective-permute-start.5 = (f32[8,2,128,128]{3,2,1,0:T(8,128)}, f32[8,2,128,128]{3,2,1,0:T(8,128)}, u32[]{:S(2)}, u32[]{:S(2)}) collective-permute-start(f32[8,2,128,128]{3,2,1,0:T(8,128)} %refs_5_.9), channel_id=1, source_target_pairs={{0,24},{8,0},{16,8},{24,16},{1,25},{9,1},{17,9},{25,17},{2,26},{10... | collective-permute-start | bytes 3145736 | tf_op jit(solution)/shard_map/ppermute | solution.py:357
  21.3 4.3 %partial_0_1_all.1.refs_8_.refs_0_ = f32[8,2,128,128]{3,2,1,0:T(8,128)} custom-call(s32[7]{0:T(128)S(1)} %pad_add_fusion.1.refs_0_, s32[32,20]{1,0:T(8,128)S(1)} %pad_add_fusion.refs_1_, f32[2,12]{1,0:T(2,128)S(1)} %copy-done.16, f32[8,2,128,128]{3,2,1,0:T(8,128)} %refs_5_.9, f32[8,2,128,128]{3,2,1,0:T(8,128)S(1)} %collective-permute-done.3.refs_4_.refs_6_, ...), custom_call_target="tpu_custom_call" | custom-call | flops 1 | bytes 1 | tf_op jit(solution)/shard_map/partial_0_1_all/pallas_call | solution.py:304
  25.6 4.9 %collective-permute-start.7 = (f32[8,2,128,128]{3,2,1,0:T(8,128)}, f32[8,2,128,128]{3,2,1,0:T(8,128)}, u32[]{:S(2)}, u32[]{:S(2)}) collective-permute-start(f32[8,2,128,128]{3,2,1,0:T(8,128)} %partial_0_1_all.1.refs_8_.refs_0_), channel_id=1, source_target_pairs={{0,2},{6,4},{1,3},{7,5},{8,10},{14,12},{9,11},{15,13},{16,18},{22,... | collective-permute-start | bytes 3145736 | tf_op jit(solution)/shard_map/ppermute | solution.py:370
  30.4 3.4 %partial_0_2_all.1.refs_9_.refs_0_ = f32[8,2,128,128]{3,2,1,0:T(8,128)S(1)} custom-call(s32[7]{0:T(128)S(1)} %pad_add_fusion.1.refs_0_, s32[32,20]{1,0:T(8,128)S(1)} %pad_add_fusion.refs_1_, f32[2,12]{1,0:T(2,128)S(1)} %copy-done.16, f32[8,2,128,128]{3,2,1,0:T(8,128)} %refs_5_.9, f32[8,2,128,128]{3,2,1,0:T(8,128)S(1)} %collective-permute-done.3.refs_4_.refs_6_, ...), custom_call_target="tpu_custom_call" | custom-call | flops 1 | bytes 1 | tf_op jit(solution)/shard_map/partial_0_2_all/pallas_call | solution.py:304
  33.9 3.9 %sums_0.1 = (f32[8,2,128,128]{3,2,1,0:T(8,128)S(1)}, f32[8,2,128,128]{3,2,1,0:T(8,128)S(1)}) custom-call(s32[7]{0:T(128)S(1)} %pad_add_fusion.1.refs_0_, s32[32,20]{1,0:T(8,128)S(1)} %pad_add_fusion.refs_1_, f32[2,12]{1,0:T(2,128)S(1)} %copy-done.16, s32[8,18]{1,0:T(8,128)S(1)} %reshape.10.refs_3_, s32[8,12]{1,0:T(8,128)S(1)} %copy-done.17, ...), custom_call_target="tpu_custom_call" | custom-call | flops 1 | bytes 1 | tf_op jit(solution)/shard_map/sums_0/pallas_call | solution.py:304
  40.2 2.3 %collective-permute-done.8.refs_1_.refs_9_ = f32[8,2,128,128]{3,2,1,0:T(8,128)} collective-permute-done((f32[8,2,128,128]{3,2,1,0:T(8,128)}, f32[8,2,128,128]{3,2,1,0:T(8,128)}, u32[]{:S(2)}, u32[]{:S(2)}) %collective-permute-start.8) | collective-permute-done | bytes 1048608 | tf_op jit(solution)/shard_map/ppermute | solution.py:370
  42.5 2.6 %add_0_1_3.1.refs_3_ = f32[8,2,128,128]{3,2,1,0:T(8,128)} custom-call(f32[8,2,128,128]{3,2,1,0:T(8,128)} %partial_0_1_all.1.refs_8_.refs_0_, f32[8,2,128,128]{3,2,1,0:T(8,128)} %collective-permute-done.8.refs_1_.refs_9_, f32[128,128]{1,0:T(8,128)S(1)} %tilt_coupling.1.refs_2_.refs_9_), custom_call_target="tpu_custom_call" | custom-call | flops 1 | bytes 1 | tf_op jit(solution)/shard_map/add_0_1_3/pallas_call | solution.py:304
  46.4 3.0 %tilt_seven.1 = (f32[8,2,128,128]{3,2,1,0:T(8,128)S(1)}, f32[4,2,128,128]{3,2,1,0:T(8,128)}, f32[4,2,128,128]{3,2,1,0:T(8,128)}) custom-call(f32[128,128]{1,0:T(8,128)S(1)} %bitcast.7, f32[128,128]{1,0:T(8,128)S(1)} %copy-done.6, f32[8,2,128,128]{3,2,1,0:T(8,128)S(1)} %copy-done.13, f32[8,2,128,128]{3,2,1,0:T(8,128)} %add_0_1_3.1.refs_3_, ...), custom_call_target="tpu_custom_call" | custom-call | flops 1 | bytes 1 | tf_op jit(solution)/shard_map/tilt_seven/pallas_call | solution.py:304
  50.2 15.6 %collective-permute-done.6.refs_3_.refs_6_ = f32[8,2,128,128]{3,2,1,0:T(8,128)} collective-permute-done((f32[8,2,128,128]{3,2,1,0:T(8,128)}, f32[8,2,128,128]{3,2,1,0:T(8,128)}, u32[]{:S(2)}, u32[]{:S(2)}) %collective-permute-start.6) | collective-permute-done | bytes 1048608 | tf_op jit(solution)/shard_map/ppermute | solution.py:357
  65.7 3.7 %collective-permute-start.12 = (f32[8,2,128,128]{3,2,1,0:T(8,128)S(1)}, f32[8,2,128,128]{3,2,1,0:T(8,128)S(1)}, u32[]{:S(2)}, u32[]{:S(2)}) collective-permute-start(f32[8,2,128,128]{3,2,1,0:T(8,128)S(1)} %partial_0_2_all.1.refs_9_.refs_0_), channel_id=1, source_target_pairs={{0,2},{6,4},{1,3},{7,5},{8,10},{14,12},{9,11},{15,13},{16,18},{22,... | collective-permute-start | bytes 3145736 | tf_op jit(solution)/shard_map/ppermute | solution.py:370
  73.1 2.5 %finish_five.1.refs_7_ = f32[8,2,128,128]{3,2,1,0:T(8,128)S(1)} custom-call(s32[8,12]{1,0:T(8,128)S(1)} %copy-done.17, f32[2,12]{1,0:T(2,128)S(1)} %copy-done.16, f32[128,128]{1,0:T(8,128)S(1)} %copy-done.12, f32[8,2,128,128]{3,2,1,0:T(8,128)S(1)} %copy-done.8, f32[8,2,128,128]{3,2,1,0:T(8,128)S(1)} %copy-done.15, ...), custom_call_target="tpu_custom_call" | custom-call | flops 1 | bytes 1 | tf_op jit(solution)/shard_map/finish_five/pallas_call | solution.py:304
  76.2 3.7 %solve_five_ends.1 = (f32[8,2,128,128]{3,2,1,0:T(8,128)S(1)}, f32[4,2,128,128]{3,2,1,0:T(8,128)S(1)}, f32[4,2,128,128]{3,2,1,0:T(8,128)S(1)}) custom-call(s32[7]{0:T(128)S(1)} %pad_add_fusion.1.refs_0_, s32[8,12]{1,0:T(8,128)S(1)} %copy-done.17, f32[12]{0:T(128)S(1)} %copy-done.20, f32[1,128]{1,0:T(1,128)S(1)} %bitcast.14, ...), custom_call_target="tpu_custom_call" | custom-call | flops 1 | bytes 1 | tf_op jit(solution)/shard_map/solve_five_ends/pallas_call | solution.py:304
  79.9 1.9 %collective-permute-start.14 = (f32[4,2,128,128]{3,2,1,0:T(8,128)S(1)}, f32[4,2,128,128]{3,2,1,0:T(8,128)S(1)}, u32[]{:S(2)}, u32[]{:S(2)}) collective-permute-start(f32[4,2,128,128]{3,2,1,0:T(8,128)S(1)} %get-tuple-element.23), channel_id=1, source_target_pairs={{0,1},{1,0},{6,7},{7,6},{8,9},{9,8},{14,15},{15,14},{16,17},{17,16... | collective-permute-start | bytes 1572872 | tf_op jit(solution)/shard_map/ppermute | solution.py:352
  81.8 2.4 %collective-permute-start.15 = (f32[4,2,128,128]{3,2,1,0:T(8,128)S(1)}, f32[4,2,128,128]{3,2,1,0:T(8,128)S(1)}, u32[]{:S(2)}, u32[]{:S(2)}) collective-permute-start(f32[4,2,128,128]{3,2,1,0:T(8,128)S(1)} %get-tuple-element.24), channel_id=1, source_target_pairs={{0,1},{1,0},{6,7},{7,6},{8,9},{9,8},{14,15},{15,14},{16,17},{17,16... | collective-permute-start | bytes 1572872 | tf_op jit(solution)/shard_map/ppermute | solution.py:352
  85.7 3.1 %partial_1_0_ends.1.refs_10_ = f32[8,2,128,128]{3,2,1,0:T(8,128)S(1)} custom-call(s32[7]{0:T(128)S(1)} %pad_add_fusion.1.refs_0_, s32[32,20]{1,0:T(8,128)S(1)} %pad_add_fusion.refs_1_, f32[2,12]{1,0:T(2,128)S(1)} %copy-done.16, f32[8,2,128,128]{3,2,1,0:T(8,128)S(1)} %get-tuple-element.19.refs_2_.refs_3_.refs_5_, ...), custom_call_target="tpu_custom_call" | custom-call | flops 1 | bytes 1 | tf_op jit(solution)/shard_map/partial_1_0_ends/pallas_call | solution.py:304
  90.3 3.9 %partial_1_1_ends.1.refs_10_ = f32[8,2,128,128]{3,2,1,0:T(8,128)} custom-call(s32[7]{0:T(128)S(1)} %pad_add_fusion.1.refs_0_, s32[32,20]{1,0:T(8,128)S(1)} %pad_add_fusion.refs_1_, f32[2,12]{1,0:T(2,128)S(1)} %copy-done.16, f32[8,2,128,128]{3,2,1,0:T(8,128)S(1)} %get-tuple-element.19.refs_2_.refs_3_.refs_5_, ...), custom_call_target="tpu_custom_call" | custom-call | flops 1 | bytes 1 | tf_op jit(solution)/shard_map/partial_1_1_ends/pallas_call | solution.py:304
  94.2 2.3 %collective-permute-start.20 = (f32[8,2,128,128]{3,2,1,0:T(8,128)}, f32[8,2,128,128]{3,2,1,0:T(8,128)}, u32[]{:S(2)}, u32[]{:S(2)}) collective-permute-start(f32[8,2,128,128]{3,2,1,0:T(8,128)} %partial_1_1_ends.1.refs_10_), channel_id=1, source_target_pairs={{0,2},{6,4},{1,3},{7,5},{8,10},{14,12},{9,11},{15,13},{16,18},{22,... | collective-permute-start | bytes 3145736 | tf_op jit(solution)/shard_map/ppermute | solution.py:370
  96.5 3.9 %partial_1_2_ends.1.refs_11_ = f32[8,2,128,128]{3,2,1,0:T(8,128)} custom-call(s32[7]{0:T(128)S(1)} %pad_add_fusion.1.refs_0_, s32[32,20]{1,0:T(8,128)S(1)} %pad_add_fusion.refs_1_, f32[2,12]{1,0:T(2,128)S(1)} %copy-done.16, f32[8,2,128,128]{3,2,1,0:T(8,128)S(1)} %get-tuple-element.19.refs_2_.refs_3_.refs_5_, ...), custom_call_target="tpu_custom_call" | custom-call | flops 1 | bytes 1 | tf_op jit(solution)/shard_map/partial_1_2_ends/pallas_call | solution.py:304
  103.3 2.3 %collective-permute-start.23 = (f32[8,2,128,128]{3,2,1,0:T(8,128)}, f32[8,2,128,128]{3,2,1,0:T(8,128)}, u32[]{:S(2)}, u32[]{:S(2)}) collective-permute-start(f32[8,2,128,128]{3,2,1,0:T(8,128)} %partial_1_2_ends.1.refs_11_), channel_id=1, source_target_pairs={{0,2},{6,4},{1,3},{7,5},{8,10},{14,12},{9,11},{15,13},{16,18},{22,... | collective-permute-start | bytes 3145736 | tf_op jit(solution)/shard_map/ppermute | solution.py:370
  105.6 1.9 %partial_1_0_rest.1.refs_10_ = f32[8,2,128,128]{3,2,1,0:T(8,128)} custom-call(s32[7]{0:T(128)S(1)} %pad_add_fusion.1.refs_0_, s32[32,20]{1,0:T(8,128)S(1)} %pad_add_fusion.refs_1_, f32[2,12]{1,0:T(2,128)S(1)} %copy-done.16, f32[8,2,128,128]{3,2,1,0:T(8,128)S(1)} %get-tuple-element.19.refs_2_.refs_3_.refs_5_, ...), custom_call_target="tpu_custom_call" | custom-call | flops 1 | bytes 1 | tf_op jit(solution)/shard_map/partial_1_0_rest/pallas_call | solution.py:304
  109.6 4.1 %collective-permute-done.19.refs_1_ = f32[8,2,128,128]{3,2,1,0:T(8,128)S(1)} collective-permute-done((f32[8,2,128,128]{3,2,1,0:T(8,128)S(1)}, f32[8,2,128,128]{3,2,1,0:T(8,128)S(1)}, u32[]{:S(2)}, u32[]{:S(2)}) %collective-permute-start.19) | collective-permute-done | bytes 1048608 | tf_op jit(solution)/shard_map/ppermute | solution.py:370
  119.5 3.7 %sums_1.1 = (f32[8,2,128,128]{3,2,1,0:T(8,128)S(1)}, f32[8,2,128,128]{3,2,1,0:T(8,128)S(1)}) custom-call(s32[7]{0:T(128)S(1)} %pad_add_fusion.1.refs_0_, s32[32,20]{1,0:T(8,128)S(1)} %pad_add_fusion.refs_1_, f32[2,12]{1,0:T(2,128)S(1)} %copy-done.16, s32[8,18]{1,0:T(8,128)S(1)} %reshape.11.refs_3_, s32[8,12]{1,0:T(8,128)S(1)} %copy-done.18, ...), custom_call_target="tpu_custom_call" | custom-call | flops 1 | bytes 1 | tf_op jit(solution)/shard_map/sums_1/pallas_call | solution.py:304
  123.2 13.1 %collective-permute-done.20.refs_1_ = f32[8,2,128,128]{3,2,1,0:T(8,128)} collective-permute-done((f32[8,2,128,128]{3,2,1,0:T(8,128)}, f32[8,2,128,128]{3,2,1,0:T(8,128)}, u32[]{:S(2)}, u32[]{:S(2)}) %collective-permute-start.20) | collective-permute-done | bytes 1048608 | tf_op jit(solution)/shard_map/ppermute | solution.py:370
  139.2 3.1 %back_five.1.refs_7_ = f32[8,2,128,128]{3,2,1,0:T(8,128)} custom-call(f32[128,128]{1,0:T(8,128)S(1)} %copy-done.6, f32[128,128]{1,0:T(8,128)S(1)} %bitcast.10, f32[8,2,128,128]{3,2,1,0:T(8,128)S(1)} %get-tuple-element.25.refs_6_.refs_8_.refs_2_, f32[4,2,128,128]{3,2,1,0:T(8,128)S(1)} %get-tuple-element.29.refs_3_), custom_call_target="tpu_custom_call" | custom-call | flops 1 | bytes 1 | tf_op jit(solution)/shard_map/back_five/pallas_call | solution.py:304
  143.5 2.2 %finish_six.1.refs_6_ = f32[8,2,128,128]{3,2,1,0:T(8,128)S(1)} custom-call(s32[8,12]{1,0:T(8,128)S(1)} %copy-done.18, f32[2,12]{1,0:T(2,128)S(1)} %copy-done.16, f32[128,128]{1,0:T(8,128)S(1)} %tilt_coupling.1.refs_2_.refs_9_, f32[8,2,128,128]{3,2,1,0:T(8,128)S(1)} %get-tuple-element.28.refs_2_.refs_3_, f32[8,2,128,128]{3,2,1,0:T(8,128)S(1)} %get-tuple-element.30.refs_4_, ...), custom_call_target="tpu_custom_call" | custom-call | flops 1 | bytes 1 | tf_op jit(solution)/shard_map/finish_six/pallas_call | solution.py:304
  145.7 12.7 %collective-permute-done.23.refs_8_ = f32[8,2,128,128]{3,2,1,0:T(8,128)} collective-permute-done((f32[8,2,128,128]{3,2,1,0:T(8,128)}, f32[8,2,128,128]{3,2,1,0:T(8,128)}, u32[]{:S(2)}, u32[]{:S(2)}) %collective-permute-start.23) | collective-permute-done | bytes 1048608 | tf_op jit(solution)/shard_map/ppermute | solution.py:370
  158.5 3.5 %solve_six_0.1.refs_11_ = f32[8,2,128,128]{3,2,1,0:T(8,128)} custom-call(s32[8,12]{1,0:T(8,128)S(1)} %copy-done.18, f32[12]{0:T(128)S(1)} %copy-done.20, f32[1,128]{1,0:T(1,128)S(1)} %bitcast.16, f32[128,1]{1,0:T(8,128)S(1)} %copy.25.refs_4_.refs_3_, f32[128,128]{1,0:T(8,128)S(1)} %copy-done.6, f32[128,128]{1,0:T(8,128)S(1)} %bitcast.11, ...), custom_call_target="tpu_custom_call" | custom-call | flops 1 | bytes 1 | tf_op jit(solution)/shard_map/solve_six_0/pallas_call | solution.py:304
  161.9 3.5 %solve_six_1.1 = f32[8,2,128,128]{3,2,1,0:T(8,128)} custom-call(s32[8,12]{1,0:T(8,128)S(1)} %copy-done.18, f32[12]{0:T(128)S(1)} %copy-done.20, f32[1,128]{1,0:T(1,128)S(1)} %bitcast.17, f32[128,1]{1,0:T(8,128)S(1)} %copy.25.refs_4_.refs_3_, f32[128,128]{1,0:T(8,128)S(1)} %copy-done.6, f32[128,128]{1,0:T(8,128)S(1)} %bitcast.12, ...), custom_call_target="tpu_custom_call", output_to_operand_aliasing={{}: (11, {})} | custom-call | flops 1 | bytes 1 | tf_op jit(solution)/shard_map/solve_six_1/pallas_call | solution.py:304
  (112 shorter events, 32.7 us)
Async XLA Ops:
  0.6 13.5 %collective-permute-start.3 = (f32[8,2,128,128]{3,2,1,0:T(8,128)}, f32[8,2,128,128]{3,2,1,0:T(8,128)S(1)}, u32[]{:S(2)}, u32[]{:S(2)}) collective-permute-start(f32[8,2,128,128]{3,2,1,0:T(8,128)} %refs_5_.9), channel_id=1, source_target_pairs={{0,1},{1,0},{2,3},{3,2},{4,5},{5,4},{6,7},{7,6},{8,9},{9,8},{10,11... | collective-permute-start | bytes 3145736 | tf_op jit(solution)/shard_map/ppermute | solution.py:352
  1.2 12.9 %collective-permute-start.4 = (f32[8,2,128,128]{3,2,1,0:T(8,128)}, f32[8,2,128,128]{3,2,1,0:T(8,128)S(1)}, u32[]{:S(2)}, u32[]{:S(2)}) collective-permute-start(f32[8,2,128,128]{3,2,1,0:T(8,128)} %refs_7_.7), channel_id=1, source_target_pairs={{0,1},{1,0},{2,3},{3,2},{4,5},{5,4},{6,7},{7,6},{8,9},{9,8},{10,11... | collective-permute-start | bytes 3145736 | tf_op jit(solution)/shard_map/ppermute | solution.py:352
  4.7 9.4 %copy-start.12 = (f32[128,128]{1,0:T(8,128)S(1)}, f32[128,128]{1,0:T(8,128)}, u32[]{:S(2)}) copy-start(f32[128,128]{1,0:T(8,128)} %refs_2_.22) | copy-start | bytes 196612
  4.9 7.0 %collective-permute-start = (s32[8,20]{1,0:T(8,128)S(1)}, s32[8,20]{1,0:T(8,128)S(1)}, u32[]{:S(2)}, u32[]{:S(2)}) collective-permute-start(s32[8,20]{1,0:T(8,128)S(1)} %concatenate.10), channel_id=1, source_target_pairs={{0,2},{1,3},{2,4},{3,5},{4,6},{5,7},{6,0},{7,1},{8,10},{9,11},{10,... | collective-permute-start | bytes 1928 | tf_op jit(solution)/shard_map/ppermute | solution.py:360
  7.9 4.5 %collective-permute-start.1 = (s32[8,20]{1,0:T(8,128)S(1)}, s32[8,20]{1,0:T(8,128)S(1)}, u32[]{:S(2)}, u32[]{:S(2)}) collective-permute-start(s32[8,20]{1,0:T(8,128)S(1)} %concatenate.10), channel_id=1, source_target_pairs={{0,4},{1,5},{2,6},{3,7},{4,0},{5,1},{6,2},{7,3},{8,12},{9,13},{10,... | collective-permute-start | bytes 1928 | tf_op jit(solution)/shard_map/ppermute | solution.py:360
  10.5 3.6 %collective-permute-start.2 = (s32[8,20]{1,0:T(8,128)S(1)}, s32[8,20]{1,0:T(8,128)S(1)}, u32[]{:S(2)}, u32[]{:S(2)}) collective-permute-start(s32[8,20]{1,0:T(8,128)S(1)} %concatenate.10), channel_id=1, source_target_pairs={{0,6},{1,7},{2,0},{3,1},{4,2},{5,3},{6,4},{7,5},{8,14},{9,15},{10,... | collective-permute-start | bytes 1928 | tf_op jit(solution)/shard_map/ppermute | solution.py:360
  14.1 7.1 %copy-start.21 = (s32[8,2,9]{2,1,0:T(2,128)S(1)}, s32[8,2,9]{2,1,0:T(2,128)}, u32[]{:S(2)}) copy-start(s32[8,2,9]{2,1,0:T(2,128)} %param.25) | copy-start | bytes 1732
  18.5 24.0 %collective-permute-start.8 = (f32[8,2,128,128]{3,2,1,0:T(8,128)}, f32[8,2,128,128]{3,2,1,0:T(8,128)}, u32[]{:S(2)}, u32[]{:S(2)}) collective-permute-start(f32[8,2,128,128]{3,2,1,0:T(8,128)} %partial_0_0_all.1.refs_8_), channel_id=1, source_target_pairs={{0,2},{6,4},{1,3},{7,5},{4,6},{2,0},{5,7},{3,1},{8,10},{14,12},{9,... | collective-permute-start | bytes 3145736 | tf_op jit(solution)/shard_map/ppermute | solution.py:370
  18.5 27.8 %collective-permute-start.5 = (f32[8,2,128,128]{3,2,1,0:T(8,128)}, f32[8,2,128,128]{3,2,1,0:T(8,128)}, u32[]{:S(2)}, u32[]{:S(2)}) collective-permute-start(f32[8,2,128,128]{3,2,1,0:T(8,128)} %refs_5_.9), channel_id=1, source_target_pairs={{0,24},{8,0},{16,8},{24,16},{1,25},{9,1},{17,9},{25,17},{2,26},{10... | collective-permute-start | bytes 3145736 | tf_op jit(solution)/shard_map/ppermute | solution.py:357
  21.2 44.6 %collective-permute-start.6 = (f32[8,2,128,128]{3,2,1,0:T(8,128)}, f32[8,2,128,128]{3,2,1,0:T(8,128)}, u32[]{:S(2)}, u32[]{:S(2)}) collective-permute-start(f32[8,2,128,128]{3,2,1,0:T(8,128)} %refs_7_.7), channel_id=1, source_target_pairs={{0,8},{8,16},{16,24},{24,0},{1,9},{9,17},{17,25},{25,1},{2,10},{10... | collective-permute-start | bytes 3145736 | tf_op jit(solution)/shard_map/ppermute | solution.py:357
  25.6 8.2 %copy-start.6 = (f32[128,128]{1,0:T(8,128)S(1)}, f32[128,128]{1,0:T(8,128)}, u32[]{:S(2)}) copy-start(f32[128,128]{1,0:T(8,128)} %refs_4_.7) | copy-start | bytes 196612
  25.6 43.9 %collective-permute-start.7 = (f32[8,2,128,128]{3,2,1,0:T(8,128)}, f32[8,2,128,128]{3,2,1,0:T(8,128)}, u32[]{:S(2)}, u32[]{:S(2)}) collective-permute-start(f32[8,2,128,128]{3,2,1,0:T(8,128)} %partial_0_1_all.1.refs_8_.refs_0_), channel_id=1, source_target_pairs={{0,2},{6,4},{1,3},{7,5},{8,10},{14,12},{9,11},{15,13},{16,18},{22,... | collective-permute-start | bytes 3145736 | tf_op jit(solution)/shard_map/ppermute | solution.py:370
  40.2 6.2 %copy-start.13 = (f32[8,2,128,128]{3,2,1,0:T(8,128)S(1)}, f32[8,2,128,128]{3,2,1,0:T(8,128)}, u32[]{:S(2)}) copy-start(f32[8,2,128,128]{3,2,1,0:T(8,128)} %refs_2_.21) | copy-start | bytes 3145732
  45.1 30.5 %collective-permute-start.13 = (f32[8,2,128,128]{3,2,1,0:T(8,128)}, f32[8,2,128,128]{3,2,1,0:T(8,128)}, u32[]{:S(2)}, u32[]{:S(2)}) collective-permute-start(f32[8,2,128,128]{3,2,1,0:T(8,128)} %add_0_1_3.1.refs_3_), channel_id=1, source_target_pairs={{2,6},{4,0},{3,7},{5,1},{10,14},{12,8},{11,15},{13,9},{18,22},{20,... | collective-permute-start | bytes 3145736 | tf_op jit(solution)/shard_map/ppermute | solution.py:370
  49.4 22.9 %collective-permute-start.10 = (f32[4,2,128,128]{3,2,1,0:T(8,128)}, f32[4,2,128,128]{3,2,1,0:T(8,128)S(1)}, u32[]{:S(2)}, u32[]{:S(2)}) collective-permute-start(f32[4,2,128,128]{3,2,1,0:T(8,128)} %get-tuple-element.21), channel_id=1, source_target_pairs={{0,1},{1,0},{2,3},{3,2},{4,5},{5,4},{6,7},{7,6},{8,9},{9,8},{10,11... | collective-permute-start | bytes 1572872 | tf_op jit(solution)/shard_map/ppermute | solution.py:352
  49.4 23.6 %collective-permute-start.9 = (f32[4,2,128,128]{3,2,1,0:T(8,128)}, f32[4,2,128,128]{3,2,1,0:T(8,128)S(1)}, u32[]{:S(2)}, u32[]{:S(2)}) collective-permute-start(f32[4,2,128,128]{3,2,1,0:T(8,128)} %get-tuple-element.20), channel_id=1, source_target_pairs={{0,1},{1,0},{2,3},{3,2},{4,5},{5,4},{6,7},{7,6},{8,9},{9,8},{10,11... | collective-permute-start | bytes 1572872 | tf_op jit(solution)/shard_map/ppermute | solution.py:352
  65.7 24.5 %collective-permute-start.12 = (f32[8,2,128,128]{3,2,1,0:T(8,128)S(1)}, f32[8,2,128,128]{3,2,1,0:T(8,128)S(1)}, u32[]{:S(2)}, u32[]{:S(2)}) collective-permute-start(f32[8,2,128,128]{3,2,1,0:T(8,128)S(1)} %partial_0_2_all.1.refs_9_.refs_0_), channel_id=1, source_target_pairs={{0,2},{6,4},{1,3},{7,5},{8,10},{14,12},{9,11},{15,13},{16,18},{22,... | collective-permute-start | bytes 3145736 | tf_op jit(solution)/shard_map/ppermute | solution.py:370
  69.4 31.0 %collective-permute-start.16 = (f32[8,2,128,128]{3,2,1,0:T(8,128)S(1)}, f32[8,2,128,128]{3,2,1,0:T(8,128)S(1)}, u32[]{:S(2)}, u32[]{:S(2)}) collective-permute-start(f32[8,2,128,128]{3,2,1,0:T(8,128)S(1)} %get-tuple-element.19.refs_2_.refs_3_.refs_5_), channel_id=1, source_target_pairs={{0,24},{8,0},{16,8},{24,16},{1,25},{9,1},{17,9},{25,17},{2,26},{10... | collective-permute-start | bytes 3145736 | tf_op jit(solution)/shard_map/ppermute | solution.py:357
  72.3 28.1 %collective-permute-start.11 = (f32[8,2,128,128]{3,2,1,0:T(8,128)S(1)}, f32[8,2,128,128]{3,2,1,0:T(8,128)S(1)}, u32[]{:S(2)}, u32[]{:S(2)}) collective-permute-start(f32[8,2,128,128]{3,2,1,0:T(8,128)S(1)} %add_0_1_2.1.refs_7_), channel_id=1, source_target_pairs={{2,4},{4,2},{3,5},{5,3},{10,12},{12,10},{11,13},{13,11},{18,20},{2... | collective-permute-start | bytes 3145736 | tf_op jit(solution)/shard_map/ppermute | solution.py:370
  79.9 4.3 %collective-permute-start.14 = (f32[4,2,128,128]{3,2,1,0:T(8,128)S(1)}, f32[4,2,128,128]{3,2,1,0:T(8,128)S(1)}, u32[]{:S(2)}, u32[]{:S(2)}) collective-permute-start(f32[4,2,128,128]{3,2,1,0:T(8,128)S(1)} %get-tuple-element.23), channel_id=1, source_target_pairs={{0,1},{1,0},{6,7},{7,6},{8,9},{9,8},{14,15},{15,14},{16,17},{17,16... | collective-permute-start | bytes 1572872 | tf_op jit(solution)/shard_map/ppermute | solution.py:352
  81.8 3.9 %collective-permute-start.15 = (f32[4,2,128,128]{3,2,1,0:T(8,128)S(1)}, f32[4,2,128,128]{3,2,1,0:T(8,128)S(1)}, u32[]{:S(2)}, u32[]{:S(2)}) collective-permute-start(f32[4,2,128,128]{3,2,1,0:T(8,128)S(1)} %get-tuple-element.24), channel_id=1, source_target_pairs={{0,1},{1,0},{6,7},{7,6},{8,9},{9,8},{14,15},{15,14},{16,17},{17,16... | collective-permute-start | bytes 1572872 | tf_op jit(solution)/shard_map/ppermute | solution.py:352
  88.9 24.8 %collective-permute-start.19 = (f32[8,2,128,128]{3,2,1,0:T(8,128)S(1)}, f32[8,2,128,128]{3,2,1,0:T(8,128)S(1)}, u32[]{:S(2)}, u32[]{:S(2)}) collective-permute-start(f32[8,2,128,128]{3,2,1,0:T(8,128)S(1)} %partial_1_0_ends.1.refs_10_), channel_id=1, source_target_pairs={{0,2},{6,4},{1,3},{7,5},{8,10},{14,12},{9,11},{15,13},{16,18},{22,... | collective-permute-start | bytes 3145736 | tf_op jit(solution)/shard_map/ppermute | solution.py:370
  94.2 42.1 %collective-permute-start.20 = (f32[8,2,128,128]{3,2,1,0:T(8,128)}, f32[8,2,128,128]{3,2,1,0:T(8,128)}, u32[]{:S(2)}, u32[]{:S(2)}) collective-permute-start(f32[8,2,128,128]{3,2,1,0:T(8,128)} %partial_1_1_ends.1.refs_10_), channel_id=1, source_target_pairs={{0,2},{6,4},{1,3},{7,5},{8,10},{14,12},{9,11},{15,13},{16,18},{22,... | collective-permute-start | bytes 3145736 | tf_op jit(solution)/shard_map/ppermute | solution.py:370
  101.4 1.9 %collective-permute-start.17 = (f32[4,2,128,128]{3,2,1,0:T(8,128)S(1)}, f32[4,2,128,128]{3,2,1,0:T(8,128)S(1)}, u32[]{:S(2)}, u32[]{:S(2)}) collective-permute-start(f32[4,2,128,128]{3,2,1,0:T(8,128)S(1)} %get-tuple-element.26), channel_id=1, source_target_pairs={{0,1},{1,0},{2,3},{3,2},{4,5},{5,4},{6,7},{7,6},{8,9},{9,8},{10,11... | collective-permute-start | bytes 1572872 | tf_op jit(solution)/shard_map/ppermute | solution.py:352
  101.8 3.8 %collective-permute-start.18 = (f32[4,2,128,128]{3,2,1,0:T(8,128)S(1)}, f32[4,2,128,128]{3,2,1,0:T(8,128)S(1)}, u32[]{:S(2)}, u32[]{:S(2)}) collective-permute-start(f32[4,2,128,128]{3,2,1,0:T(8,128)S(1)} %get-tuple-element.27), channel_id=1, source_target_pairs={{0,1},{1,0},{2,3},{3,2},{4,5},{5,4},{6,7},{7,6},{8,9},{9,8},{10,11... | collective-permute-start | bytes 1572872 | tf_op jit(solution)/shard_map/ppermute | solution.py:352
  101.9 36.4 %collective-permute-start.21 = (f32[8,2,128,128]{3,2,1,0:T(8,128)S(1)}, f32[8,2,128,128]{3,2,1,0:T(8,128)}, u32[]{:S(2)}, u32[]{:S(2)}) collective-permute-start(f32[8,2,128,128]{3,2,1,0:T(8,128)S(1)} %get-tuple-element.25.refs_6_.refs_8_.refs_2_), channel_id=1, source_target_pairs={{0,8},{8,16},{16,24},{24,0},{1,9},{9,17},{17,25},{25,1},{2,10},{10... | collective-permute-start | bytes 3145736 | tf_op jit(solution)/shard_map/ppermute | solution.py:357
  103.3 55.1 %collective-permute-start.23 = (f32[8,2,128,128]{3,2,1,0:T(8,128)}, f32[8,2,128,128]{3,2,1,0:T(8,128)}, u32[]{:S(2)}, u32[]{:S(2)}) collective-permute-start(f32[8,2,128,128]{3,2,1,0:T(8,128)} %partial_1_2_ends.1.refs_11_), channel_id=1, source_target_pairs={{0,2},{6,4},{1,3},{7,5},{8,10},{14,12},{9,11},{15,13},{16,18},{22,... | collective-permute-start | bytes 3145736 | tf_op jit(solution)/shard_map/ppermute | solution.py:370
  107.5 51.0 %collective-permute-start.25 = (f32[8,2,128,128]{3,2,1,0:T(8,128)}, f32[8,2,128,128]{3,2,1,0:T(8,128)}, u32[]{:S(2)}, u32[]{:S(2)}) collective-permute-start(f32[8,2,128,128]{3,2,1,0:T(8,128)} %partial_1_0_rest.1.refs_10_), channel_id=1, source_target_pairs={{4,6},{2,0},{5,7},{3,1},{12,14},{10,8},{13,15},{11,9},{20,22},{18,... | collective-permute-start | bytes 3145736 | tf_op jit(solution)/shard_map/ppermute | solution.py:370
  109.6 6.5 %copy-start.22 = (s32[8,2,9]{2,1,0:T(2,128)S(1)}, s32[8,2,9]{2,1,0:T(2,128)}, u32[]{:S(2)}) copy-start(s32[8,2,9]{2,1,0:T(2,128)} %param.29) | copy-start | bytes 1732
  114.8 43.6 %collective-permute-start.24 = (f32[8,2,128,128]{3,2,1,0:T(8,128)}, f32[8,2,128,128]{3,2,1,0:T(8,128)}, u32[]{:S(2)}, u32[]{:S(2)}) collective-permute-start(f32[8,2,128,128]{3,2,1,0:T(8,128)} %add_1_1_3.1.refs_10_), channel_id=1, source_target_pairs={{2,6},{4,0},{3,7},{5,1},{10,14},{12,8},{11,15},{13,9},{18,22},{20,... | collective-permute-start | bytes 3145736 | tf_op jit(solution)/shard_map/ppermute | solution.py:370
  137.6 20.8 %collective-permute-start.26 = (f32[4,2,128,128]{3,2,1,0:T(8,128)S(1)}, f32[4,2,128,128]{3,2,1,0:T(8,128)S(1)}, u32[]{:S(2)}, u32[]{:S(2)}) collective-permute-start(f32[4,2,128,128]{3,2,1,0:T(8,128)S(1)} %get-tuple-element.29.refs_3_), channel_id=1, source_target_pairs={{2,4},{4,2},{3,5},{5,3},{10,12},{12,10},{11,13},{13,11},{18,20},{2... | collective-permute-start | bytes 1572872 | tf_op jit(solution)/shard_map/ppermute | solution.py:370
  138.4 23.6 %collective-permute-start.22 = (f32[4,2,128,128]{3,2,1,0:T(8,128)S(1)}, f32[4,2,128,128]{3,2,1,0:T(8,128)S(1)}, u32[]{:S(2)}, u32[]{:S(2)}) collective-permute-start(f32[4,2,128,128]{3,2,1,0:T(8,128)S(1)} %get-tuple-element.31), channel_id=1, source_target_pairs={{2,4},{4,2},{3,5},{5,3},{10,12},{12,10},{11,13},{13,11},{18,20},{2... | collective-permute-start | bytes 1572872 | tf_op jit(solution)/shard_map/ppermute | solution.py:370
  (21 other events, 35.9 us)

commit v5 on v4

--- a/solution.py
+++ b/solution.py
@@ -513,14 +513,6 @@
         sent_five[slot] = partial(0, slot, upper_five, lower_five, coupling, "all")
         moving_five[goals[slot]] = start(sent_five, goals[slot])
     sums_five = sums(0, upper_five, lower_five, local_five, occupation_five)
-    tilted = call(
-        turn_one_kernel,
-        [jax.ShapeDtypeStruct((n, n), jnp.float32)],
-        [],
-        [turned, eigenbasis, coupling],
-        (),
-        "tilt_coupling",
-    )[0]
     moving_five[far] = go_on(0, sent_five, moving_five[far], far)
     eigen_seven, *pieces = call(
         turn_kernel,
@@ -534,9 +526,17 @@
     pieces = [sibling_of(piece, every) for piece in pieces]
     upper_six = (eigen_seven, *pieces)
     raised_six = along(eigen_seven, -1)
+    tilted = call(
+        turn_one_kernel,
+        [jax.ShapeDtypeStruct((n, n), jnp.float32)],
+        [],
+        [turned, eigenbasis, coupling],
+        (),
+        "tilt_coupling",
+        after=pieces,
+    )[0]
     for g in goals[1:]:
-        after = [lowered_five] if g == goals[-2] else []
-        moving_five[g] = go_on(0, sent_five, moving_five[g], g, after)
+        moving_five[g] = go_on(0, sent_five, moving_five[g], g)
     own_five = call(
         finish_kernel,
         [whole],
@@ -544,7 +544,6 @@
         [coupling, *sums_five, raised_five, lowered_five],
         (),
         "finish_five",
-        after=pieces,
     )[0]
     last = [moving_five[far], *beside_five]
     ends_five, pieces = solve_five(own_five, last, "ends", [], [per] * HALVES)

time: 169 us -> 166 us (0.982)
  the two profiles are of different devices: /device:TPU:0 before, /device:TPU:18 now
where the time goes in v5:
time: 166 us; the launch traced here: 165 us
  Pallas kernels  61.9 us (37%)
  waiting for transfers between devices  51.9 us (31%)
  starting transfers between devices  38.6 us (23%)
  local copies, waits for them, and re-layouts  11.6 us (7%)
    pallas_call x24, Pallas kernels, call(): pl.pallas_call(without_waits, out_shape=outs, in_specs=[pl.BlockSpec(memo...  61.9 us
    ppermute x12, waiting for transfers between devices, hop(): return lax.ppermute(array, 'mb', pairs)  47.7 us
    ppermute x12, starting transfers between devices, hop(): return lax.ppermute(array, 'mb', pairs)  27.4 us
    unnamed x65, local copies, waits for them, and re-layouts  11.1 us
    ppermute x4, starting transfers between devices, along(): lax.ppermute(array, 'ma', [(i, (i + by) % row_count) for i in range(row_c...  4.9 us
  transfers between devices with their start and end apart: 27, of which 11 were waited for; matrix products, arithmetic and copies ran while one was open for 1% of the time, Pallas kernels for 33%

profile of v5, /device:TPU:18, one launch (start us, length us, event | category | flops | bytes accessed | tf_op | source)
XLA Modules:
  0.0 165.2 jit_solution(2211280641277648363)
XLA Ops:
  8.5 2.5 %collective-permute-done.1 = s32[8,20]{1,0:T(8,128)S(1)} collective-permute-done((s32[8,20]{1,0:T(8,128)S(1)}, s32[8,20]{1,0:T(8,128)S(1)}, u32[]{:S(2)}, u32[]{:S(2)}) %collective-permute-start.1) | collective-permute-done | bytes 672 | tf_op jit(solution)/shard_map/ppermute | solution.py:360
  12.2 4.0 %partial_0_0_all.1.refs_8_ = f32[8,2,128,128]{3,2,1,0:T(8,128)} custom-call(s32[7]{0:T(128)S(1)} %pad_add_fusion.1.refs_0_, s32[32,20]{1,0:T(8,128)S(1)} %pad_add_fusion.refs_1_, f32[2,12]{1,0:T(2,128)S(1)} %copy-done.20, f32[8,2,128,128]{3,2,1,0:T(8,128)} %refs_5_.9, f32[8,2,128,128]{3,2,1,0:T(8,128)S(1)} %collective-permute-done.3.refs_4_.refs_6_, ...), custom_call_target="tpu_custom_call" | custom-call | flops 1 | bytes 1 | tf_op jit(solution)/shard_map/partial_0_0_all/pallas_call | solution.py:304
  16.2 2.8 %collective-permute-start.8 = (f32[8,2,128,128]{3,2,1,0:T(8,128)}, f32[8,2,128,128]{3,2,1,0:T(8,128)}, u32[]{:S(2)}, u32[]{:S(2)}) collective-permute-start(f32[8,2,128,128]{3,2,1,0:T(8,128)} %partial_0_0_all.1.refs_8_), channel_id=1, source_target_pairs={{0,2},{6,4},{1,3},{7,5},{4,6},{2,0},{5,7},{3,1},{8,10},{14,12},{9,... | collective-permute-start | bytes 3145736 | tf_op jit(solution)/shard_map/ppermute | solution.py:370
  19.6 4.1 %partial_0_1_all.1.refs_8_.refs_0_ = f32[8,2,128,128]{3,2,1,0:T(8,128)} custom-call(s32[7]{0:T(128)S(1)} %pad_add_fusion.1.refs_0_, s32[32,20]{1,0:T(8,128)S(1)} %pad_add_fusion.refs_1_, f32[2,12]{1,0:T(2,128)S(1)} %copy-done.20, f32[8,2,128,128]{3,2,1,0:T(8,128)} %refs_5_.9, f32[8,2,128,128]{3,2,1,0:T(8,128)S(1)} %collective-permute-done.3.refs_4_.refs_6_, ...), custom_call_target="tpu_custom_call" | custom-call | flops 1 | bytes 1 | tf_op jit(solution)/shard_map/partial_0_1_all/pallas_call | solution.py:304
  25.0 3.0 %partial_0_2_all.1.refs_9_.refs_0_ = f32[8,2,128,128]{3,2,1,0:T(8,128)S(1)} custom-call(s32[7]{0:T(128)S(1)} %pad_add_fusion.1.refs_0_, s32[32,20]{1,0:T(8,128)S(1)} %pad_add_fusion.refs_1_, f32[2,12]{1,0:T(2,128)S(1)} %copy-done.20, f32[8,2,128,128]{3,2,1,0:T(8,128)} %refs_5_.9, f32[8,2,128,128]{3,2,1,0:T(8,128)S(1)} %collective-permute-done.3.refs_4_.refs_6_, ...), custom_call_target="tpu_custom_call" | custom-call | flops 1 | bytes 1 | tf_op jit(solution)/shard_map/partial_0_2_all/pallas_call | solution.py:304
  28.1 2.4 %collective-permute-start.6 = (f32[8,2,128,128]{3,2,1,0:T(8,128)S(1)}, f32[8,2,128,128]{3,2,1,0:T(8,128)}, u32[]{:S(2)}, u32[]{:S(2)}) collective-permute-start(f32[8,2,128,128]{3,2,1,0:T(8,128)S(1)} %copy-done.1), channel_id=1, source_target_pairs={{0,8},{8,16},{16,24},{24,0},{1,9},{9,17},{17,25},{25,1},{2,10},{10... | collective-permute-start | bytes 3145736 | tf_op jit(solution)/shard_map/ppermute | solution.py:357
  30.5 3.6 %sums_0.1 = (f32[8,2,128,128]{3,2,1,0:T(8,128)S(1)}, f32[8,2,128,128]{3,2,1,0:T(8,128)S(1)}) custom-call(s32[7]{0:T(128)S(1)} %pad_add_fusion.1.refs_0_, s32[32,20]{1,0:T(8,128)S(1)} %pad_add_fusion.refs_1_, f32[2,12]{1,0:T(2,128)S(1)} %copy-done.20, s32[8,18]{1,0:T(8,128)S(1)} %reshape.10.refs_3_, s32[8,12]{1,0:T(8,128)S(1)} %copy-done.21, ...), custom_call_target="tpu_custom_call" | custom-call | flops 1 | bytes 1 | tf_op jit(solution)/shard_map/sums_0/pallas_call | solution.py:304
  35.1 8.3 %collective-permute-done.8.refs_1_.refs_9_ = f32[8,2,128,128]{3,2,1,0:T(8,128)} collective-permute-done((f32[8,2,128,128]{3,2,1,0:T(8,128)}, f32[8,2,128,128]{3,2,1,0:T(8,128)}, u32[]{:S(2)}, u32[]{:S(2)}) %collective-permute-start.8) | collective-permute-done | bytes 1048608 | tf_op jit(solution)/shard_map/ppermute | solution.py:370
  43.4 2.6 %add_0_1_3.1.refs_3_ = f32[8,2,128,128]{3,2,1,0:T(8,128)} custom-call(f32[8,2,128,128]{3,2,1,0:T(8,128)} %partial_0_1_all.1.refs_8_.refs_0_, f32[8,2,128,128]{3,2,1,0:T(8,128)} %collective-permute-done.8.refs_1_.refs_9_, f32[8,2,128,128]{3,2,1,0:T(8,128)S(1)} %get-tuple-element.17.refs_2_.refs_3_), custom_call_target="tpu_custom_call" | custom-call | flops 1 | bytes 1 | tf_op jit(solution)/shard_map/add_0_1_3/pallas_call | solution.py:304
  46.1 2.3 %collective-permute-start.13 = (f32[8,2,128,128]{3,2,1,0:T(8,128)}, f32[8,2,128,128]{3,2,1,0:T(8,128)}, u32[]{:S(2)}, u32[]{:S(2)}) collective-permute-start(f32[8,2,128,128]{3,2,1,0:T(8,128)} %add_0_1_3.1.refs_3_), channel_id=1, source_target_pairs={{2,6},{4,0},{3,7},{5,1},{10,14},{12,8},{11,15},{13,9},{18,22},{20,... | collective-permute-start | bytes 3145736 | tf_op jit(solution)/shard_map/ppermute | solution.py:370
  49.7 2.9 %tilt_seven.1 = (f32[8,2,128,128]{3,2,1,0:T(8,128)S(1)}, f32[4,2,128,128]{3,2,1,0:T(8,128)}, f32[4,2,128,128]{3,2,1,0:T(8,128)}) custom-call(f32[128,128]{1,0:T(8,128)S(1)} %bitcast.6, f32[128,128]{1,0:T(8,128)S(1)} %copy-done.10, f32[8,2,128,128]{3,2,1,0:T(8,128)S(1)} %copy-done.17, f32[8,2,128,128]{3,2,1,0:T(8,128)} %add_0_1_3.1.refs_3_, ...), custom_call_target="tpu_custom_call" | custom-call | flops 1 | bytes 1 | tf_op jit(solution)/shard_map/tilt_seven/pallas_call | solution.py:304
  57.0 8.9 %collective-permute-done.7.refs_1_ = f32[8,2,128,128]{3,2,1,0:T(8,128)} collective-permute-done((f32[8,2,128,128]{3,2,1,0:T(8,128)}, f32[8,2,128,128]{3,2,1,0:T(8,128)}, u32[]{:S(2)}, u32[]{:S(2)}) %collective-permute-start.7) | collective-permute-done | bytes 1048608 | tf_op jit(solution)/shard_map/ppermute | solution.py:370
  67.3 1.9 %collective-permute-start.11 = (f32[8,2,128,128]{3,2,1,0:T(8,128)S(1)}, f32[8,2,128,128]{3,2,1,0:T(8,128)S(1)}, u32[]{:S(2)}, u32[]{:S(2)}) collective-permute-start(f32[8,2,128,128]{3,2,1,0:T(8,128)S(1)} %add_0_1_2.1.refs_7_), channel_id=1, source_target_pairs={{2,4},{4,2},{3,5},{5,3},{10,12},{12,10},{11,13},{13,11},{18,20},{2... | collective-permute-start | bytes 3145736 | tf_op jit(solution)/shard_map/ppermute | solution.py:370
  69.2 2.4 %finish_five.1.refs_7_ = f32[8,2,128,128]{3,2,1,0:T(8,128)S(1)} custom-call(s32[8,12]{1,0:T(8,128)S(1)} %copy-done.21, f32[2,12]{1,0:T(2,128)S(1)} %copy-done.20, f32[128,128]{1,0:T(8,128)S(1)} %copy-done.16, f32[8,2,128,128]{3,2,1,0:T(8,128)S(1)} %copy-done.15, f32[8,2,128,128]{3,2,1,0:T(8,128)S(1)} %copy-done.19, ...), custom_call_target="tpu_custom_call" | custom-call | flops 1 | bytes 1 | tf_op jit(solution)/shard_map/finish_five/pallas_call | solution.py:304
  77.7 8.3 %collective-permute-done.12.refs_11_.refs_9_ = f32[8,2,128,128]{3,2,1,0:T(8,128)S(1)} collective-permute-done((f32[8,2,128,128]{3,2,1,0:T(8,128)}, f32[8,2,128,128]{3,2,1,0:T(8,128)S(1)}, u32[]{:S(2)}, u32[]{:S(2)}) %collective-permute-start.12) | collective-permute-done | bytes 1048608 | tf_op jit(solution)/shard_map/ppermute | solution.py:370
  89.0 1.9 %partial_1_2_ends.1.refs_11_ = f32[8,2,128,128]{3,2,1,0:T(8,128)} custom-call(s32[7]{0:T(128)S(1)} %pad_add_fusion.1.refs_0_, s32[32,20]{1,0:T(8,128)S(1)} %pad_add_fusion.refs_1_, f32[2,12]{1,0:T(2,128)S(1)} %copy-done.20, f32[8,2,128,128]{3,2,1,0:T(8,128)S(1)} %get-tuple-element.19.refs_3_.refs_5_, ...), custom_call_target="tpu_custom_call" | custom-call | flops 1 | bytes 1 | tf_op jit(solution)/shard_map/partial_1_2_ends/pallas_call | solution.py:304
  92.0 2.7 %solve_five_rest.1 = (f32[8,2,128,128]{3,2,1,0:T(8,128)S(1)}, f32[4,2,128,128]{3,2,1,0:T(8,128)S(1)}, f32[4,2,128,128]{3,2,1,0:T(8,128)S(1)}) custom-call(s32[7]{0:T(128)S(1)} %pad_add_fusion.1.refs_0_, s32[8,12]{1,0:T(8,128)S(1)} %copy-done.21, f32[12]{0:T(128)S(1)} %copy-done.24, f32[1,128]{1,0:T(1,128)S(1)} %bitcast.15, ...), custom_call_target="tpu_custom_call" | custom-call | flops 1 | bytes 1 | tf_op jit(solution)/shard_map/solve_five_rest/pallas_call | solution.py:304
  98.1 4.0 %partial_1_0_rest.1.refs_10_ = f32[8,2,128,128]{3,2,1,0:T(8,128)} custom-call(s32[7]{0:T(128)S(1)} %pad_add_fusion.1.refs_0_, s32[32,20]{1,0:T(8,128)S(1)} %pad_add_fusion.refs_1_, f32[2,12]{1,0:T(2,128)S(1)} %copy-done.20, f32[8,2,128,128]{3,2,1,0:T(8,128)S(1)} %get-tuple-element.19.refs_3_.refs_5_, ...), custom_call_target="tpu_custom_call" | custom-call | flops 1 | bytes 1 | tf_op jit(solution)/shard_map/partial_1_0_rest/pallas_call | solution.py:304
  102.0 5.8 %collective-permute-start.25 = (f32[8,2,128,128]{3,2,1,0:T(8,128)}, f32[8,2,128,128]{3,2,1,0:T(8,128)}, u32[]{:S(2)}, u32[]{:S(2)}) collective-permute-start(f32[8,2,128,128]{3,2,1,0:T(8,128)} %partial_1_0_rest.1.refs_10_), channel_id=1, source_target_pairs={{4,6},{2,0},{5,7},{3,1},{12,14},{10,8},{13,15},{11,9},{20,22},{18,... | collective-permute-start | bytes 3145736 | tf_op jit(solution)/shard_map/ppermute | solution.py:370
  107.8 2.9 %partial_1_1_rest.1.refs_0_ = f32[8,2,128,128]{3,2,1,0:T(8,128)S(1)} custom-call(s32[7]{0:T(128)S(1)} %pad_add_fusion.1.refs_0_, s32[32,20]{1,0:T(8,128)S(1)} %pad_add_fusion.refs_1_, f32[2,12]{1,0:T(2,128)S(1)} %copy-done.20, f32[8,2,128,128]{3,2,1,0:T(8,128)S(1)} %get-tuple-element.19.refs_3_.refs_5_, ...), custom_call_target="tpu_custom_call" | custom-call | flops 1 | bytes 1 | tf_op jit(solution)/shard_map/partial_1_1_rest/pallas_call | solution.py:304
  112.5 2.3 %collective-permute-start.24 = (f32[8,2,128,128]{3,2,1,0:T(8,128)}, f32[8,2,128,128]{3,2,1,0:T(8,128)}, u32[]{:S(2)}, u32[]{:S(2)}) collective-permute-start(f32[8,2,128,128]{3,2,1,0:T(8,128)} %add_1_1_3.1.refs_10_), channel_id=1, source_target_pairs={{2,6},{4,0},{3,7},{5,1},{10,14},{12,8},{11,15},{13,9},{18,22},{20,... | collective-permute-start | bytes 3145736 | tf_op jit(solution)/shard_map/ppermute | solution.py:370
  116.9 3.1 %partial_1_2_rest.1.refs_11_.refs_0_ = f32[8,2,128,128]{3,2,1,0:T(8,128)S(1)} custom-call(s32[7]{0:T(128)S(1)} %pad_add_fusion.1.refs_0_, s32[32,20]{1,0:T(8,128)S(1)} %pad_add_fusion.refs_1_, f32[2,12]{1,0:T(2,128)S(1)} %copy-done.20, f32[8,2,128,128]{3,2,1,0:T(8,128)S(1)} %get-tuple-element.19.refs_3_.refs_5_, ...), custom_call_target="tpu_custom_call" | custom-call | flops 1 | bytes 1 | tf_op jit(solution)/shard_map/partial_1_2_rest/pallas_call | solution.py:304
  120.1 3.9 %sums_1.1 = (f32[8,2,128,128]{3,2,1,0:T(8,128)S(1)}, f32[8,2,128,128]{3,2,1,0:T(8,128)S(1)}) custom-call(s32[7]{0:T(128)S(1)} %pad_add_fusion.1.refs_0_, s32[32,20]{1,0:T(8,128)S(1)} %pad_add_fusion.refs_1_, f32[2,12]{1,0:T(2,128)S(1)} %copy-done.20, s32[8,18]{1,0:T(8,128)S(1)} %reshape.11.refs_3_, s32[8,12]{1,0:T(8,128)S(1)} %copy-done.22, ...), custom_call_target="tpu_custom_call" | custom-call | flops 1 | bytes 1 | tf_op jit(solution)/shard_map/sums_1/pallas_call | solution.py:304
  124.0 9.9 %collective-permute-done.20.refs_1_ = f32[8,2,128,128]{3,2,1,0:T(8,128)} collective-permute-done((f32[8,2,128,128]{3,2,1,0:T(8,128)}, f32[8,2,128,128]{3,2,1,0:T(8,128)}, u32[]{:S(2)}, u32[]{:S(2)}) %collective-permute-start.20) | collective-permute-done | bytes 1048608 | tf_op jit(solution)/shard_map/ppermute | solution.py:370
  135.3 1.9 %collective-permute-start.26 = (f32[4,2,128,128]{3,2,1,0:T(8,128)S(1)}, f32[4,2,128,128]{3,2,1,0:T(8,128)S(1)}, u32[]{:S(2)}, u32[]{:S(2)}) collective-permute-start(f32[4,2,128,128]{3,2,1,0:T(8,128)S(1)} %get-tuple-element.29.refs_3_), channel_id=1, source_target_pairs={{2,4},{4,2},{3,5},{5,3},{10,12},{12,10},{11,13},{13,11},{18,20},{2... | collective-permute-start | bytes 1572872 | tf_op jit(solution)/shard_map/ppermute | solution.py:370
  137.2 4.1 %collective-permute-start.22 = (f32[4,2,128,128]{3,2,1,0:T(8,128)S(1)}, f32[4,2,128,128]{3,2,1,0:T(8,128)S(1)}, u32[]{:S(2)}, u32[]{:S(2)}) collective-permute-start(f32[4,2,128,128]{3,2,1,0:T(8,128)S(1)} %get-tuple-element.31), channel_id=1, source_target_pairs={{2,4},{4,2},{3,5},{5,3},{10,12},{12,10},{11,13},{13,11},{18,20},{2... | collective-permute-start | bytes 1572872 | tf_op jit(solution)/shard_map/ppermute | solution.py:370
  141.3 3.1 %back_five.1.refs_7_ = f32[8,2,128,128]{3,2,1,0:T(8,128)} custom-call(f32[128,128]{1,0:T(8,128)S(1)} %copy-done.10, f32[128,128]{1,0:T(8,128)S(1)} %bitcast.10, f32[8,2,128,128]{3,2,1,0:T(8,128)S(1)} %get-tuple-element.25.refs_6_.refs_8_.refs_2_, f32[4,2,128,128]{3,2,1,0:T(8,128)S(1)} %get-tuple-element.29.refs_3_), custom_call_target="tpu_custom_call" | custom-call | flops 1 | bytes 1 | tf_op jit(solution)/shard_map/back_five/pallas_call | solution.py:304
  145.6 2.2 %finish_six.1.refs_6_ = f32[8,2,128,128]{3,2,1,0:T(8,128)S(1)} custom-call(s32[8,12]{1,0:T(8,128)S(1)} %copy-done.22, f32[2,12]{1,0:T(2,128)S(1)} %copy-done.20, f32[128,128]{1,0:T(8,128)S(1)} %tilt_coupling.1.refs_2_.refs_9_, f32[8,2,128,128]{3,2,1,0:T(8,128)S(1)} %get-tuple-element.28.refs_2_.refs_3_, f32[8,2,128,128]{3,2,1,0:T(8,128)S(1)} %get-tuple-element.30.refs_4_, ...), custom_call_target="tpu_custom_call" | custom-call | flops 1 | bytes 1 | tf_op jit(solution)/shard_map/finish_six/pallas_call | solution.py:304
  147.8 8.3 %collective-permute-done.23.refs_8_ = f32[8,2,128,128]{3,2,1,0:T(8,128)} collective-permute-done((f32[8,2,128,128]{3,2,1,0:T(8,128)}, f32[8,2,128,128]{3,2,1,0:T(8,128)}, u32[]{:S(2)}, u32[]{:S(2)}) %collective-permute-start.23) | collective-permute-done | bytes 1048608 | tf_op jit(solution)/shard_map/ppermute | solution.py:370
  156.2 3.4 %solve_six_0.1.refs_11_ = f32[8,2,128,128]{3,2,1,0:T(8,128)} custom-call(s32[8,12]{1,0:T(8,128)S(1)} %copy-done.22, f32[12]{0:T(128)S(1)} %copy-done.24, f32[1,128]{1,0:T(1,128)S(1)} %bitcast.16, f32[128,1]{1,0:T(8,128)S(1)} %copy.25.refs_4_.refs_3_, f32[128,128]{1,0:T(8,128)S(1)} %copy-done.10, f32[128,128]{1,0:T(8,128)S(1)} %bitcast.11, ...), custom_call_target="tpu_custom_call" | custom-call | flops 1 | bytes 1 | tf_op jit(solution)/shard_map/solve_six_0/pallas_call | solution.py:304
  159.6 2.2 %collective-permute-done.22.refs_7_ = f32[4,2,128,128]{3,2,1,0:T(8,128)S(1)} collective-permute-done((f32[4,2,128,128]{3,2,1,0:T(8,128)S(1)}, f32[4,2,128,128]{3,2,1,0:T(8,128)S(1)}, u32[]{:S(2)}, u32[]{:S(2)}) %collective-permute-start.22) | collective-permute-done | bytes 524320 | tf_op jit(solution)/shard_map/ppermute | solution.py:370
  161.8 3.4 %solve_six_1.1 = f32[8,2,128,128]{3,2,1,0:T(8,128)} custom-call(s32[8,12]{1,0:T(8,128)S(1)} %copy-done.22, f32[12]{0:T(128)S(1)} %copy-done.24, f32[1,128]{1,0:T(1,128)S(1)} %bitcast.17, f32[128,1]{1,0:T(8,128)S(1)} %copy.25.refs_4_.refs_3_, f32[128,128]{1,0:T(8,128)S(1)} %copy-done.10, f32[128,128]{1,0:T(8,128)S(1)} %bitcast.12, ...), custom_call_target="tpu_custom_call", output_to_operand_aliasing={{}: (11, {})} | custom-call | flops 1 | bytes 1 | tf_op jit(solution)/shard_map/solve_six_1/pallas_call | solution.py:304
  (120 shorter events, 38.9 us)
Async XLA Ops:
  0.6 10.3 %collective-permute-start.3 = (f32[8,2,128,128]{3,2,1,0:T(8,128)}, f32[8,2,128,128]{3,2,1,0:T(8,128)S(1)}, u32[]{:S(2)}, u32[]{:S(2)}) collective-permute-start(f32[8,2,128,128]{3,2,1,0:T(8,128)} %refs_5_.9), channel_id=1, source_target_pairs={{0,1},{1,0},{2,3},{3,2},{4,5},{5,4},{6,7},{7,6},{8,9},{9,8},{10,11... | collective-permute-start | bytes 3145736 | tf_op jit(solution)/shard_map/ppermute | solution.py:352
  0.7 10.3 %collective-permute-start.4 = (f32[8,2,128,128]{3,2,1,0:T(8,128)}, f32[8,2,128,128]{3,2,1,0:T(8,128)S(1)}, u32[]{:S(2)}, u32[]{:S(2)}) collective-permute-start(f32[8,2,128,128]{3,2,1,0:T(8,128)} %refs_7_.7), channel_id=1, source_target_pairs={{0,1},{1,0},{2,3},{3,2},{4,5},{5,4},{6,7},{7,6},{8,9},{9,8},{10,11... | collective-permute-start | bytes 3145736 | tf_op jit(solution)/shard_map/ppermute | solution.py:352
  4.9 3.6 %collective-permute-start = (s32[8,20]{1,0:T(8,128)S(1)}, s32[8,20]{1,0:T(8,128)S(1)}, u32[]{:S(2)}, u32[]{:S(2)}) collective-permute-start(s32[8,20]{1,0:T(8,128)S(1)} %concatenate.10), channel_id=1, source_target_pairs={{0,2},{1,3},{2,4},{3,5},{4,6},{5,7},{6,0},{7,1},{8,10},{9,11},{10,... | collective-permute-start | bytes 1928 | tf_op jit(solution)/shard_map/ppermute | solution.py:360
  6.4 4.5 %collective-permute-start.1 = (s32[8,20]{1,0:T(8,128)S(1)}, s32[8,20]{1,0:T(8,128)S(1)}, u32[]{:S(2)}, u32[]{:S(2)}) collective-permute-start(s32[8,20]{1,0:T(8,128)S(1)} %concatenate.10), channel_id=1, source_target_pairs={{0,4},{1,5},{2,6},{3,7},{4,0},{5,1},{6,2},{7,3},{8,12},{9,13},{10,... | collective-permute-start | bytes 1928 | tf_op jit(solution)/shard_map/ppermute | solution.py:360
  6.8 4.2 %collective-permute-start.2 = (s32[8,20]{1,0:T(8,128)S(1)}, s32[8,20]{1,0:T(8,128)S(1)}, u32[]{:S(2)}, u32[]{:S(2)}) collective-permute-start(s32[8,20]{1,0:T(8,128)S(1)} %concatenate.10), channel_id=1, source_target_pairs={{0,6},{1,7},{2,0},{3,1},{4,2},{5,3},{6,4},{7,5},{8,14},{9,15},{10,... | collective-permute-start | bytes 1928 | tf_op jit(solution)/shard_map/ppermute | solution.py:360
  16.2 27.2 %collective-permute-start.8 = (f32[8,2,128,128]{3,2,1,0:T(8,128)}, f32[8,2,128,128]{3,2,1,0:T(8,128)}, u32[]{:S(2)}, u32[]{:S(2)}) collective-permute-start(f32[8,2,128,128]{3,2,1,0:T(8,128)} %partial_0_0_all.1.refs_8_), channel_id=1, source_target_pairs={{0,2},{6,4},{1,3},{7,5},{4,6},{2,0},{5,7},{3,1},{8,10},{14,12},{9,... | collective-permute-start | bytes 3145736 | tf_op jit(solution)/shard_map/ppermute | solution.py:370
  19.1 29.4 %collective-permute-start.5 = (f32[8,2,128,128]{3,2,1,0:T(8,128)}, f32[8,2,128,128]{3,2,1,0:T(8,128)}, u32[]{:S(2)}, u32[]{:S(2)}) collective-permute-start(f32[8,2,128,128]{3,2,1,0:T(8,128)} %refs_5_.9), channel_id=1, source_target_pairs={{0,24},{8,0},{16,8},{24,16},{1,25},{9,1},{17,9},{25,17},{2,26},{10... | collective-permute-start | bytes 3145736 | tf_op jit(solution)/shard_map/ppermute | solution.py:357
  23.6 42.3 %collective-permute-start.7 = (f32[8,2,128,128]{3,2,1,0:T(8,128)}, f32[8,2,128,128]{3,2,1,0:T(8,128)}, u32[]{:S(2)}, u32[]{:S(2)}) collective-permute-start(f32[8,2,128,128]{3,2,1,0:T(8,128)} %partial_0_1_all.1.refs_8_.refs_0_), channel_id=1, source_target_pairs={{0,2},{6,4},{1,3},{7,5},{8,10},{14,12},{9,11},{15,13},{16,18},{22,... | collective-permute-start | bytes 3145736 | tf_op jit(solution)/shard_map/ppermute | solution.py:370
  28.1 41.1 %collective-permute-start.6 = (f32[8,2,128,128]{3,2,1,0:T(8,128)S(1)}, f32[8,2,128,128]{3,2,1,0:T(8,128)}, u32[]{:S(2)}, u32[]{:S(2)}) collective-permute-start(f32[8,2,128,128]{3,2,1,0:T(8,128)S(1)} %copy-done.1), channel_id=1, source_target_pairs={{0,8},{8,16},{16,24},{24,0},{1,9},{9,17},{17,25},{25,1},{2,10},{10... | collective-permute-start | bytes 3145736 | tf_op jit(solution)/shard_map/ppermute | solution.py:357
  35.1 11.0 %copy-start.14 = (f32[8,2,128,128]{3,2,1,0:T(8,128)}, f32[8,2,128,128]{3,2,1,0:T(8,128)S(1)}, u32[]{:S(2)}) copy-start(f32[8,2,128,128]{3,2,1,0:T(8,128)S(1)} %get-tuple-element.17.refs_2_.refs_3_) | copy-start | bytes 3145732
  46.1 25.6 %collective-permute-start.13 = (f32[8,2,128,128]{3,2,1,0:T(8,128)}, f32[8,2,128,128]{3,2,1,0:T(8,128)}, u32[]{:S(2)}, u32[]{:S(2)}) collective-permute-start(f32[8,2,128,128]{3,2,1,0:T(8,128)} %add_0_1_3.1.refs_3_), channel_id=1, source_target_pairs={{2,6},{4,0},{3,7},{5,1},{10,14},{12,8},{11,15},{13,9},{18,22},{20,... | collective-permute-start | bytes 3145736 | tf_op jit(solution)/shard_map/ppermute | solution.py:370
  52.6 2.1 %collective-permute-start.10 = (f32[4,2,128,128]{3,2,1,0:T(8,128)}, f32[4,2,128,128]{3,2,1,0:T(8,128)S(1)}, u32[]{:S(2)}, u32[]{:S(2)}) collective-permute-start(f32[4,2,128,128]{3,2,1,0:T(8,128)} %get-tuple-element.21), channel_id=1, source_target_pairs={{0,1},{1,0},{2,3},{3,2},{4,5},{5,4},{6,7},{7,6},{8,9},{9,8},{10,11... | collective-permute-start | bytes 1572872 | tf_op jit(solution)/shard_map/ppermute | solution.py:352
  52.7 3.4 %collective-permute-start.9 = (f32[4,2,128,128]{3,2,1,0:T(8,128)}, f32[4,2,128,128]{3,2,1,0:T(8,128)S(1)}, u32[]{:S(2)}, u32[]{:S(2)}) collective-permute-start(f32[4,2,128,128]{3,2,1,0:T(8,128)} %get-tuple-element.20), channel_id=1, source_target_pairs={{0,1},{1,0},{2,3},{3,2},{4,5},{5,4},{6,7},{7,6},{8,9},{9,8},{10,11... | collective-permute-start | bytes 1572872 | tf_op jit(solution)/shard_map/ppermute | solution.py:352
  54.8 31.2 %collective-permute-start.12 = (f32[8,2,128,128]{3,2,1,0:T(8,128)}, f32[8,2,128,128]{3,2,1,0:T(8,128)S(1)}, u32[]{:S(2)}, u32[]{:S(2)}) collective-permute-start(f32[8,2,128,128]{3,2,1,0:T(8,128)} %copy-done.2), channel_id=1, source_target_pairs={{0,2},{6,4},{1,3},{7,5},{8,10},{14,12},{9,11},{15,13},{16,18},{22,... | collective-permute-start | bytes 3145736 | tf_op jit(solution)/shard_map/ppermute | solution.py:370
  56.1 9.8 %copy-start.3 = (f32[8,2,128,128]{3,2,1,0:T(8,128)S(1)}, f32[8,2,128,128]{3,2,1,0:T(8,128)}, u32[]{:S(2)}) copy-start(f32[8,2,128,128]{3,2,1,0:T(8,128)} %copy-done.2) | copy-start | bytes 3145732
  56.1 34.8 %collective-permute-start.16 = (f32[8,2,128,128]{3,2,1,0:T(8,128)S(1)}, f32[8,2,128,128]{3,2,1,0:T(8,128)S(1)}, u32[]{:S(2)}, u32[]{:S(2)}) collective-permute-start(f32[8,2,128,128]{3,2,1,0:T(8,128)S(1)} %get-tuple-element.19.refs_3_.refs_5_), channel_id=1, source_target_pairs={{0,24},{8,0},{16,8},{24,16},{1,25},{9,1},{17,9},{25,17},{2,26},{10... | collective-permute-start | bytes 3145736 | tf_op jit(solution)/shard_map/ppermute | solution.py:357
  57.0 12.2 %copy-start.15 = (f32[8,2,128,128]{3,2,1,0:T(8,128)S(1)}, f32[8,2,128,128]{3,2,1,0:T(8,128)}, u32[]{:S(2)}) copy-start(f32[8,2,128,128]{3,2,1,0:T(8,128)} %copy-done.14) | copy-start | bytes 3145732
  57.0 12.2 %copy-start.19 = (f32[8,2,128,128]{3,2,1,0:T(8,128)S(1)}, f32[8,2,128,128]{3,2,1,0:T(8,128)}, u32[]{:S(2)}) copy-start(f32[8,2,128,128]{3,2,1,0:T(8,128)} %copy-done.18) | copy-start | bytes 3145732
  67.3 24.7 %collective-permute-start.11 = (f32[8,2,128,128]{3,2,1,0:T(8,128)S(1)}, f32[8,2,128,128]{3,2,1,0:T(8,128)S(1)}, u32[]{:S(2)}, u32[]{:S(2)}) collective-permute-start(f32[8,2,128,128]{3,2,1,0:T(8,128)S(1)} %add_0_1_2.1.refs_7_), channel_id=1, source_target_pairs={{2,4},{4,2},{3,5},{5,3},{10,12},{12,10},{11,13},{13,11},{18,20},{2... | collective-permute-start | bytes 3145736 | tf_op jit(solution)/shard_map/ppermute | solution.py:370
  73.9 1.4 collective-permute-start.14
  74.6 0.7 collective-permute-start.15
  76.4 35.0 %collective-permute-start.19 = (f32[8,2,128,128]{3,2,1,0:T(8,128)S(1)}, f32[8,2,128,128]{3,2,1,0:T(8,128)S(1)}, u32[]{:S(2)}, u32[]{:S(2)}) collective-permute-start(f32[8,2,128,128]{3,2,1,0:T(8,128)S(1)} %partial_1_0_ends.1.refs_10_), channel_id=1, source_target_pairs={{0,2},{6,4},{1,3},{7,5},{8,10},{14,12},{9,11},{15,13},{16,18},{22,... | collective-permute-start | bytes 3145736 | tf_op jit(solution)/shard_map/ppermute | solution.py:370
  87.7 46.2 %collective-permute-start.20 = (f32[8,2,128,128]{3,2,1,0:T(8,128)}, f32[8,2,128,128]{3,2,1,0:T(8,128)}, u32[]{:S(2)}, u32[]{:S(2)}) collective-permute-start(f32[8,2,128,128]{3,2,1,0:T(8,128)} %partial_1_1_ends.1.refs_10_), channel_id=1, source_target_pairs={{0,2},{6,4},{1,3},{7,5},{8,10},{14,12},{9,11},{15,13},{16,18},{22,... | collective-permute-start | bytes 3145736 | tf_op jit(solution)/shard_map/ppermute | solution.py:370
  94.8 2.0 %collective-permute-start.17 = (f32[4,2,128,128]{3,2,1,0:T(8,128)S(1)}, f32[4,2,128,128]{3,2,1,0:T(8,128)S(1)}, u32[]{:S(2)}, u32[]{:S(2)}) collective-permute-start(f32[4,2,128,128]{3,2,1,0:T(8,128)S(1)} %get-tuple-element.26), channel_id=1, source_target_pairs={{0,1},{1,0},{2,3},{3,2},{4,5},{5,4},{6,7},{7,6},{8,9},{9,8},{10,11... | collective-permute-start | bytes 1572872 | tf_op jit(solution)/shard_map/ppermute | solution.py:352
  94.9 3.2 %collective-permute-start.18 = (f32[4,2,128,128]{3,2,1,0:T(8,128)S(1)}, f32[4,2,128,128]{3,2,1,0:T(8,128)S(1)}, u32[]{:S(2)}, u32[]{:S(2)}) collective-permute-start(f32[4,2,128,128]{3,2,1,0:T(8,128)S(1)} %get-tuple-element.27), channel_id=1, source_target_pairs={{0,1},{1,0},{2,3},{3,2},{4,5},{5,4},{6,7},{7,6},{8,9},{9,8},{10,11... | collective-permute-start | bytes 1572872 | tf_op jit(solution)/shard_map/ppermute | solution.py:352
  95.4 41.8 %collective-permute-start.21 = (f32[8,2,128,128]{3,2,1,0:T(8,128)S(1)}, f32[8,2,128,128]{3,2,1,0:T(8,128)}, u32[]{:S(2)}, u32[]{:S(2)}) collective-permute-start(f32[8,2,128,128]{3,2,1,0:T(8,128)S(1)} %get-tuple-element.25.refs_6_.refs_8_.refs_2_), channel_id=1, source_target_pairs={{0,8},{8,16},{16,24},{24,0},{1,9},{9,17},{17,25},{25,1},{2,10},{10... | collective-permute-start | bytes 3145736 | tf_op jit(solution)/shard_map/ppermute | solution.py:357
  96.8 11.0 %copy-start.4 = (f32[4,2,128,128]{3,2,1,0:T(8,128)}, f32[4,2,128,128]{3,2,1,0:T(8,128)S(1)}, u32[]{:S(2)}) copy-start(f32[4,2,128,128]{3,2,1,0:T(8,128)S(1)} %collective-permute-done.17.refs_7_.refs_9_) | copy-start | bytes 1572868
  96.8 59.4 %collective-permute-start.23 = (f32[8,2,128,128]{3,2,1,0:T(8,128)}, f32[8,2,128,128]{3,2,1,0:T(8,128)}, u32[]{:S(2)}, u32[]{:S(2)}) collective-permute-start(f32[8,2,128,128]{3,2,1,0:T(8,128)} %partial_1_2_ends.1.refs_11_), channel_id=1, source_target_pairs={{0,2},{6,4},{1,3},{7,5},{8,10},{14,12},{9,11},{15,13},{16,18},{22,... | collective-permute-start | bytes 3145736 | tf_op jit(solution)/shard_map/ppermute | solution.py:370
  102.0 54.1 %collective-permute-start.25 = (f32[8,2,128,128]{3,2,1,0:T(8,128)}, f32[8,2,128,128]{3,2,1,0:T(8,128)}, u32[]{:S(2)}, u32[]{:S(2)}) collective-permute-start(f32[8,2,128,128]{3,2,1,0:T(8,128)} %partial_1_0_rest.1.refs_10_), channel_id=1, source_target_pairs={{4,6},{2,0},{5,7},{3,1},{12,14},{10,8},{13,15},{11,9},{20,22},{18,... | collective-permute-start | bytes 3145736 | tf_op jit(solution)/shard_map/ppermute | solution.py:370
  112.5 43.7 %collective-permute-start.24 = (f32[8,2,128,128]{3,2,1,0:T(8,128)}, f32[8,2,128,128]{3,2,1,0:T(8,128)}, u32[]{:S(2)}, u32[]{:S(2)}) collective-permute-start(f32[8,2,128,128]{3,2,1,0:T(8,128)} %add_1_1_3.1.refs_10_), channel_id=1, source_target_pairs={{2,6},{4,0},{3,7},{5,1},{10,14},{12,8},{11,15},{13,9},{18,22},{20,... | collective-permute-start | bytes 3145736 | tf_op jit(solution)/shard_map/ppermute | solution.py:370
  135.3 20.9 %collective-permute-start.26 = (f32[4,2,128,128]{3,2,1,0:T(8,128)S(1)}, f32[4,2,128,128]{3,2,1,0:T(8,128)S(1)}, u32[]{:S(2)}, u32[]{:S(2)}) collective-permute-start(f32[4,2,128,128]{3,2,1,0:T(8,128)S(1)} %get-tuple-element.29.refs_3_), channel_id=1, source_target_pairs={{2,4},{4,2},{3,5},{5,3},{10,12},{12,10},{11,13},{13,11},{18,20},{2... | collective-permute-start | bytes 1572872 | tf_op jit(solution)/shard_map/ppermute | solution.py:370
  137.2 24.6 %collective-permute-start.22 = (f32[4,2,128,128]{3,2,1,0:T(8,128)S(1)}, f32[4,2,128,128]{3,2,1,0:T(8,128)S(1)}, u32[]{:S(2)}, u32[]{:S(2)}) collective-permute-start(f32[4,2,128,128]{3,2,1,0:T(8,128)S(1)} %get-tuple-element.31), channel_id=1, source_target_pairs={{2,4},{4,2},{3,5},{5,3},{10,12},{12,10},{11,13},{13,11},{18,20},{2... | collective-permute-start | bytes 1572872 | tf_op jit(solution)/shard_map/ppermute | solution.py:370
  (25 other events, 80.9 us)

commit v6 on v5

--- a/solution.py
+++ b/solution.py
@@ -299,23 +299,25 @@
         count = len(scalars) + len(arrays)
 
         def without_waits(*refs):
-            kernel(*refs[:count], *refs[count + len(waits) :])
+            rest = refs[count + len(waits) :]
+            kernel(*refs[:count], *rest[: len(outs)], *rest[len(outs) + 1 :])
+            rest[len(outs)][...] = jnp.zeros_like(rest[len(outs)])
 
         got = pl.pallas_call(
             without_waits,
-            out_shape=outs,
+            out_shape=[*outs, jax.ShapeDtypeStruct((8, 128), jnp.float32)],
             in_specs=[pl.BlockSpec(memory_space=SMEM)] * len(scalars)
             + (in_specs or [plain] * len(arrays))
             + [pl.BlockSpec(memory_space=pl.ANY)] * len(waits),
-            out_specs=options.pop("out_specs", [plain] * len(outs)),
+            out_specs=options.pop("out_specs", [plain] * len(outs)) + [plain],
             scratch_shapes=scratch,
             compiler_params=pltpu.CompilerParams(vmem_limit_bytes=12 * 1024 * 1024),
             cost_estimate=pl.CostEstimate(flops=1, bytes_accessed=1, transcendentals=0),
             name=name,
             **options,
         )(*scalars, *arrays, *waits)
-        self.latest = [got[0]]
-        return got
+        self.latest = [got[-1]]
+        return got[:-1]
 
 
 def body(
@@ -380,7 +382,7 @@
         ],
         axis=1,
     )
-    tables = [mine] + [turn_line(mine, by) for by in range(1, chips)]
+    tables = [mine] + [turn_line(mine, by) for by in range(chips - 1, 0, -1)]
     table = jnp.concatenate(tables, axis=0)
     columns = (0, mine.shape[1] // 2)
 
@@ -400,7 +402,7 @@
     seen = jnp.where(order < depth, order, chips - 1 - order + depth)
     goal = jnp.where(mirrored, chips - 1 - seen, seen)
     place = jnp.concatenate(
-        [jnp.stack([chip, index % 2, depth]), (chip - goal + chips) % chips]
+        [jnp.stack([chip, index % 2, depth]), (goal - chip + chips) % chips]
     ).astype(jnp.int32)
 
     def partial(tier, slot, upper, lower, c, role, after=()):
@@ -472,7 +474,7 @@
         )
         return got[0], got[1:]
 
-    last_cuts = [per] * HALVES
+    last_cuts = [rows - rows // 4, rows // 4]
 
     def solve_six(own, last, number, previous):
         cut = last_cuts[number]

time: 166 us -> 165 us (level)
  the two profiles are of different devices: /device:TPU:18 before, /device:TPU:0 now
where the time goes in v6:
time: 165 us; the launch traced here: 162 us
  Pallas kernels  65.4 us (40%)
  starting transfers between devices  44.7 us (27%)
  waiting for transfers between devices  43.1 us (26%)
  local copies, waits for them, and re-layouts  7.79 us (5%)
    pallas_call x24, Pallas kernels, call(): pl.pallas_call(without_waits, out_shape=[*outs, jax.ShapeDtypeStruct((8,...  65.4 us
    ppermute x12, waiting for transfers between devices, hop(): return lax.ppermute(array, 'mb', pairs)  37.2 us
    ppermute x12, starting transfers between devices, hop(): return lax.ppermute(array, 'mb', pairs)  25 us
    unnamed x51, local copies, waits for them, and re-layouts  7.3 us
    ppermute x3, starting transfers between devices, turn_line(): lax.ppermute(array, 'mb', [(i, (i + 2 * by) % peer_count) for i in range(...  6.94 us
    ppermute x4, starting transfers between devices, along(): lax.ppermute(array, 'ma', [(i, (i + by) % row_count) for i in range(row_c...  6.72 us
    ppermute x8, starting transfers between devices, sibling_of(): lax.ppermute(array, 'mb', [(2 * i + c, 2 * i + 1 - c) for i in of_chips f...  6.01 us
    ppermute x8, waiting for transfers between devices, sibling_of(): lax.ppermute(array, 'mb', [(2 * i + c, 2 * i + 1 - c) for i in of_chips f...  3.64 us
  transfers between devices with their start and end apart: 27, of which 10 were waited for; matrix products, arithmetic and copies ran while one was open for 1% of the time, Pallas kernels for 36%

profile of v6, /device:TPU:0, one launch (start us, length us, event | category | flops | bytes accessed | tf_op | source)
XLA Modules:
  0.0 162.0 jit_solution(946825682308084490)
XLA Ops:
  4.9 3.0 %collective-permute-start.2 = (s32[8,20]{1,0:T(8,128)S(1)}, s32[8,20]{1,0:T(8,128)S(1)}, u32[]{:S(2)}, u32[]{:S(2)}) collective-permute-start(s32[8,20]{1,0:T(8,128)S(1)} %concatenate.10), channel_id=1, source_target_pairs={{0,2},{1,3},{2,4},{3,5},{4,6},{5,7},{6,0},{7,1},{8,10},{9,11},{10,... | collective-permute-start | bytes 1928 | tf_op jit(solution)/shard_map/ppermute | solution.py:362
  7.9 2.6 %collective-permute-start.1 = (s32[8,20]{1,0:T(8,128)S(1)}, s32[8,20]{1,0:T(8,128)S(1)}, u32[]{:S(2)}, u32[]{:S(2)}) collective-permute-start(s32[8,20]{1,0:T(8,128)S(1)} %concatenate.10), channel_id=1, source_target_pairs={{0,4},{1,5},{2,6},{3,7},{4,0},{5,1},{6,2},{7,3},{8,12},{9,13},{10,... | collective-permute-start | bytes 1928 | tf_op jit(solution)/shard_map/ppermute | solution.py:362
  14.1 4.3 %partial_0_0_all.1 = (f32[8,2,128,128]{3,2,1,0:T(8,128)}, f32[8,128]{1,0:T(8,128)S(1)}) custom-call(s32[7]{0:T(128)S(1)} %pad_add_fusion.1.refs_0_, s32[32,20]{1,0:T(8,128)S(1)} %pad_add_fusion.refs_1_, f32[2,12]{1,0:T(2,128)S(1)} %copy-done.13, f32[8,2,128,128]{3,2,1,0:T(8,128)} %refs_5_.9, f32[8,2,128,128]{3,2,1,0:T(8,128)S(1)} %collective-permute-done.3.refs_4_.refs_6_, ...), custom_call_target="tpu_custom_call" | custom-call | flops 1 | bytes 1 | tf_op jit(solution)/shard_map/partial_0_0_all/pallas_call | solution.py:306
  18.5 2.6 %collective-permute-start.5 = (f32[8,2,128,128]{3,2,1,0:T(8,128)}, f32[8,2,128,128]{3,2,1,0:T(8,128)S(1)}, u32[]{:S(2)}, u32[]{:S(2)}) collective-permute-start(f32[8,2,128,128]{3,2,1,0:T(8,128)} %refs_5_.9), channel_id=1, source_target_pairs={{0,24},{8,0},{16,8},{24,16},{1,25},{9,1},{17,9},{25,17},{2,26},{10... | collective-permute-start | bytes 3145736 | tf_op jit(solution)/shard_map/ppermute | solution.py:359
  21.1 4.3 %partial_0_1_all.1 = (f32[8,2,128,128]{3,2,1,0:T(8,128)}, f32[8,128]{1,0:T(8,128)S(1)}) custom-call(s32[7]{0:T(128)S(1)} %pad_add_fusion.1.refs_0_, s32[32,20]{1,0:T(8,128)S(1)} %pad_add_fusion.refs_1_, f32[2,12]{1,0:T(2,128)S(1)} %copy-done.13, f32[8,2,128,128]{3,2,1,0:T(8,128)} %refs_5_.9, f32[8,2,128,128]{3,2,1,0:T(8,128)S(1)} %collective-permute-done.3.refs_4_.refs_6_, ...), custom_call_target="tpu_custom_call" | custom-call | flops 1 | bytes 1 | tf_op jit(solution)/shard_map/partial_0_1_all/pallas_call | solution.py:306
  25.4 4.7 %collective-permute-start.7 = (f32[8,2,128,128]{3,2,1,0:T(8,128)}, f32[8,2,128,128]{3,2,1,0:T(8,128)}, u32[]{:S(2)}, u32[]{:S(2)}) collective-permute-start(f32[8,2,128,128]{3,2,1,0:T(8,128)} %get-tuple-element.64.refs_0_), channel_id=1, source_target_pairs={{0,2},{6,4},{1,3},{7,5},{8,10},{14,12},{9,11},{15,13},{16,18},{22,... | collective-permute-start | bytes 3145736 | tf_op jit(solution)/shard_map/ppermute | solution.py:372
  30.2 4.3 %partial_0_2_all.1 = (f32[8,2,128,128]{3,2,1,0:T(8,128)}, f32[8,128]{1,0:T(8,128)S(1)}) custom-call(s32[7]{0:T(128)S(1)} %pad_add_fusion.1.refs_0_, s32[32,20]{1,0:T(8,128)S(1)} %pad_add_fusion.refs_1_, f32[2,12]{1,0:T(2,128)S(1)} %copy-done.13, f32[8,2,128,128]{3,2,1,0:T(8,128)} %refs_5_.9, f32[8,2,128,128]{3,2,1,0:T(8,128)S(1)} %collective-permute-done.3.refs_4_.refs_6_, ...), custom_call_target="tpu_custom_call" | custom-call | flops 1 | bytes 1 | tf_op jit(solution)/shard_map/partial_0_2_all/pallas_call | solution.py:306
  34.5 4.0 %sums_0.1 = (f32[8,2,128,128]{3,2,1,0:T(8,128)S(1)}, f32[8,2,128,128]{3,2,1,0:T(8,128)S(1)}, f32[8,128]{1,0:T(8,128)S(1)}) custom-call(s32[7]{0:T(128)S(1)} %pad_add_fusion.1.refs_0_, s32[32,20]{1,0:T(8,128)S(1)} %pad_add_fusion.refs_1_, f32[2,12]{1,0:T(2,128)S(1)} %copy-done.13, s32[8,18]{1,0:T(8,128)S(1)} %reshape.10.refs_3_, s32[8,12]{1,0:T(8,128)S(1)} %copy-done.14, ...), custom_call_target="tpu_custom_call" | custom-call | flops 1 | bytes 1 | tf_op jit(solution)/shard_map/sums_0/pallas_call | solution.py:306
  39.5 2.9 %collective-permute-done.8.refs_1_.refs_9_ = f32[8,2,128,128]{3,2,1,0:T(8,128)} collective-permute-done((f32[8,2,128,128]{3,2,1,0:T(8,128)}, f32[8,2,128,128]{3,2,1,0:T(8,128)}, u32[]{:S(2)}, u32[]{:S(2)}) %collective-permute-start.8) | collective-permute-done | bytes 1048608 | tf_op jit(solution)/shard_map/ppermute | solution.py:372
  42.5 2.7 %add_0_1_3.1 = (f32[8,2,128,128]{3,2,1,0:T(8,128)}, f32[8,128]{1,0:T(8,128)S(1)}) custom-call(f32[8,2,128,128]{3,2,1,0:T(8,128)} %get-tuple-element.64.refs_0_, f32[8,2,128,128]{3,2,1,0:T(8,128)} %collective-permute-done.8.refs_1_.refs_9_, f32[8,128]{1,0:T(8,128)S(1)} %get-tuple-element.66.refs_2_), custom_call_target="tpu_custom_call" | custom-call | flops 1 | bytes 1 | tf_op jit(solution)/shard_map/add_0_1_3/pallas_call | solution.py:306
  46.6 2.9 %tilt_seven.1 = (f32[8,2,128,128]{3,2,1,0:T(8,128)S(1)}, f32[4,2,128,128]{3,2,1,0:T(8,128)S(1)}, f32[4,2,128,128]{3,2,1,0:T(8,128)}, f32[8,128]{1,0:T(8,128)S(1)}) custom-call(f32[128,128]{1,0:T(8,128)S(1)} %bitcast.6, f32[128,128]{1,0:T(8,128)S(1)} %copy-done.4, f32[8,2,128,128]{3,2,1,0:T(8,128)S(1)} %copy-done.12, f32[8,128]{1,0:T(8,128)S(1)} %get-tuple-element.67.refs_3_, ...), custom_call_target="tpu_custom_call" | custom-call | flops 1 | bytes 1 | tf_op jit(solution)/shard_map/tilt_seven/pallas_call | solution.py:306
  50.0 2.1 %collective-permute-done.9.refs_4_.refs_6_ = f32[4,2,128,128]{3,2,1,0:T(8,128)S(1)} collective-permute-done((f32[4,2,128,128]{3,2,1,0:T(8,128)S(1)}, f32[4,2,128,128]{3,2,1,0:T(8,128)S(1)}, u32[]{:S(2)}, u32[]{:S(2)}) %collective-permute-start.9) | collective-permute-done | bytes 524320 | tf_op jit(solution)/shard_map/ppermute | solution.py:354
  52.2 8.2 %collective-permute-start.12 = (f32[8,2,128,128]{3,2,1,0:T(8,128)}, f32[8,2,128,128]{3,2,1,0:T(8,128)}, u32[]{:S(2)}, u32[]{:S(2)}) collective-permute-start(f32[8,2,128,128]{3,2,1,0:T(8,128)} %get-tuple-element.63.refs_0_), channel_id=1, source_target_pairs={{0,2},{6,4},{1,3},{7,5},{8,10},{14,12},{9,11},{15,13},{16,18},{22,... | collective-permute-start | bytes 3145736 | tf_op jit(solution)/shard_map/ppermute | solution.py:372
  60.5 2.5 %collective-permute-start.16 = (f32[8,2,128,128]{3,2,1,0:T(8,128)S(1)}, f32[8,2,128,128]{3,2,1,0:T(8,128)S(1)}, u32[]{:S(2)}, u32[]{:S(2)}) collective-permute-start(f32[8,2,128,128]{3,2,1,0:T(8,128)S(1)} %get-tuple-element.78.refs_3_.refs_5_), channel_id=1, source_target_pairs={{0,24},{8,0},{16,8},{24,16},{1,25},{9,1},{17,9},{25,17},{2,26},{10... | collective-permute-start | bytes 3145736 | tf_op jit(solution)/shard_map/ppermute | solution.py:359
  67.5 2.2 %finish_five.1 = (f32[8,2,128,128]{3,2,1,0:T(8,128)S(1)}, f32[8,128]{1,0:T(8,128)S(1)}) custom-call(s32[8,12]{1,0:T(8,128)S(1)} %copy-done.14, f32[2,12]{1,0:T(2,128)S(1)} %copy-done.13, f32[128,128]{1,0:T(8,128)S(1)} %copy-done.7, f32[8,2,128,128]{3,2,1,0:T(8,128)S(1)} %copy-done.9, f32[8,2,128,128]{3,2,1,0:T(8,128)S(1)} %copy-done.11, ...), custom_call_target="tpu_custom_call" | custom-call | flops 1 | bytes 1 | tf_op jit(solution)/shard_map/finish_five/pallas_call | solution.py:306
  69.7 2.6 %collective-permute-done.13.refs_8_ = f32[8,2,128,128]{3,2,1,0:T(8,128)} collective-permute-done((f32[8,2,128,128]{3,2,1,0:T(8,128)}, f32[8,2,128,128]{3,2,1,0:T(8,128)}, u32[]{:S(2)}, u32[]{:S(2)}) %collective-permute-start.13) | collective-permute-done | bytes 1048608 | tf_op jit(solution)/shard_map/ppermute | solution.py:372
  72.9 3.7 %solve_five_ends.1 = (f32[8,2,128,128]{3,2,1,0:T(8,128)S(1)}, f32[4,2,128,128]{3,2,1,0:T(8,128)S(1)}, f32[4,2,128,128]{3,2,1,0:T(8,128)S(1)}, f32[8,128]{1,0:T(8,128)S(1)}) custom-call(s32[7]{0:T(128)S(1)} %pad_add_fusion.1.refs_0_, s32[8,12]{1,0:T(8,128)S(1)} %copy-done.14, f32[12]{0:T(128)S(1)} %copy-done.17, f32[1,128]{1,0:T(1,128)S(1)} %bitcast.14, ...), custom_call_target="tpu_custom_call" | custom-call | flops 1 | bytes 1 | tf_op jit(solution)/shard_map/solve_five_ends/pallas_call | solution.py:306
  76.6 1.9 %collective-permute-start.14 = (f32[4,2,128,128]{3,2,1,0:T(8,128)S(1)}, f32[4,2,128,128]{3,2,1,0:T(8,128)S(1)}, u32[]{:S(2)}, u32[]{:S(2)}) collective-permute-start(f32[4,2,128,128]{3,2,1,0:T(8,128)S(1)} %get-tuple-element.79), channel_id=1, source_target_pairs={{0,1},{1,0},{6,7},{7,6},{8,9},{9,8},{14,15},{15,14},{16,17},{17,16... | collective-permute-start | bytes 1572872 | tf_op jit(solution)/shard_map/ppermute | solution.py:354
  78.5 2.4 %collective-permute-start.15 = (f32[4,2,128,128]{3,2,1,0:T(8,128)S(1)}, f32[4,2,128,128]{3,2,1,0:T(8,128)S(1)}, u32[]{:S(2)}, u32[]{:S(2)}) collective-permute-start(f32[4,2,128,128]{3,2,1,0:T(8,128)S(1)} %get-tuple-element.80), channel_id=1, source_target_pairs={{0,1},{1,0},{6,7},{7,6},{8,9},{9,8},{14,15},{15,14},{16,17},{17,16... | collective-permute-start | bytes 1572872 | tf_op jit(solution)/shard_map/ppermute | solution.py:354
  82.5 3.1 %partial_1_0_ends.1 = (f32[8,2,128,128]{3,2,1,0:T(8,128)S(1)}, f32[8,128]{1,0:T(8,128)S(1)}) custom-call(s32[7]{0:T(128)S(1)} %pad_add_fusion.1.refs_0_, s32[32,20]{1,0:T(8,128)S(1)} %pad_add_fusion.refs_1_, f32[2,12]{1,0:T(2,128)S(1)} %copy-done.13, f32[8,2,128,128]{3,2,1,0:T(8,128)S(1)} %get-tuple-element.78.refs_3_.refs_5_, ...), custom_call_target="tpu_custom_call" | custom-call | flops 1 | bytes 1 | tf_op jit(solution)/shard_map/partial_1_0_ends/pallas_call | solution.py:306
  87.0 3.9 %partial_1_1_ends.1 = (f32[8,2,128,128]{3,2,1,0:T(8,128)}, f32[8,128]{1,0:T(8,128)S(1)}) custom-call(s32[7]{0:T(128)S(1)} %pad_add_fusion.1.refs_0_, s32[32,20]{1,0:T(8,128)S(1)} %pad_add_fusion.refs_1_, f32[2,12]{1,0:T(2,128)S(1)} %copy-done.13, f32[8,2,128,128]{3,2,1,0:T(8,128)S(1)} %get-tuple-element.78.refs_3_.refs_5_, ...), custom_call_target="tpu_custom_call" | custom-call | flops 1 | bytes 1 | tf_op jit(solution)/shard_map/partial_1_1_ends/pallas_call | solution.py:306
  90.9 2.3 %collective-permute-start.20 = (f32[8,2,128,128]{3,2,1,0:T(8,128)}, f32[8,2,128,128]{3,2,1,0:T(8,128)}, u32[]{:S(2)}, u32[]{:S(2)}) collective-permute-start(f32[8,2,128,128]{3,2,1,0:T(8,128)} %get-tuple-element.96), channel_id=1, source_target_pairs={{0,2},{6,4},{1,3},{7,5},{8,10},{14,12},{9,11},{15,13},{16,18},{22,... | collective-permute-start | bytes 3145736 | tf_op jit(solution)/shard_map/ppermute | solution.py:372
  93.2 4.0 %partial_1_2_ends.1 = (f32[8,2,128,128]{3,2,1,0:T(8,128)}, f32[8,128]{1,0:T(8,128)S(1)}) custom-call(s32[7]{0:T(128)S(1)} %pad_add_fusion.1.refs_0_, s32[32,20]{1,0:T(8,128)S(1)} %pad_add_fusion.refs_1_, f32[2,12]{1,0:T(2,128)S(1)} %copy-done.13, f32[8,2,128,128]{3,2,1,0:T(8,128)S(1)} %get-tuple-element.78.refs_3_.refs_5_, ...), custom_call_target="tpu_custom_call" | custom-call | flops 1 | bytes 1 | tf_op jit(solution)/shard_map/partial_1_2_ends/pallas_call | solution.py:306
  101.2 2.3 %collective-permute-start.23 = (f32[8,2,128,128]{3,2,1,0:T(8,128)}, f32[8,2,128,128]{3,2,1,0:T(8,128)}, u32[]{:S(2)}, u32[]{:S(2)}) collective-permute-start(f32[8,2,128,128]{3,2,1,0:T(8,128)} %get-tuple-element.106), channel_id=1, source_target_pairs={{0,2},{6,4},{1,3},{7,5},{8,10},{14,12},{9,11},{15,13},{16,18},{22,... | collective-permute-start | bytes 3145736 | tf_op jit(solution)/shard_map/ppermute | solution.py:372
  107.5 3.0 %collective-permute-done.19.refs_1_ = f32[8,2,128,128]{3,2,1,0:T(8,128)S(1)} collective-permute-done((f32[8,2,128,128]{3,2,1,0:T(8,128)S(1)}, f32[8,2,128,128]{3,2,1,0:T(8,128)S(1)}, u32[]{:S(2)}, u32[]{:S(2)}) %collective-permute-start.19) | collective-permute-done | bytes 1048608 | tf_op jit(solution)/shard_map/ppermute | solution.py:372
  116.1 3.8 %sums_1.1 = (f32[8,2,128,128]{3,2,1,0:T(8,128)S(1)}, f32[8,2,128,128]{3,2,1,0:T(8,128)S(1)}, f32[8,128]{1,0:T(8,128)S(1)}) custom-call(s32[7]{0:T(128)S(1)} %pad_add_fusion.1.refs_0_, s32[32,20]{1,0:T(8,128)S(1)} %pad_add_fusion.refs_1_, f32[2,12]{1,0:T(2,128)S(1)} %copy-done.13, s32[8,18]{1,0:T(8,128)S(1)} %reshape.11.refs_3_, s32[8,12]{1,0:T(8,128)S(1)} %copy-done.15, ...), custom_call_target="tpu_custom_call" | custom-call | flops 1 | bytes 1 | tf_op jit(solution)/shard_map/sums_1/pallas_call | solution.py:306
  119.9 13.2 %collective-permute-done.20.refs_1_ = f32[8,2,128,128]{3,2,1,0:T(8,128)} collective-permute-done((f32[8,2,128,128]{3,2,1,0:T(8,128)}, f32[8,2,128,128]{3,2,1,0:T(8,128)}, u32[]{:S(2)}, u32[]{:S(2)}) %collective-permute-start.20) | collective-permute-done | bytes 1048608 | tf_op jit(solution)/shard_map/ppermute | solution.py:372
  135.9 3.1 %back_five.1 = (f32[8,2,128,128]{3,2,1,0:T(8,128)}, f32[8,128]{1,0:T(8,128)S(1)}) custom-call(f32[128,128]{1,0:T(8,128)S(1)} %copy-done.4, f32[128,128]{1,0:T(8,128)S(1)} %bitcast.10, f32[8,2,128,128]{3,2,1,0:T(8,128)S(1)} %get-tuple-element.86.refs_6_.refs_8_.refs_2_, f32[8,128]{1,0:T(8,128)S(1)} %get-tuple-element.99.refs_3_), custom_call_target="tpu_custom_call" | custom-call | flops 1 | bytes 1 | tf_op jit(solution)/shard_map/back_five/pallas_call | solution.py:306
  139.0 2.2 %finish_six.1 = (f32[8,2,128,128]{3,2,1,0:T(8,128)S(1)}, f32[8,128]{1,0:T(8,128)S(1)}) custom-call(s32[8,12]{1,0:T(8,128)S(1)} %copy-done.15, f32[2,12]{1,0:T(2,128)S(1)} %copy-done.13, f32[128,128]{1,0:T(8,128)S(1)} %get-tuple-element.81.refs_9_.refs_2_, f32[8,2,128,128]{3,2,1,0:T(8,128)S(1)} %get-tuple-element.101.refs_3_, ...), custom_call_target="tpu_custom_call" | custom-call | flops 1 | bytes 1 | tf_op jit(solution)/shard_map/finish_six/pallas_call | solution.py:306
  141.2 13.9 %collective-permute-done.23.refs_8_ = f32[8,2,128,128]{3,2,1,0:T(8,128)} collective-permute-done((f32[8,2,128,128]{3,2,1,0:T(8,128)}, f32[8,2,128,128]{3,2,1,0:T(8,128)}, u32[]{:S(2)}, u32[]{:S(2)}) %collective-permute-start.23) | collective-permute-done | bytes 1048608 | tf_op jit(solution)/shard_map/ppermute | solution.py:372
  155.2 4.2 %solve_six_0.1 = (f32[8,2,128,128]{3,2,1,0:T(8,128)}, f32[8,128]{1,0:T(8,128)S(1)}) custom-call(s32[8,12]{1,0:T(8,128)S(1)} %copy-done.15, f32[12]{0:T(128)S(1)} %copy-done.17, f32[1,128]{1,0:T(1,128)S(1)} %bitcast.16, f32[128,1]{1,0:T(8,128)S(1)} %copy.25.refs_4_.refs_3_, f32[128,128]{1,0:T(8,128)S(1)} %copy-done.4, f32[128,128]{1,0:T(8,128)S(1)} %bitcast.11, ...), custom_call_target="tpu_custom_call" | custom-call | flops 1 | bytes 1 | tf_op jit(solution)/shard_map/solve_six_0/pallas_call | solution.py:306
  159.4 2.6 %solve_six_1.1 = (f32[8,2,128,128]{3,2,1,0:T(8,128)}, f32[8,128]{1,0:T(8,128)}) custom-call(s32[8,12]{1,0:T(8,128)S(1)} %copy-done.15, f32[12]{0:T(128)S(1)} %copy-done.17, f32[1,128]{1,0:T(1,128)S(1)} %bitcast.17, f32[128,1]{1,0:T(8,128)S(1)} %copy.25.refs_4_.refs_3_, f32[128,128]{1,0:T(8,128)S(1)} %copy-done.4, ...), custom_call_target="tpu_custom_call", output_to_operand_aliasing={{0}: (11, {})} | custom-call | flops 1 | bytes 1 | tf_op jit(solution)/shard_map/solve_six_1/pallas_call | solution.py:306
  (106 shorter events, 35.5 us)
Async XLA Ops:
  0.6 13.5 %collective-permute-start.4 = (f32[8,2,128,128]{3,2,1,0:T(8,128)}, f32[8,2,128,128]{3,2,1,0:T(8,128)S(1)}, u32[]{:S(2)}, u32[]{:S(2)}) collective-permute-start(f32[8,2,128,128]{3,2,1,0:T(8,128)} %refs_7_.7), channel_id=1, source_target_pairs={{0,1},{1,0},{2,3},{3,2},{4,5},{5,4},{6,7},{7,6},{8,9},{9,8},{10,11... | collective-permute-start | bytes 3145736 | tf_op jit(solution)/shard_map/ppermute | solution.py:354
  1.2 12.9 %collective-permute-start.3 = (f32[8,2,128,128]{3,2,1,0:T(8,128)}, f32[8,2,128,128]{3,2,1,0:T(8,128)S(1)}, u32[]{:S(2)}, u32[]{:S(2)}) collective-permute-start(f32[8,2,128,128]{3,2,1,0:T(8,128)} %refs_5_.9), channel_id=1, source_target_pairs={{0,1},{1,0},{2,3},{3,2},{4,5},{5,4},{6,7},{7,6},{8,9},{9,8},{10,11... | collective-permute-start | bytes 3145736 | tf_op jit(solution)/shard_map/ppermute | solution.py:354
  4.7 9.4 %copy-start.7 = (f32[128,128]{1,0:T(8,128)S(1)}, f32[128,128]{1,0:T(8,128)}, u32[]{:S(2)}) copy-start(f32[128,128]{1,0:T(8,128)} %refs_2_.22) | copy-start | bytes 196612
  4.9 7.0 %collective-permute-start.2 = (s32[8,20]{1,0:T(8,128)S(1)}, s32[8,20]{1,0:T(8,128)S(1)}, u32[]{:S(2)}, u32[]{:S(2)}) collective-permute-start(s32[8,20]{1,0:T(8,128)S(1)} %concatenate.10), channel_id=1, source_target_pairs={{0,2},{1,3},{2,4},{3,5},{4,6},{5,7},{6,0},{7,1},{8,10},{9,11},{10,... | collective-permute-start | bytes 1928 | tf_op jit(solution)/shard_map/ppermute | solution.py:362
  7.9 4.5 %collective-permute-start.1 = (s32[8,20]{1,0:T(8,128)S(1)}, s32[8,20]{1,0:T(8,128)S(1)}, u32[]{:S(2)}, u32[]{:S(2)}) collective-permute-start(s32[8,20]{1,0:T(8,128)S(1)} %concatenate.10), channel_id=1, source_target_pairs={{0,4},{1,5},{2,6},{3,7},{4,0},{5,1},{6,2},{7,3},{8,12},{9,13},{10,... | collective-permute-start | bytes 1928 | tf_op jit(solution)/shard_map/ppermute | solution.py:362
  10.5 3.6 %collective-permute-start = (s32[8,20]{1,0:T(8,128)S(1)}, s32[8,20]{1,0:T(8,128)S(1)}, u32[]{:S(2)}, u32[]{:S(2)}) collective-permute-start(s32[8,20]{1,0:T(8,128)S(1)} %concatenate.10), channel_id=1, source_target_pairs={{0,6},{1,7},{2,0},{3,1},{4,2},{5,3},{6,4},{7,5},{8,14},{9,15},{10,... | collective-permute-start | bytes 1928 | tf_op jit(solution)/shard_map/ppermute | solution.py:362
  18.4 24.0 %collective-permute-start.8 = (f32[8,2,128,128]{3,2,1,0:T(8,128)}, f32[8,2,128,128]{3,2,1,0:T(8,128)}, u32[]{:S(2)}, u32[]{:S(2)}) collective-permute-start(f32[8,2,128,128]{3,2,1,0:T(8,128)} %get-tuple-element.65), channel_id=1, source_target_pairs={{0,2},{6,4},{1,3},{7,5},{4,6},{2,0},{5,7},{3,1},{8,10},{14,12},{9,... | collective-permute-start | bytes 3145736 | tf_op jit(solution)/shard_map/ppermute | solution.py:372
  18.5 28.0 %collective-permute-start.5 = (f32[8,2,128,128]{3,2,1,0:T(8,128)}, f32[8,2,128,128]{3,2,1,0:T(8,128)S(1)}, u32[]{:S(2)}, u32[]{:S(2)}) collective-permute-start(f32[8,2,128,128]{3,2,1,0:T(8,128)} %refs_5_.9), channel_id=1, source_target_pairs={{0,24},{8,0},{16,8},{24,16},{1,25},{9,1},{17,9},{25,17},{2,26},{10... | collective-permute-start | bytes 3145736 | tf_op jit(solution)/shard_map/ppermute | solution.py:359
  21.1 46.4 %collective-permute-start.6 = (f32[8,2,128,128]{3,2,1,0:T(8,128)}, f32[8,2,128,128]{3,2,1,0:T(8,128)}, u32[]{:S(2)}, u32[]{:S(2)}) collective-permute-start(f32[8,2,128,128]{3,2,1,0:T(8,128)} %refs_7_.7), channel_id=1, source_target_pairs={{0,8},{8,16},{16,24},{24,0},{1,9},{9,17},{17,25},{25,1},{2,10},{10... | collective-permute-start | bytes 3145736 | tf_op jit(solution)/shard_map/ppermute | solution.py:359
  21.1 9.0 %copy-start.18 = (s32[8,2,9]{2,1,0:T(2,128)S(1)}, s32[8,2,9]{2,1,0:T(2,128)}, u32[]{:S(2)}) copy-start(s32[8,2,9]{2,1,0:T(2,128)} %param.25) | copy-start | bytes 1732
  25.4 39.5 %collective-permute-start.7 = (f32[8,2,128,128]{3,2,1,0:T(8,128)}, f32[8,2,128,128]{3,2,1,0:T(8,128)}, u32[]{:S(2)}, u32[]{:S(2)}) collective-permute-start(f32[8,2,128,128]{3,2,1,0:T(8,128)} %get-tuple-element.64.refs_0_), channel_id=1, source_target_pairs={{0,2},{6,4},{1,3},{7,5},{8,10},{14,12},{9,11},{15,13},{16,18},{22,... | collective-permute-start | bytes 3145736 | tf_op jit(solution)/shard_map/ppermute | solution.py:372
  39.5 5.6 %copy-start.10 = (f32[8,2,128,128]{3,2,1,0:T(8,128)}, f32[8,2,128,128]{3,2,1,0:T(8,128)S(1)}, u32[]{:S(2)}) copy-start(f32[8,2,128,128]{3,2,1,0:T(8,128)S(1)} %get-tuple-element.62.refs_4_) | copy-start | bytes 3145732
  45.2 27.1 %collective-permute-start.13 = (f32[8,2,128,128]{3,2,1,0:T(8,128)}, f32[8,2,128,128]{3,2,1,0:T(8,128)}, u32[]{:S(2)}, u32[]{:S(2)}) collective-permute-start(f32[8,2,128,128]{3,2,1,0:T(8,128)} %get-tuple-element.75), channel_id=1, source_target_pairs={{2,6},{4,0},{3,7},{5,1},{10,14},{12,8},{11,15},{13,9},{18,22},{20,... | collective-permute-start | bytes 3145736 | tf_op jit(solution)/shard_map/ppermute | solution.py:372
  49.5 2.6 %collective-permute-start.9 = (f32[4,2,128,128]{3,2,1,0:T(8,128)S(1)}, f32[4,2,128,128]{3,2,1,0:T(8,128)S(1)}, u32[]{:S(2)}, u32[]{:S(2)}) collective-permute-start(f32[4,2,128,128]{3,2,1,0:T(8,128)S(1)} %get-tuple-element.69), channel_id=1, source_target_pairs={{0,1},{1,0},{2,3},{3,2},{4,5},{5,4},{6,7},{7,6},{8,9},{9,8},{10,11... | collective-permute-start | bytes 1572872 | tf_op jit(solution)/shard_map/ppermute | solution.py:354
  49.5 10.9 %collective-permute-start.10 = (f32[4,2,128,128]{3,2,1,0:T(8,128)}, f32[4,2,128,128]{3,2,1,0:T(8,128)S(1)}, u32[]{:S(2)}, u32[]{:S(2)}) collective-permute-start(f32[4,2,128,128]{3,2,1,0:T(8,128)} %get-tuple-element.70), channel_id=1, source_target_pairs={{0,1},{1,0},{2,3},{3,2},{4,5},{5,4},{6,7},{7,6},{8,9},{9,8},{10,11... | collective-permute-start | bytes 1572872 | tf_op jit(solution)/shard_map/ppermute | solution.py:354
  52.2 8.2 %copy-start.16 = (f32[128]{0:T(128)S(1)}, f32[128]{0:T(128)}, u32[]{:S(2)}) copy-start(f32[128]{0:T(128)} %param.21) | copy-start | bytes 1540
  52.2 34.8 %collective-permute-start.12 = (f32[8,2,128,128]{3,2,1,0:T(8,128)}, f32[8,2,128,128]{3,2,1,0:T(8,128)}, u32[]{:S(2)}, u32[]{:S(2)}) collective-permute-start(f32[8,2,128,128]{3,2,1,0:T(8,128)} %get-tuple-element.63.refs_0_), channel_id=1, source_target_pairs={{0,2},{6,4},{1,3},{7,5},{8,10},{14,12},{9,11},{15,13},{16,18},{22,... | collective-permute-start | bytes 3145736 | tf_op jit(solution)/shard_map/ppermute | solution.py:372
  60.5 36.7 %collective-permute-start.16 = (f32[8,2,128,128]{3,2,1,0:T(8,128)S(1)}, f32[8,2,128,128]{3,2,1,0:T(8,128)S(1)}, u32[]{:S(2)}, u32[]{:S(2)}) collective-permute-start(f32[8,2,128,128]{3,2,1,0:T(8,128)S(1)} %get-tuple-element.78.refs_3_.refs_5_), channel_id=1, source_target_pairs={{0,24},{8,0},{16,8},{24,16},{1,25},{9,1},{17,9},{25,17},{2,26},{10... | collective-permute-start | bytes 3145736 | tf_op jit(solution)/shard_map/ppermute | solution.py:359
  66.7 30.4 %collective-permute-start.11 = (f32[8,2,128,128]{3,2,1,0:T(8,128)S(1)}, f32[8,2,128,128]{3,2,1,0:T(8,128)S(1)}, u32[]{:S(2)}, u32[]{:S(2)}) collective-permute-start(f32[8,2,128,128]{3,2,1,0:T(8,128)S(1)} %get-tuple-element.74), channel_id=1, source_target_pairs={{2,4},{4,2},{3,5},{5,3},{10,12},{12,10},{11,13},{13,11},{18,20},{2... | collective-permute-start | bytes 3145736 | tf_op jit(solution)/shard_map/ppermute | solution.py:372
  76.6 4.3 %collective-permute-start.14 = (f32[4,2,128,128]{3,2,1,0:T(8,128)S(1)}, f32[4,2,128,128]{3,2,1,0:T(8,128)S(1)}, u32[]{:S(2)}, u32[]{:S(2)}) collective-permute-start(f32[4,2,128,128]{3,2,1,0:T(8,128)S(1)} %get-tuple-element.79), channel_id=1, source_target_pairs={{0,1},{1,0},{6,7},{7,6},{8,9},{9,8},{14,15},{15,14},{16,17},{17,16... | collective-permute-start | bytes 1572872 | tf_op jit(solution)/shard_map/ppermute | solution.py:354
  78.5 3.9 %collective-permute-start.15 = (f32[4,2,128,128]{3,2,1,0:T(8,128)S(1)}, f32[4,2,128,128]{3,2,1,0:T(8,128)S(1)}, u32[]{:S(2)}, u32[]{:S(2)}) collective-permute-start(f32[4,2,128,128]{3,2,1,0:T(8,128)S(1)} %get-tuple-element.80), channel_id=1, source_target_pairs={{0,1},{1,0},{6,7},{7,6},{8,9},{9,8},{14,15},{15,14},{16,17},{17,16... | collective-permute-start | bytes 1572872 | tf_op jit(solution)/shard_map/ppermute | solution.py:354
  85.6 24.8 %collective-permute-start.19 = (f32[8,2,128,128]{3,2,1,0:T(8,128)S(1)}, f32[8,2,128,128]{3,2,1,0:T(8,128)S(1)}, u32[]{:S(2)}, u32[]{:S(2)}) collective-permute-start(f32[8,2,128,128]{3,2,1,0:T(8,128)S(1)} %get-tuple-element.92), channel_id=1, source_target_pairs={{0,2},{6,4},{1,3},{7,5},{8,10},{14,12},{9,11},{15,13},{16,18},{22,... | collective-permute-start | bytes 3145736 | tf_op jit(solution)/shard_map/ppermute | solution.py:372
  90.9 42.1 %collective-permute-start.20 = (f32[8,2,128,128]{3,2,1,0:T(8,128)}, f32[8,2,128,128]{3,2,1,0:T(8,128)}, u32[]{:S(2)}, u32[]{:S(2)}) collective-permute-start(f32[8,2,128,128]{3,2,1,0:T(8,128)} %get-tuple-element.96), channel_id=1, source_target_pairs={{0,2},{6,4},{1,3},{7,5},{8,10},{14,12},{9,11},{15,13},{16,18},{22,... | collective-permute-start | bytes 3145736 | tf_op jit(solution)/shard_map/ppermute | solution.py:372
  99.0 2.2 %collective-permute-start.17 = (f32[4,2,128,128]{3,2,1,0:T(8,128)S(1)}, f32[4,2,128,128]{3,2,1,0:T(8,128)S(1)}, u32[]{:S(2)}, u32[]{:S(2)}) collective-permute-start(f32[4,2,128,128]{3,2,1,0:T(8,128)S(1)} %get-tuple-element.87), channel_id=1, source_target_pairs={{0,1},{1,0},{2,3},{3,2},{4,5},{5,4},{6,7},{7,6},{8,9},{9,8},{10,11... | collective-permute-start | bytes 1572872 | tf_op jit(solution)/shard_map/ppermute | solution.py:354
  99.4 4.0 %collective-permute-start.18 = (f32[4,2,128,128]{3,2,1,0:T(8,128)S(1)}, f32[4,2,128,128]{3,2,1,0:T(8,128)S(1)}, u32[]{:S(2)}, u32[]{:S(2)}) collective-permute-start(f32[4,2,128,128]{3,2,1,0:T(8,128)S(1)} %get-tuple-element.88), channel_id=1, source_target_pairs={{0,1},{1,0},{2,3},{3,2},{4,5},{5,4},{6,7},{7,6},{8,9},{9,8},{10,11... | collective-permute-start | bytes 1572872 | tf_op jit(solution)/shard_map/ppermute | solution.py:354
  99.5 35.7 %collective-permute-start.21 = (f32[8,2,128,128]{3,2,1,0:T(8,128)S(1)}, f32[8,2,128,128]{3,2,1,0:T(8,128)}, u32[]{:S(2)}, u32[]{:S(2)}) collective-permute-start(f32[8,2,128,128]{3,2,1,0:T(8,128)S(1)} %get-tuple-element.86.refs_6_.refs_8_.refs_2_), channel_id=1, source_target_pairs={{0,8},{8,16},{16,24},{24,0},{1,9},{9,17},{17,25},{25,1},{2,10},{10... | collective-permute-start | bytes 3145736 | tf_op jit(solution)/shard_map/ppermute | solution.py:359
  101.1 5.4 %copy-start = (f32[4,2,128,128]{3,2,1,0:T(8,128)}, f32[4,2,128,128]{3,2,1,0:T(8,128)S(1)}, u32[]{:S(2)}) copy-start(f32[4,2,128,128]{3,2,1,0:T(8,128)S(1)} %collective-permute-done.17.refs_7_.refs_9_) | copy-start | bytes 1572868
  101.2 54.0 %collective-permute-start.23 = (f32[8,2,128,128]{3,2,1,0:T(8,128)}, f32[8,2,128,128]{3,2,1,0:T(8,128)}, u32[]{:S(2)}, u32[]{:S(2)}) collective-permute-start(f32[8,2,128,128]{3,2,1,0:T(8,128)} %get-tuple-element.106), channel_id=1, source_target_pairs={{0,2},{6,4},{1,3},{7,5},{8,10},{14,12},{9,11},{15,13},{16,18},{22,... | collective-permute-start | bytes 3145736 | tf_op jit(solution)/shard_map/ppermute | solution.py:372
  105.3 49.9 %collective-permute-start.25 = (f32[8,2,128,128]{3,2,1,0:T(8,128)}, f32[8,2,128,128]{3,2,1,0:T(8,128)}, u32[]{:S(2)}, u32[]{:S(2)}) collective-permute-start(f32[8,2,128,128]{3,2,1,0:T(8,128)} %get-tuple-element.108), channel_id=1, source_target_pairs={{4,6},{2,0},{5,7},{3,1},{12,14},{10,8},{13,15},{11,9},{20,22},{18,... | collective-permute-start | bytes 3145736 | tf_op jit(solution)/shard_map/ppermute | solution.py:372
  111.6 43.7 %collective-permute-start.24 = (f32[8,2,128,128]{3,2,1,0:T(8,128)}, f32[8,2,128,128]{3,2,1,0:T(8,128)}, u32[]{:S(2)}, u32[]{:S(2)}) collective-permute-start(f32[8,2,128,128]{3,2,1,0:T(8,128)} %get-tuple-element.107), channel_id=1, source_target_pairs={{2,6},{4,0},{3,7},{5,1},{10,14},{12,8},{11,15},{13,9},{18,22},{20,... | collective-permute-start | bytes 3145736 | tf_op jit(solution)/shard_map/ppermute | solution.py:372
  134.4 20.9 %collective-permute-start.26 = (f32[6,2,128,128]{3,2,1,0:T(8,128)S(1)}, f32[6,2,128,128]{3,2,1,0:T(8,128)S(1)}, u32[]{:S(2)}, u32[]{:S(2)}) collective-permute-start(f32[6,2,128,128]{3,2,1,0:T(8,128)S(1)} %get-tuple-element.109), channel_id=1, source_target_pairs={{2,4},{4,2},{3,5},{5,3},{10,12},{12,10},{11,13},{13,11},{18,20},{2... | collective-permute-start | bytes 2359304 | tf_op jit(solution)/shard_map/ppermute | solution.py:372
  135.2 24.2 %collective-permute-start.22 = (f32[2,2,128,128]{3,2,1,0:T(8,128)S(1)}, f32[2,2,128,128]{3,2,1,0:T(8,128)S(1)}, u32[]{:S(2)}, u32[]{:S(2)}) collective-permute-start(f32[2,2,128,128]{3,2,1,0:T(8,128)S(1)} %get-tuple-element.105), channel_id=1, source_target_pairs={{2,4},{4,2},{3,5},{5,3},{10,12},{12,10},{11,13},{13,11},{18,20},{2... | collective-permute-start | bytes 786440 | tf_op jit(solution)/shard_map/ppermute | solution.py:372
  (18 other events, 35.3 us)
